TPU v7x, 32 devices: a whole 2x2x4 slice. The times are simulated.
32 devices in a mesh: dp: 16 (over z, x, core), mp: 2 (over y).
Axes of the slice: x: 2, y: 2, z: 4, core: 2. Of those that a mesh axis runs over, the one named last changes fastest.
Arguments:
- tokens: bfloat16 [147456, 512], P(('dp', 'mp')), may hold values from -6 to 6
- cotangent: bfloat16 [147456, 512], P(('dp', 'mp')), may hold values from -6 to 6
- frame_count: int32 [3072], P('dp'), may hold values from 1 to 6
- live_count: int32 [16], P('dp'), may hold values from 1 to 192, as said below
- w_query: bfloat16 [512, 512], P('dp', 'mp'), may hold values from -0.25 to 0.25
- w_key: bfloat16 [512, 512], P('dp', 'mp'), may hold values from -0.25 to 0.25
- w_value: bfloat16 [512, 512], P('dp', 'mp'), may hold values from -0.25 to 0.25
- w_out: bfloat16 [512, 512], P('mp', 'dp'), may hold values from -1 to 1
- w_up: bfloat16 [512, 2048], P('dp', 'mp'), may hold values from -0.25 to 0.25
- w_down: bfloat16 [2048, 512], P('mp', 'dp'), may hold values from -0.1875 to 0.1875
- gain_one: bfloat16 [512], P('dp'), may hold values from 0.5 to 1.5
- shift_one: bfloat16 [512], P('dp'), may hold values from -4 to 4
- gain_two: bfloat16 [512], P('dp'), may hold values from 0.5 to 1.5
- shift_two: bfloat16 [512], P('dp'), may hold values from -4 to 4
Outputs:
- mixed: bfloat16 [147456, 512], P(('dp', 'mp'))
- grad_input: float32 [147456, 512], P(('dp', 'mp'))
- grad_w_query: float32 [512, 512], P('dp', 'mp')
- grad_w_key: float32 [512, 512], P('dp', 'mp')
- grad_w_value: float32 [512, 512], P('dp', 'mp')
- grad_w_out: float32 [512, 512], P('mp', 'dp')
- grad_w_up: float32 [512, 2048], P('dp', 'mp')
- grad_w_down: float32 [2048, 512], P('mp', 'dp')
- grad_gain_one: float32 [512], P('dp')
- grad_shift_one: float32 [512], P('dp')
- grad_gain_two: float32 [512], P('dp')
- grad_shift_two: float32 [512], P('dp')
Inputs may be any that keep to these rules, and one draw needn't show every extreme that they name: The first live_count[d] sequence slots of data group d are live, the rest are padding; in every draw some group has all 192 slots live. The first frame_count[s] frames of slot s are valid keys.
All inputs are finite; a program needn't handle non-finite values.
Results may differ from a plain program's by a relative error of at most 0.012.
Values may be sent and summed in bfloat16 or wider, within the bound.
No kernel may reach another device: no remote copies, remote signals or barrier semaphores. Data moves between devices by JAX's collectives and lax.ppermute only.
A program may use at most 384 MiB of HBM per device.

v0:
```python
import jax
import jax.numpy as jnp
from jax import lax
from jax.sharding import PartitionSpec as P

HEAD = 64
FRAMES = 6
FTOK = 8


EPS = 1e-05


def layer_norm(rows, gain, shift):
    mean = jnp.mean(rows, axis=-1, keepdims=True)
    centered = rows - mean
    spread = jnp.mean(centered * centered, axis=-1, keepdims=True)
    return centered * lax.rsqrt(spread + EPS) * gain + shift


def key_mask(frame_count, seqlen, ftok):
    places = jnp.arange(seqlen, dtype=jnp.int32)
    causal = places[None, :] <= places[:, None]
    valid = (places // ftok)[None, :] < frame_count[:, None]
    return causal[None, None, :, :] & valid[:, None, None, :]


def inner(left, right):
    return lax.dot_general(
        left, right, (((0,), (0,)), ((), ())), preferred_element_type=jnp.float32
    )


def times_transposed(left, right):
    return lax.dot_general(
        left, right, (((1,), (1,)), ((), ())), preferred_element_type=jnp.float32
    )


def masked_scores(query, keys, mask, scale):
    scores = jnp.einsum("sqhe,skhe->shqk", query, keys, preferred_element_type=jnp.float32) * scale
    return jnp.where(mask, scores, -1000000000.0)


def attend(query, keys, values, mask, scale):
    scores = masked_scores(query, keys, mask, scale)
    top = jnp.max(scores, axis=-1, keepdims=True)
    expd = jnp.exp(scores - top)
    total = jnp.sum(expd, axis=-1, keepdims=True)
    probs = (expd / total).astype(jnp.bfloat16)
    output = jnp.einsum("shqk,skhe->sqhe", probs, values, preferred_element_type=jnp.float32)
    return (output.astype(jnp.bfloat16), top + jnp.log(total))


def attend_back(query, keys, values, grad_heads, log_total, mask, scale):
    probs = jnp.exp(masked_scores(query, keys, mask, scale) - log_total)
    grad_values = jnp.einsum(
        "shqk,sqhe->skhe",
        probs.astype(jnp.bfloat16),
        grad_heads,
        preferred_element_type=jnp.float32,
    )
    grad_probs = jnp.einsum(
        "sqhe,skhe->shqk", grad_heads, values, preferred_element_type=jnp.float32
    )
    delta = jnp.sum(probs * grad_probs, axis=-1, keepdims=True)
    grad_scores = (probs * (grad_probs - delta)).astype(jnp.bfloat16)
    grad_query = (
        jnp.einsum("shqk,skhe->sqhe", grad_scores, keys, preferred_element_type=jnp.float32) * scale
    )
    grad_keys = (
        jnp.einsum("shqk,sqhe->skhe", grad_scores, query, preferred_element_type=jnp.float32)
        * scale
    )
    return (
        grad_query.astype(jnp.bfloat16),
        grad_keys.astype(jnp.bfloat16),
        grad_values.astype(jnp.bfloat16),
    )


def shards(
    tokens,
    cotangent,
    frame_count,
    live_count,
    w_query,
    w_key,
    w_value,
    w_out,
    w_up,
    w_down,
    gain_one,
    shift_one,
    gain_two,
    shift_two,
):
    seqlen = FRAMES * FTOK
    place = lax.axis_index("mp")
    local_rows = tokens.shape[0]
    scale = HEAD ** (-0.5)
    gathered = (
        lax.all_gather(w_query, "dp", axis=0, tiled=True),
        lax.all_gather(w_key, "dp", axis=0, tiled=True),
        lax.all_gather(w_value, "dp", axis=0, tiled=True),
        lax.all_gather(w_out, "dp", axis=1, tiled=True),
        lax.all_gather(w_up, "dp", axis=0, tiled=True),
        lax.all_gather(w_down, "dp", axis=1, tiled=True),
        lax.all_gather(gain_one, "dp", axis=0, tiled=True),
        lax.all_gather(shift_one, "dp", axis=0, tiled=True),
        lax.all_gather(gain_two, "dp", axis=0, tiled=True),
        lax.all_gather(shift_two, "dp", axis=0, tiled=True),
    )
    wq, wk, wv, wo, wu, wd = (
        gathered[0],
        gathered[1],
        gathered[2],
        gathered[3],
        gathered[4],
        gathered[5],
    )
    g_one = gathered[6].astype(jnp.float32)
    b_one = gathered[7].astype(jnp.float32)
    g_two = gathered[8].astype(jnp.float32)
    b_two = gathered[9].astype(jnp.float32)
    rows = tokens.astype(jnp.float32)
    normed = layer_norm(rows, g_one, b_one).astype(jnp.bfloat16)
    normed_all = lax.all_gather(normed, "mp", axis=0, tiled=True)
    all_rows = normed_all.shape[0]
    seqs_here = all_rows // seqlen
    heads_here = wq.shape[1] // HEAD

    def split_heads(value):
        return value.astype(jnp.bfloat16).reshape(seqs_here, seqlen, heads_here, HEAD)

    query = split_heads(jnp.dot(normed_all, wq, preferred_element_type=jnp.float32))
    keys = split_heads(jnp.dot(normed_all, wk, preferred_element_type=jnp.float32))
    values = split_heads(jnp.dot(normed_all, wv, preferred_element_type=jnp.float32))
    mask = key_mask(frame_count, seqlen, FTOK)
    heads_out, log_total = attend(query, keys, values, mask, scale)
    flat_heads = heads_out.reshape(all_rows, heads_here * HEAD)
    attn_part = jnp.dot(flat_heads, wo, preferred_element_type=jnp.float32)
    attended = lax.psum_scatter(attn_part, "mp", scatter_dimension=0, tiled=True)
    hidden = rows + attended
    normed_two = layer_norm(hidden, g_two, b_two).astype(jnp.bfloat16)
    normed_two_all = lax.all_gather(normed_two, "mp", axis=0, tiled=True)
    up_value = jnp.dot(normed_two_all, wu, preferred_element_type=jnp.float32)
    act = jax.nn.gelu(up_value).astype(jnp.bfloat16)
    down_part = jnp.dot(act, wd, preferred_element_type=jnp.float32)
    down = lax.psum_scatter(
        down_part.astype(jnp.bfloat16), "mp", scatter_dimension=0, tiled=True
    ).astype(jnp.float32)
    mixed = (hidden + down).astype(jnp.bfloat16)
    slot_of_row = (place * local_rows + jnp.arange(local_rows, dtype=jnp.int32)) // seqlen
    live = (slot_of_row < live_count[0]).astype(jnp.float32)[:, None]
    grad_live = cotangent.astype(jnp.float32) * live
    grad_out = grad_live.astype(jnp.bfloat16)
    grad_out_all = lax.all_gather(grad_out, "mp", axis=0, tiled=True)
    grad_w_down = inner(act, grad_out_all)
    grad_act = times_transposed(grad_out_all, wd)
    gelu_pull = jax.vjp(jax.nn.gelu, up_value)[1]
    grad_up = gelu_pull(grad_act)[0].astype(jnp.bfloat16)
    grad_w_up = inner(normed_two_all, grad_up)
    grad_two_part = times_transposed(grad_up, wu)
    grad_normed_two = lax.psum_scatter(grad_two_part, "mp", scatter_dimension=0, tiled=True)
    norm_two_pull = jax.vjp(layer_norm, hidden, g_two, b_two)[1]
    grad_hidden_norm, grad_g_two, grad_b_two = norm_two_pull(grad_normed_two)
    grad_hidden = grad_live + grad_hidden_norm
    grad_attended = grad_hidden.astype(jnp.bfloat16)
    grad_attended_all = lax.all_gather(grad_attended, "mp", axis=0, tiled=True)
    grad_w_out = inner(flat_heads, grad_attended_all)
    grad_heads = times_transposed(grad_attended_all, wo).astype(jnp.bfloat16)
    grad_heads = grad_heads.reshape(seqs_here, seqlen, heads_here, HEAD)
    grad_query, grad_keys, grad_values = attend_back(
        query, keys, values, grad_heads, log_total, mask, scale
    )
    flat_query = grad_query.reshape(all_rows, heads_here * HEAD)
    flat_keys = grad_keys.reshape(all_rows, heads_here * HEAD)
    flat_values = grad_values.reshape(all_rows, heads_here * HEAD)
    grad_w_query = inner(normed_all, flat_query)
    grad_w_key = inner(normed_all, flat_keys)
    grad_w_value = inner(normed_all, flat_values)
    grad_one_part = (
        times_transposed(flat_query, wq)
        + times_transposed(flat_keys, wk)
        + times_transposed(flat_values, wv)
    )
    grad_normed = lax.psum_scatter(
        grad_one_part.astype(jnp.bfloat16), "mp", scatter_dimension=0, tiled=True
    ).astype(jnp.float32)
    norm_one_pull = jax.vjp(layer_norm, rows, g_one, b_one)[1]
    grad_rows_norm, grad_g_one, grad_b_one = norm_one_pull(grad_normed)
    grad_input = grad_hidden + grad_rows_norm
    norm_grads = lax.psum((grad_g_one, grad_b_one, grad_g_two, grad_b_two), "mp")
    summed = (
        lax.psum_scatter(grad_w_query, "dp", scatter_dimension=0, tiled=True),
        lax.psum_scatter(grad_w_key, "dp", scatter_dimension=0, tiled=True),
        lax.psum_scatter(grad_w_value, "dp", scatter_dimension=0, tiled=True),
        lax.psum_scatter(grad_w_out, "dp", scatter_dimension=1, tiled=True),
        lax.psum_scatter(grad_w_up, "dp", scatter_dimension=0, tiled=True),
        lax.psum_scatter(grad_w_down, "dp", scatter_dimension=1, tiled=True),
        lax.psum_scatter(norm_grads[0], "dp", scatter_dimension=0, tiled=True),
        lax.psum_scatter(norm_grads[1], "dp", scatter_dimension=0, tiled=True),
        lax.psum_scatter(norm_grads[2], "dp", scatter_dimension=0, tiled=True),
        lax.psum_scatter(norm_grads[3], "dp", scatter_dimension=0, tiled=True),
    )
    return (
        mixed,
        grad_input,
        summed[0],
        summed[1],
        summed[2],
        summed[3],
        summed[4],
        summed[5],
        summed[6],
        summed[7],
        summed[8],
        summed[9],
    )


def solution(mesh):
    return jax.shard_map(
        shards,
        mesh=mesh,
        in_specs=(
            P(("dp", "mp"), None),
            P(("dp", "mp"), None),
            P("dp"),
            P("dp"),
            P("dp", "mp"),
            P("dp", "mp"),
            P("dp", "mp"),
            P("mp", "dp"),
            P("dp", "mp"),
            P("mp", "dp"),
            P("dp"),
            P("dp"),
            P("dp"),
            P("dp"),
        ),
        out_specs=(
            P(("dp", "mp"), None),
            P(("dp", "mp"), None),
            P("dp", "mp"),
            P("dp", "mp"),
            P("dp", "mp"),
            P("mp", "dp"),
            P("dp", "mp"),
            P("mp", "dp"),
            P("dp"),
            P("dp"),
            P("dp"),
            P("dp"),
        ),
        check_vma=False,
    )
```

profile of v0, /device:TPU:0, one launch (start us, length us, event | category | flops | bytes accessed | tf_op | source)
XLA Modules:
  0.0 2037.0 jit_solution(9787934403674804329)
XLA Ops:
  13.5 34.9 %all-reduce.10 = (bf16[512]{0:T(512)(128)(2,1)S(1)}, bf16[512]{0:T(512)(128)(2,1)S(1)}, bf16[512]{0:T(512)(128)(2,1)S(1)}, bf16[512]{0:T(512)(128)(2,1)S(1)}) all-reduce(bf16[512]{0:T(512)(128)(2,1)S(1)} %dynamic-update-slice.1, bf16[512]{0:T(512)(128)(2,1)S(1)} %dynamic-update-slice, ...), channel_id=1, replica_groups=mesh['dp'=16,'mp'=2] {'dp'}, use_global_device_ids=true, to_apply=%add.1 | all-reduce | flops 2048 | bytes 8192
  61.5 17.8 all_gather.46
  79.3 19.9 all_gather.47
  99.3 18.1 all_gather.45
  117.4 21.1 %all_gather.48 = bf16[256,512]{0,1:T(8,128)(2,1)} all-gather(bf16[256,32]{0,1:T(8,128)(2,1)S(1)} %copy-done.42), channel_id=1, replica_groups=mesh['dp'=16,'mp'=2] {'dp'}, dimensions={1}, use_global_device_ids=true | all-gather | bytes 278528 | tf_op jit(solution)/shard_map/all_gather | solution.py:106
  140.3 36.6 %all-gather.7.cloned.1.call-done = bf16[9216,512]{1,0:T(8,128)(2,1)} async-done(((bf16[4608,512]{1,0:T(8,128)(2,1)}), bf16[9216,512]{1,0:T(8,128)(2,1)}) %all-gather.7.cloned.1.call-update) | async-done | bytes 9437200 | tf_op jit(solution)/shard_map/all_gather | solution.py:128
  176.9 8.5 convolution_convert_fusion.2
  185.3 14.3 reshape.193
  199.6 8.5 convolution_convert_fusion.3
  208.1 14.3 reshape.192
  222.4 8.5 convolution_convert_fusion.4
  230.9 14.3 reshape.191
  245.2 13.7 fusion.63
  258.9 11.2 fusion.7
  270.1 13.1 convert_bitcast_fusion.1
  283.2 9.2 copy.54
  292.4 14.2 reshape.194
  306.6 10.2 fusion.64
  317.6 211.2 %reduce-scatter.11.cloned.1.call-done = f32[4608,512]{1,0:T(8,128)} async-done(((f32[9216,512]{1,0:T(8,128)}), f32[4608,512]{1,0:T(8,128)}) %reduce-scatter.11.cloned.1.call-update) | async-done | bytes 9437200 | tf_op jit(solution)/shard_map/reduce_scatter | solution.py:143
  528.7 9.6 fusion.61
  557.2 110.9 %all-gather.9.cloned.1.call-done = bf16[9216,512]{1,0:T(8,128)(2,1)} async-done(((bf16[4608,512]{1,0:T(8,128)(2,1)}), bf16[9216,512]{1,0:T(8,128)(2,1)}) %all-gather.9.cloned.1.call-update) | async-done | bytes 9437200 | tf_op jit(solution)/shard_map/all_gather | solution.py:146
  668.1 27.6 %multiply_convert_fusion = (bf16[9216,1024]{1,0:T(8,128)(2,1)}, f32[9216,1024]{1,0:T(8,128)}) fusion(bf16[9216,512]{1,0:T(8,128)(2,1)} %all-gather.9.cloned.1.call-done, bf16[512,1024]{1,0:T(8,128)(2,1)} %all-gather.11.cloned.1.call-done), kind=kOutput, calls=%fused_computation.9 | convolution fusion | flops 9748611072 | bytes 67108864 | tf_op jit(solution)/shard_map/dot_general | solution.py:147
  695.7 12.5 all-gather.13.cloned.1.call-done
  708.2 118.5 %all-gather.15.cloned.1.call-done = bf16[9216,512]{1,0:T(8,128)(2,1)} async-done(((bf16[4608,512]{1,0:T(8,128)(2,1)}), bf16[9216,512]{1,0:T(8,128)(2,1)}) %all-gather.15.cloned.1.call-update) | async-done | bytes 9437200 | tf_op jit(solution)/shard_map/all_gather | solution.py:158
  826.6 37.9 %fusion.6 = bf16[9216,1024]{1,0:T(8,128)(2,1)} fusion(f32[9216,1024]{1,0:T(8,128)} %get-tuple-element.41, bf16[9216,512]{1,0:T(8,128)(2,1)} %all-gather.15.cloned.1.call-done, bf16[1024,512]{0,1:T(8,128)(2,1)} %all-gather.13.cloned.1.call-done), kind=kOutput, calls=%fused_computation.8 | convolution fusion | flops 9852420096 | bytes 67108864 | tf_op jit(solution)/shard_map/dot_general | solution.py:35
  864.5 17.8 fusion.65
  883.5 19.6 convolution_convert_fusion
  903.2 190.8 %reduce-scatter.15.cloned.1.call-done = f32[4608,512]{1,0:T(8,128)} async-done(((f32[9216,512]{1,0:T(8,128)}), f32[4608,512]{1,0:T(8,128)}) %reduce-scatter.15.cloned.1.call-update) | async-done | bytes 9437200 | tf_op jit(solution)/shard_map/reduce_scatter | solution.py:165
  1094.0 9.3 multiply_reduce_fusion.1
  1103.4 103.4 %reduce-scatter.13.cloned.1.call-done = bf16[4608,512]{1,0:T(8,128)(2,1)} async-done(((bf16[9216,512]{1,0:T(8,128)(2,1)}), bf16[4608,512]{1,0:T(8,128)(2,1)}) %reduce-scatter.13.cloned.1.call-update) | async-done | bytes 4718608 | tf_op jit(solution)/shard_map/reduce_scatter | solution.py:150
  1206.8 11.2 fusion.60
  1221.7 6.7 fusion.54
  1228.6 118.0 %all-gather.17.cloned.1.call-done = bf16[9216,512]{1,0:T(8,128)(2,1)} async-done(((bf16[4608,512]{1,0:T(8,128)(2,1)}), bf16[9216,512]{1,0:T(8,128)(2,1)}) %all-gather.17.cloned.1.call-update) | async-done | bytes 9437200 | tf_op jit(solution)/shard_map/all_gather | solution.py:170
  1346.6 8.5 convolution_convert_fusion.1
  1355.1 14.4 reshape.195
  1369.5 14.9 convert_bitcast_fusion
  1384.4 21.3 %multiply_reduce_fusion = (f32[192,4,48]{2,1,0:T(4,128)S(1)}, f32[192,4,48,48]{2,3,1,0:T(8,128)}) fusion(f32[192,4,48,48]{2,3,1,0:T(8,128)} %get-tuple-element.39, f32[192,4,48]{2,1,0:T(4,128)S(1)} %bitcast.56, bf16[192,48,4,64]{3,2,1,0:T(4,128)(2,1)} %reshape.191, bf16[192,48,4,64]{3,2,1,0:T(4,128)(2,1)} %reshape.195), kind=kOutput, calls=%fused_computation.14 | convolution fusion | flops 231763968 | bytes 23887872 | tf_op jit(solution)/shard_map/sqhe,skhe->shqk/dot_general | solution.py:63
  1405.7 14.1 multiply_convert_fusion.3
  1423.4 9.8 fusion.23
  1433.1 10.8 fusion.22
  1443.9 9.2 copy.63
  1453.1 14.1 reshape.198
  1467.3 9.2 copy.59
  1476.5 14.1 reshape.196
  1490.6 9.2 copy.61
  1499.8 14.2 reshape.197
  1514.0 10.4 fusion.66
  1524.4 7.9 fusion.67
  1532.3 18.4 add_convert_fusion
  1550.8 18.6 fusion.72
  1569.5 17.9 fusion.73
  1588.1 9.9 fusion.71
  1598.3 8.6 fusion.69
  1606.9 8.7 fusion.70
  1615.7 8.8 fusion.68
  1624.5 37.0 %reduce-scatter.17.cloned.1.call-done = bf16[4608,512]{1,0:T(8,128)(2,1)} async-done(((bf16[9216,512]{1,0:T(8,128)(2,1)}), bf16[4608,512]{1,0:T(8,128)(2,1)}) %reduce-scatter.17.cloned.1.call-update) | async-done | bytes 4718608 | tf_op jit(solution)/shard_map/reduce_scatter | solution.py:188
  1668.2 7.7 fusion.19
  1676.0 10.6 add_add_fusion.2
  1686.5 33.8 %all-reduce.8 = (f32[512]{0:T(512)S(1)}, f32[512]{0:T(512)S(1)}, f32[512]{0:T(512)S(1)}, f32[512]{0:T(512)S(1)}) all-reduce(f32[512]{0:T(512)S(1)} %get-tuple-element.14, f32[512]{0:T(512)S(1)} %get-tuple-element.17, f32[512]{0:T(512)S(1)} %copy-done.43, f32[512]{0:T(512)S(1)} %copy-done.44), channel_id=12, replica_groups=mesh['dp'=16,'mp'=2] {'dp'}, use_global_device_ids=true, to_apply=%region_23.24.clone | all-reduce | flops 2048 | bytes 16384
  1727.7 65.2 %reduce-scatter.29.cloned.1.call-done = f32[1024,32]{0,1:T(8,128)} async-done(((f32[1024,512]{0,1:T(8,128)}), f32[1024,32]{0,1:T(8,128)}) %reduce-scatter.29.cloned.1.call-update) | async-done | bytes 131088 | tf_op jit(solution)/shard_map/reduce_scatter | solution.py:201
  1792.9 58.8 %reduce-scatter.25.cloned.1.call-done = f32[256,32]{0,1:T(8,128)} async-done(((f32[256,512]{0,1:T(8,128)}), f32[256,32]{0,1:T(8,128)}) %reduce-scatter.25.cloned.1.call-update) | async-done | bytes 32784 | tf_op jit(solution)/shard_map/reduce_scatter | solution.py:199
  1851.8 59.4 %reduce-scatter.21.cloned.1.call-done = f32[32,256]{1,0:T(8,128)} async-done(((f32[512,256]{1,0:T(8,128)}), f32[32,256]{1,0:T(8,128)}) %reduce-scatter.21.cloned.1.call-update) | async-done | bytes 32784 | tf_op jit(solution)/shard_map/reduce_scatter | solution.py:197
  1911.2 59.0 %reduce-scatter.23.cloned.1.call-done = f32[32,256]{1,0:T(8,128)} async-done(((f32[512,256]{1,0:T(8,128)}), f32[32,256]{1,0:T(8,128)}) %reduce-scatter.23.cloned.1.call-update) | async-done | bytes 32784 | tf_op jit(solution)/shard_map/reduce_scatter | solution.py:198
  1970.1 59.2 %reduce-scatter.19.cloned.1.call-done = f32[32,256]{1,0:T(8,128)} async-done(((f32[512,256]{1,0:T(8,128)}), f32[32,256]{1,0:T(8,128)}) %reduce-scatter.19.cloned.1.call-update) | async-done | bytes 32784 | tf_op jit(solution)/shard_map/reduce_scatter | solution.py:196
  (174 shorter events, 61.5 us)
Async XLA Ops:
  8.0 168.8 %all-gather.7.cloned.1.call-start = ((), (), s32[]{:S(2)}) async-start(), calls=%async_computation.10 | async-start | bytes 14155776 | tf_op jit(solution)/shard_map/all_gather | solution.py:128
  48.4 9.0 copy-start.1
  48.4 8.4 copy-start.35
  51.6 5.2 copy-start.18
  51.6 9.9 copy-start.39
  51.6 27.7 %copy-start.40 = (bf16[32,256]{1,0:T(8,128)(2,1)S(1)}, bf16[32,256]{1,0:T(8,128)(2,1)}, u32[]{:S(2)}) copy-start(bf16[32,256]{1,0:T(8,128)(2,1)} %param.19) | copy-start | bytes 49156
  51.6 47.6 %copy-start.41 = (bf16[32,256]{1,0:T(8,128)(2,1)S(1)}, bf16[32,256]{1,0:T(8,128)(2,1)}, u32[]{:S(2)}) copy-start(bf16[32,256]{1,0:T(8,128)(2,1)} %param.20) | copy-start | bytes 49156
  51.6 65.7 %copy-start.42 = (bf16[256,32]{0,1:T(8,128)(2,1)S(1)}, bf16[256,32]{0,1:T(8,128)(2,1)}, u32[]{:S(2)}) copy-start(bf16[256,32]{0,1:T(8,128)(2,1)} %param.21) | copy-start | bytes 49156
  51.7 86.8 %copy-start.45 = (s32[192]{0:T(256)S(1)}, s32[192]{0:T(256)}, u32[]{:S(2)}) copy-start(s32[192]{0:T(256)} %param.16) | copy-start | bytes 2308
  56.2 0.6 copy-start.31
  61.4 467.3 %reduce-scatter.11.cloned.1.call-start = ((), (), s32[]{:S(2)}) async-start(), calls=%async_computation.11 | async-start | bytes 28311552 | tf_op jit(solution)/shard_map/reduce_scatter | solution.py:143
  79.3 120.3 %copy-start.14 = (bf16[512,256]{1,0:T(8,128)(2,1)}, bf16[512,256]{1,0:T(8,128)(2,1)S(1)}, u32[]{:S(2)}) copy-start(bf16[512,256]{1,0:T(8,128)(2,1)S(1)} %all_gather.46) | copy-start | bytes 786436
  99.3 86.1 %copy-start.12 = (bf16[512,256]{1,0:T(8,128)(2,1)}, bf16[512,256]{1,0:T(8,128)(2,1)S(1)}, u32[]{:S(2)}) copy-start(bf16[512,256]{1,0:T(8,128)(2,1)S(1)} %all_gather.47) | copy-start | bytes 786436
  117.4 105.0 %copy-start.10 = (bf16[512,256]{1,0:T(8,128)(2,1)}, bf16[512,256]{1,0:T(8,128)(2,1)S(1)}, u32[]{:S(2)}) copy-start(bf16[512,256]{1,0:T(8,128)(2,1)S(1)} %all_gather.45) | copy-start | bytes 786436
  258.9 11.2 copy-start.7
  258.9 11.2 copy-start.5
  292.4 14.2 copy-start.16
  316.9 240.3 %all-gather.11.cloned.1.call-start = ((), (), s32[]{:S(2)}) async-start(), calls=%async_computation.13 | async-start | bytes 1114112 | tf_op jit(solution)/shard_map/all_gather | solution.py:107
  317.5 350.6 %all-gather.9.cloned.1.call-start = ((), (), s32[]{:S(2)}) async-start(), calls=%async_computation.12 | async-start | bytes 14155776 | tf_op jit(solution)/shard_map/all_gather | solution.py:146
  317.5 227.9 %copy-start.37 = (f32[512]{0:T(512)}, f32[512]{0:T(512)S(1)}, u32[]{:S(2)}) copy-start(f32[512]{0:T(512)S(1)} %convert_element_type.113) | copy-start | bytes 6148
  538.3 7.8 copy-start
  538.3 7.2 copy-start.20
  544.9 0.6 copy-start.33
  545.5 0.6 copy-start.27
  550.1 158.1 %all-gather.13.cloned.1.call-start = ((), (), s32[]{:S(2)}) async-start(), calls=%async_computation.14 | async-start | bytes 1114112 | tf_op jit(solution)/shard_map/all_gather | solution.py:108
  550.7 276.0 %all-gather.15.cloned.1.call-start = ((), (), s32[]{:S(2)}) async-start(), calls=%async_computation.16 | async-start | bytes 14155776 | tf_op jit(solution)/shard_map/all_gather | solution.py:158
  557.1 536.9 %reduce-scatter.15.cloned.1.call-start = ((), (), s32[]{:S(2)}) async-start(), calls=%async_computation.17 | async-start | bytes 28311552 | tf_op jit(solution)/shard_map/reduce_scatter | solution.py:165
  826.6 37.9 %copy-start.46 = (bf16[512,1024]{1,0:T(8,128)(2,1)S(1)}, bf16[512,1024]{1,0:T(8,128)(2,1)}, u32[]{:S(2)}) copy-start(bf16[512,1024]{1,0:T(8,128)(2,1)} %all-gather.11.cloned.1.call-done) | copy-start | bytes 3145732
  882.3 1.2 copy-start.47
  882.3 324.5 %reduce-scatter.13.cloned.1.call-start = ((), (), s32[]{:S(2)}) async-start(), calls=%async_computation.15 | async-start | bytes 14155776 | tf_op jit(solution)/shard_map/reduce_scatter | solution.py:150
  903.2 190.9 %copy-start.21 = (f32[4608]{0:T(1024)S(1)}, f32[4608]{0:T(1024)}, u32[]{:S(2)}) copy-start(f32[4608]{0:T(1024)} %copy-done.20) | copy-start | bytes 55300
  903.2 190.9 %copy-start.28 = (f32[4608]{0:T(1024)S(1)}, f32[4608]{0:T(1024)}, u32[]{:S(2)}) copy-start(f32[4608]{0:T(1024)} %copy-done.27) | copy-start | bytes 55300
  903.2 190.9 %copy-start.38 = (f32[512]{0:T(512)S(1)}, f32[512]{0:T(512)}, u32[]{:S(2)}) copy-start(f32[512]{0:T(512)} %copy-done.37) | copy-start | bytes 6148
  903.2 200.2 %copy-start.34 = (f32[4608]{0:T(1024)S(1)}, f32[4608]{0:T(1024)}, u32[]{:S(2)}) copy-start(f32[4608]{0:T(1024)} %copy-done.33) | copy-start | bytes 55300
  903.2 443.4 %all-gather.17.cloned.1.call-start = ((), (), s32[]{:S(2)}) async-start(), calls=%async_computation.18 | async-start | bytes 14155776 | tf_op jit(solution)/shard_map/all_gather | solution.py:170
  1103.4 118.3 %copy-start.25 = (f32[4608]{0:T(1024)S(1)}, f32[4608]{0:T(1024)}, u32[]{:S(2)}) copy-start(f32[4608]{0:T(1024)} %copy-done.24) | copy-start | bytes 55300
  1218.1 3.6 copy-start.3
  1218.1 10.3 copy-start.29
  1221.7 6.8 copy-start.8
  1221.7 6.8 copy-start.9
  1221.7 124.9 %copy-start.17 = (bf16[256,512]{0,1:T(8,128)(2,1)S(1)}, bf16[256,512]{0,1:T(8,128)(2,1)}, u32[]{:S(2)}) copy-start(bf16[256,512]{0,1:T(8,128)(2,1)} %all_gather.48) | copy-start | bytes 786436
  1228.4 433.0 %reduce-scatter.17.cloned.1.call-start = ((), (), s32[]{:S(2)}) async-start(), calls=%async_computation.19 | async-start | bytes 14155776 | tf_op jit(solution)/shard_map/reduce_scatter | solution.py:188
  1419.8 3.5 copy-start.2
  1499.8 14.2 copy-start.15
  1514.0 10.4 copy-start.4
  1514.0 10.4 copy-start.13
  1524.4 7.9 copy-start.11
  1550.8 176.9 %reduce-scatter.27.cloned.1.call-start = ((), (), s32[]{:S(2)}) async-start(), calls=%async_computation.24 | async-start | bytes 2228224 | tf_op jit(solution)/shard_map/reduce_scatter | solution.py:200
  1569.4 223.5 %reduce-scatter.29.cloned.1.call-start = ((), (), s32[]{:S(2)}) async-start(), calls=%async_computation.25 | async-start | bytes 2228224 | tf_op jit(solution)/shard_map/reduce_scatter | solution.py:201
  1587.4 264.4 %reduce-scatter.25.cloned.1.call-start = ((), (), s32[]{:S(2)}) async-start(), calls=%async_computation.23 | async-start | bytes 557056 | tf_op jit(solution)/shard_map/reduce_scatter | solution.py:199
  1598.1 313.1 %reduce-scatter.21.cloned.1.call-start = ((), (), s32[]{:S(2)}) async-start(), calls=%async_computation.21 | async-start | bytes 557056 | tf_op jit(solution)/shard_map/reduce_scatter | solution.py:197
  1606.9 363.3 %reduce-scatter.23.cloned.1.call-start = ((), (), s32[]{:S(2)}) async-start(), calls=%async_computation.22 | async-start | bytes 557056 | tf_op jit(solution)/shard_map/reduce_scatter | solution.py:198
  1615.6 45.9 %copy-start.19 = (f32[4608]{0:T(1024)S(1)}, f32[4608]{0:T(1024)}, u32[]{:S(2)}) copy-start(f32[4608]{0:T(1024)} %copy-done.18) | copy-start | bytes 55300
  1615.6 45.8 %copy-start.36 = (f32[512]{0:T(512)S(1)}, f32[512]{0:T(512)}, u32[]{:S(2)}) copy-start(f32[512]{0:T(512)} %copy-done.35) | copy-start | bytes 6148
  1615.6 413.7 %reduce-scatter.19.cloned.1.call-start = ((), (), s32[]{:S(2)}) async-start(), calls=%async_computation.20 | async-start | bytes 557056 | tf_op jit(solution)/shard_map/reduce_scatter | solution.py:196
  1624.5 43.7 %copy-start.32 = (f32[4608]{0:T(1024)S(1)}, f32[4608]{0:T(1024)}, u32[]{:S(2)}) copy-start(f32[4608]{0:T(1024)} %copy-done.31) | copy-start | bytes 55300
  1624.5 43.7 %copy-start.23 = (f32[4608]{0:T(1024)S(1)}, f32[4608]{0:T(1024)}, u32[]{:S(2)}) copy-start(f32[4608]{0:T(1024)} %copy-done.22) | copy-start | bytes 55300
  1624.5 51.4 %slice-start = ((s8[4718592]{0:T(1024)(128)(4,1)}), s8[524288]{0:T(1024)(128)(4,1)S(1)}, s32[]{:S(2)}) async-start(s8[4718592]{0:T(1024)(128)(4,1)} %bitcast.53), calls=%async_computation.26 | async-start | bytes 1048576
  1624.5 51.4 %copy-start.26 = (f32[4608]{0:T(1024)S(1)}, f32[4608]{0:T(1024)}, u32[]{:S(2)}) copy-start(f32[4608]{0:T(1024)} %copy-done.24) | copy-start | bytes 55300
  1624.5 51.4 %copy-start.30 = (f32[4608]{0:T(1024)S(1)}, f32[4608]{0:T(1024)}, u32[]{:S(2)}) copy-start(f32[4608]{0:T(1024)} %copy-done.29) | copy-start | bytes 55300
  1661.5 6.7 copy-start.6
  1668.2 7.7 slice-start.1
  1676.0 10.6 copy-start.43
  1676.0 10.6 copy-start.44
  (2 other events, 1.2 us)
Sparse Core Ops, SparseCore 0:
  61.5 115.2 all-gather.6
  317.0 211.6 reduce-scatter.10
  1228.6 117.9 all-gather.16
  1550.9 110.5 reduce-scatter.16
  1665.6 62.0 reduce-scatter.26
  1732.3 60.5 reduce-scatter.28
  1797.1 54.6 reduce-scatter.24
  1856.3 54.7 reduce-scatter.20
  1915.3 54.8 reduce-scatter.22
  1974.5 54.7 reduce-scatter.18
Sparse Core Ops, SparseCore 1:
  319.5 38.1 all-gather.10
  550.2 117.8 all-gather.8
  670.1 38.0 all-gather.12
  709.7 116.9 all-gather.14
  882.4 211.5 reduce-scatter.14
  1096.3 110.4 reduce-scatter.12
where the time goes:
time: 2050 us; the launch traced here: 2040 us
  waiting for transfers between devices  1240 us (60%)
  matrix products  340 us (17%)
  local copies, waits for them, and re-layouts  167 us (8%)
  blocking collectives  151 us (7%)
  other arithmetic  116 us (6%)
    reduce_scatter x1, waiting for transfers between devices, shards(): lax.psum_scatter(attn_part, 'mp', scatter_dimension=0, tiled=True)  211 us
    reduce_scatter x1, waiting for transfers between devices, shards(): lax.psum_scatter(grad_two_part, 'mp', scatter_dimension=0, tiled=True)  191 us
    all_gather x1, waiting for transfers between devices, shards(): grad_out_all = lax.all_gather(grad_out, 'mp', axis=0, tiled=True)  118 us
    all_gather x1, waiting for transfers between devices, shards(): grad_attended_all = lax.all_gather(grad_attended, 'mp', axis=0, tiled=True)  118 us
    all_gather x1, waiting for transfers between devices, shards(): normed_two_all = lax.all_gather(normed_two, 'mp', axis=0, tiled=True)  111 us
    reduce_scatter x1, waiting for transfers between devices, shards(): lax.psum_scatter(down_part.astype(jnp.bfloat16), 'mp', scatter_dimension=...  103 us
    dot_general x6, matrix products, times_transposed(): lax.dot_general(left, right, (((1,), (1,)), ((), ())), preferred_element_...  101 us
    dot_general x6, matrix products, inner(): lax.dot_general(left, right, (((0,), (0,)), ((), ())), preferred_element_...  72.4 us
  transfers between devices with their start and end apart: 16, of which 15 were waited for; matrix products, arithmetic and copies ran while one was open for 9% of the time, Pallas kernels for 0%

commit v1 on v0

v1 whole, which is shorter than its diff:
```python
import jax
import jax.numpy as jnp
from jax import lax
from jax.experimental import pallas as pl
from jax.experimental.pallas import tpu as pltpu
from jax.sharding import PartitionSpec as P

D = 512
FF = 2048
HEAD = 64
FTOK = 8
SEQ = 48
HALVES = 2
HW = D // HALVES
FW = FF // HALVES
GC = 128
EPS = 1e-05
SEQS_STEP = 8
ROWS = SEQS_STEP * SEQ
BF = jnp.bfloat16
F32 = jnp.float32


def nn(a, b):
    return lax.dot_general(a, b, (((1,), (0,)), ((), ())), preferred_element_type=F32)


def nt(a, b):
    return lax.dot_general(a, b, (((1,), (1,)), ((), ())), preferred_element_type=F32)


def tn(a, b):
    return lax.dot_general(a, b, (((0,), (0,)), ((), ())), preferred_element_type=F32)


def norm_parts(rows):
    mean = jnp.mean(rows, axis=-1, keepdims=True)
    centered = rows - mean
    spread = jnp.mean(centered * centered, axis=-1, keepdims=True)
    rstd = lax.rsqrt(spread + EPS)
    return centered * rstd, rstd


def norm_back(n, rstd, gain, gy):
    gg = gy * gain
    first = jnp.mean(gg, axis=-1, keepdims=True)
    second = jnp.mean(gg * n, axis=-1, keepdims=True)
    return rstd * (gg - first - n * second)


def fold_rows(value):
    return jnp.sum(value.reshape(value.shape[0] // 8, 8, value.shape[1]), axis=0)


def per_head(rows):
    width = rows.shape[1]
    lane = lax.broadcasted_iota(jnp.int32, rows.shape, 1) // HEAD
    pad = jnp.zeros((HEAD - SEQ, width), rows.dtype)
    parts = []
    for h in range(width // HEAD):
        parts.append(jnp.where(lane == h, rows, jnp.zeros_like(rows)))
        parts.append(pad)
    return jnp.concatenate(parts, axis=0)


def pair_blocks(product):
    lane = lax.broadcasted_iota(jnp.int32, (SEQ, 2 * HEAD), 1)
    return jnp.where(lane < HEAD, product[:SEQ], product[HEAD : HEAD + SEQ])


def seq_slice(s, c, width):
    return (slice(s * SEQ, (s + 1) * SEQ), slice(c * width, (c + 1) * width))


def attn_forward_kernel(
    frames, x_ref, wa_ref, vec_ref, q_ref, k_ref, v_ref, p_ref, ho_ref, hidden_ref, s_ref
):
    step = pl.program_id(0)
    x = x_ref[...].astype(F32)
    n, _ = norm_parts(x)
    normed = (n * vec_ref[0:1] + vec_ref[1:2]).astype(BF)
    for m in range(HALVES):
        qkv = nn(normed, wa_ref[m, :, : 3 * HW]).astype(BF)
        cols = slice(m * HW, (m + 1) * HW)
        q_ref[:, cols] = qkv[:, :HW]
        k_ref[:, cols] = qkv[:, HW : 2 * HW]
        v_ref[:, cols] = qkv[:, 2 * HW :]
    for s in range(SEQS_STEP):
        for m in range(HALVES):
            at = seq_slice(s, m, HW)
            s_ref[at] = nt(k_ref[at], per_head(q_ref[at]))
    key = lax.broadcasted_iota(jnp.int32, (SEQ, 2 * HEAD), 0)
    query = lax.broadcasted_iota(jnp.int32, (SEQ, 2 * HEAD), 1) % HEAD
    for s in range(SEQS_STEP):
        allowed = (key <= query) & (key < frames[step * SEQS_STEP + s] * FTOK)
        for c in range(D // (2 * HEAD)):
            at = seq_slice(s, c, 2 * HEAD)
            scores = jnp.where(allowed, s_ref[at] * HEAD**-0.5, -1000000000.0)
            expd = jnp.exp(scores - jnp.max(scores, axis=0, keepdims=True))
            p_ref[at] = (expd * (1.0 / jnp.sum(expd, axis=0, keepdims=True))).astype(BF)
    for s in range(SEQS_STEP):
        for c in range(D // (2 * HEAD)):
            at = seq_slice(s, c, 2 * HEAD)
            ho_ref[at] = pair_blocks(tn(p_ref[at], v_ref[at])).astype(BF)
    attended = nt(ho_ref[:, :HW], wa_ref[0, :, 3 * HW : 4 * HW])
    attended += nt(ho_ref[:, HW:], wa_ref[1, :, 3 * HW : 4 * HW])
    hidden_ref[...] = x + attended


GELU_A = (2.0 / jnp.pi) ** 0.5
GELU_B = 0.044715


def feed_forward_kernel(
    live, hidden_ref, cot_ref, wf_ref, vec_ref, mixed_ref, gh_ref, gf_ref, gv_ref,
    acc_ref, gvacc_ref, act_ref, gup_ref, go_ref,
):
    step = pl.program_id(0)
    last = pl.num_programs(0) - 1

    @pl.when(step == 0)
    def _():
        acc_ref[...] = jnp.zeros_like(acc_ref)
        gvacc_ref[...] = jnp.zeros_like(gvacc_ref)

    hidden = hidden_ref[...]
    n, rstd = norm_parts(hidden)
    normed = (n * vec_ref[2:3] + vec_ref[3:4]).astype(BF)
    row = lax.broadcasted_iota(jnp.int32, (ROWS, 1), 0) + step * ROWS
    go = jnp.where(row < live[0] * SEQ, cot_ref[...].astype(F32), 0.0)
    go_ref[...] = go.astype(BF)
    for m in range(HALVES):
        cols = slice(m * FW, (m + 1) * FW)
        up = nn(normed, wf_ref[m, :, :FW])
        ga = nn(go_ref[...], wf_ref[m, :, FW:])
        sq = up * up
        th = jnp.tanh(up * (GELU_A + (GELU_A * GELU_B) * sq))
        half = 0.5 + 0.5 * th
        act_ref[:, cols] = (up * half).astype(BF)
        slope = half + (0.5 * up) * (1.0 - th * th) * (GELU_A + (3.0 * GELU_A * GELU_B) * sq)
        gup_ref[:, cols] = (ga * slope).astype(BF)
    down = jnp.zeros((ROWS, D), F32)
    gy = jnp.zeros((ROWS, D), F32)
    for m in range(HALVES):
        cols = slice(m * FW, (m + 1) * FW)
        down += nt(act_ref[:, cols], wf_ref[m, :, FW:])
        gy += nt(gup_ref[:, cols], wf_ref[m, :, :FW])
        acc_ref[m, :, :FW] += tn(normed, gup_ref[:, cols])
        acc_ref[m, :, FW:] += tn(go_ref[...], act_ref[:, cols])
    mixed_ref[...] = (hidden + down).astype(BF)
    gh_ref[...] = go + norm_back(n, rstd, vec_ref[2:3], gy)
    gvacc_ref[0] += fold_rows(gy * n)
    gvacc_ref[1] += fold_rows(gy)

    @pl.when(step == last)
    def _():
        gf_ref[...] = acc_ref[...].astype(BF)
        gv_ref[0:1] = jnp.sum(gvacc_ref[0], axis=0, keepdims=True)
        gv_ref[1:2] = jnp.sum(gvacc_ref[1], axis=0, keepdims=True)


def attn_backward_kernel(
    x_ref, gh_ref, q_ref, k_ref, v_ref, p_ref, ho_ref, wa_ref, vec_ref, gi_ref, ga_ref, gv_ref,
    acc_ref, gvacc_ref, s_ref, ds_ref, dh_ref, dqkv_ref,
):
    step = pl.program_id(0)
    last = pl.num_programs(0) - 1

    @pl.when(step == 0)
    def _():
        acc_ref[...] = jnp.zeros_like(acc_ref)
        gvacc_ref[...] = jnp.zeros_like(gvacc_ref)

    x = x_ref[...].astype(F32)
    n, rstd = norm_parts(x)
    normed = (n * vec_ref[0:1] + vec_ref[1:2]).astype(BF)
    gh = gh_ref[...]
    gat = gh.astype(BF)
    for m in range(HALVES):
        cols = slice(m * HW, (m + 1) * HW)
        wo = slice(3 * HW, 4 * HW)
        dh_ref[:, cols] = nn(gat, wa_ref[m, :, wo]).astype(BF)
        acc_ref[m, :, wo] += tn(gat, ho_ref[:, cols])
    for s in range(SEQS_STEP):
        for m in range(HALVES):
            at = seq_slice(s, m, HW)
            s_ref[at] = nt(v_ref[at], per_head(dh_ref[at]))
    for s in range(SEQS_STEP):
        for c in range(D // (2 * HEAD)):
            at = seq_slice(s, c, 2 * HEAD)
            probs = p_ref[at].astype(F32)
            gp = s_ref[at]
            delta = jnp.sum(probs * gp, axis=0, keepdims=True)
            ds_ref[at] = (probs * ((gp - delta) * HEAD**-0.5)).astype(BF)
    for s in range(SEQS_STEP):
        for m in range(HALVES):
            at = seq_slice(s, m, HW)
            rows = at[0]
            base = 3 * HW * m
            dqkv_ref[rows, base + 2 * HW : base + 3 * HW] = nn(p_ref[at], per_head(dh_ref[at])).astype(BF)
            dqkv_ref[rows, base + HW : base + 2 * HW] = nn(ds_ref[at], per_head(q_ref[at])).astype(BF)
    for s in range(SEQS_STEP):
        for c in range(D // (2 * HEAD)):
            at = seq_slice(s, c, 2 * HEAD)
            base = 3 * HW * (c // 2) + 2 * HEAD * (c % 2)
            dqkv_ref[at[0], base : base + 2 * HEAD] = pair_blocks(tn(ds_ref[at], k_ref[at])).astype(BF)
    gy = jnp.zeros((ROWS, D), F32)
    for m in range(HALVES):
        cols = slice(3 * HW * m, 3 * HW * (m + 1))
        gy += nt(dqkv_ref[:, cols], wa_ref[m, :, : 3 * HW])
        acc_ref[m, :, : 3 * HW] += tn(normed, dqkv_ref[:, cols])
    gi_ref[...] = gh + norm_back(n, rstd, vec_ref[0:1], gy)
    gvacc_ref[0] += fold_rows(gy * n)
    gvacc_ref[1] += fold_rows(gy)

    @pl.when(step == last)
    def _():
        ga_ref[...] = acc_ref[...].astype(BF)
        gv_ref[0:1] = jnp.sum(gvacc_ref[0], axis=0, keepdims=True)
        gv_ref[1:2] = jnp.sum(gvacc_ref[1], axis=0, keepdims=True)


def row_block(width):
    return pl.BlockSpec((ROWS, width), lambda i, *_: (i, 0))


def held(shape):
    return pl.BlockSpec(shape, lambda i, *_: (0,) * len(shape), pipeline_mode=pl.Buffered(1))


def shape(dims, dtype):
    return jax.ShapeDtypeStruct(dims, dtype)


PARAMS = pltpu.CompilerParams(vmem_limit_bytes=56 * 1024 * 1024)


def attn_forward(frames, tokens, wa, vec):
    rows = tokens.shape[0]
    return pl.pallas_call(
        attn_forward_kernel,
        grid_spec=pltpu.PrefetchScalarGridSpec(
            num_scalar_prefetch=1,
            grid=(rows // ROWS,),
            in_specs=[row_block(D), held(wa.shape), held(vec.shape)],
            out_specs=[row_block(D)] * 6,
            scratch_shapes=[pltpu.VMEM((ROWS, D), F32)],
        ),
        out_shape=[shape((rows, D), BF)] * 5 + [shape((rows, D), F32)],
        compiler_params=PARAMS,
        name="attn_forward",
    )(frames, tokens, wa, vec)


def feed_forward(live, hidden, cotangent, wf, vec):
    rows = hidden.shape[0]
    return pl.pallas_call(
        feed_forward_kernel,
        grid_spec=pltpu.PrefetchScalarGridSpec(
            num_scalar_prefetch=1,
            grid=(rows // ROWS,),
            in_specs=[row_block(D), row_block(D), held(wf.shape), held(vec.shape)],
            out_specs=[row_block(D), row_block(D), held(wf.shape), held((2, D))],
            scratch_shapes=[
                pltpu.VMEM(wf.shape, F32),
                pltpu.VMEM((2, 8, D), F32),
                pltpu.VMEM((ROWS, FF), BF),
                pltpu.VMEM((ROWS, FF), BF),
                pltpu.VMEM((ROWS, D), BF),
            ],
        ),
        out_shape=[
            shape((rows, D), BF),
            shape((rows, D), F32),
            shape(wf.shape, BF),
            shape((2, D), F32),
        ],
        compiler_params=PARAMS,
        name="feed_forward",
    )(live, hidden, cotangent, wf, vec)


def attn_backward(tokens, gh, q, k, v, p, ho, wa, vec):
    rows = tokens.shape[0]
    return pl.pallas_call(
        attn_backward_kernel,
        grid=(rows // ROWS,),
        in_specs=[row_block(D)] * 7 + [held(wa.shape), held(vec.shape)],
        out_specs=[row_block(D), held(wa.shape), held((2, D))],
        scratch_shapes=[
            pltpu.VMEM(wa.shape, F32),
            pltpu.VMEM((2, 8, D), F32),
            pltpu.VMEM((ROWS, D), F32),
            pltpu.VMEM((ROWS, D), BF),
            pltpu.VMEM((ROWS, D), BF),
            pltpu.VMEM((ROWS, 3 * D), BF),
        ],
        out_shape=[shape((rows, D), F32), shape(wa.shape, BF), shape((2, D), F32)],
        compiler_params=PARAMS,
        name="attn_backward",
    )(tokens, gh, q, k, v, p, ho, wa, vec)


def merge_parts(gathered, parts):
    mp, depth, columns = gathered.shape
    if mp == HALVES:
        return gathered
    width = columns // parts
    split = gathered.reshape(HALVES, mp // HALVES, depth, parts, width)
    return split.transpose(0, 2, 3, 1, 4).reshape(HALVES, depth, -1)


def split_parts(whole, parts, mp):
    if mp == HALVES:
        return whole
    depth = whole.shape[1]
    split = whole.reshape(HALVES, depth, parts, mp // HALVES, -1)
    return split.transpose(0, 3, 1, 2, 4).reshape(mp, depth, -1)


def build(mesh):
    n_dp, n_mp = mesh.shape["dp"], mesh.shape["mp"]

    def gather(block):
        out = lax.all_gather(block, ("mp", "dp"), axis=0, tiled=True)
        return out.reshape(n_mp, n_dp * block.shape[0], block.shape[1])

    def scatter(whole):
        flat = whole.reshape(-1, whole.shape[-1])
        return lax.psum_scatter(flat, ("mp", "dp"), scatter_dimension=0, tiled=True)

    def shards(
        tokens, cotangent, frame_count, live_count, w_query, w_key, w_value, w_out, w_up, w_down,
        gain_one, shift_one, gain_two, shift_two,
    ):
        place = lax.axis_index("mp")
        seqs = tokens.shape[0] // SEQ
        frames = lax.dynamic_slice(frame_count, (place * seqs,), (seqs,))
        live = live_count - place * seqs
        vec = jnp.stack([gain_one, shift_one, gain_two, shift_two], axis=1)
        depth = vec.shape[0]
        vec = jnp.pad(vec, ((0, 0), (0, GC - 4)))
        own_a = jnp.concatenate([w_query, w_key, w_value, w_out.T, vec], axis=1)
        own_f = jnp.concatenate([w_up, w_down.T], axis=1)
        got_a = gather(own_a)
        vec = got_a[0, :, -GC:-GC + 4].T.astype(F32)
        wa = merge_parts(got_a[:, :, :-GC], 4)
        wf = merge_parts(gather(own_f), 2)
        q, k, v, p, ho, hidden = attn_forward(frames, tokens, wa, vec)
        mixed, gh, gf, gv_two = feed_forward(live, hidden, cotangent, wf, vec)
        grad_input, ga, gv_one = attn_backward(tokens, gh, q, k, v, p, ho, wa, vec)
        gvec = jnp.concatenate([gv_one, gv_two], axis=0).T.astype(BF)
        gvec = jnp.broadcast_to(jnp.pad(gvec, ((0, 0), (0, GC - 4))), (n_mp, D, GC))
        gf_own = scatter(split_parts(gf, 2, n_mp)).astype(F32)
        ga_own = scatter(jnp.concatenate([split_parts(ga, 4, n_mp), gvec], axis=2)).astype(F32)
        wide = w_query.shape[1]
        tall = w_up.shape[1]
        gains = ga_own[:, 4 * wide :]
        return (
            mixed,
            grad_input,
            ga_own[:, :wide],
            ga_own[:, wide : 2 * wide],
            ga_own[:, 2 * wide : 3 * wide],
            ga_own[:, 3 * wide : 4 * wide].T,
            gf_own[:, :tall],
            gf_own[:, tall:].T,
            gains[:, 0],
            gains[:, 1],
            gains[:, 2],
            gains[:, 3],
        )

    return shards


def solution(mesh):
    rows = P(("dp", "mp"), None)
    wide, tall, dp = P("dp", "mp"), P("mp", "dp"), P("dp")
    return jax.shard_map(
        build(mesh),
        mesh=mesh,
        in_specs=(rows, rows, dp, dp, wide, wide, wide, tall, wide, tall, dp, dp, dp, dp),
        out_specs=(rows, rows, wide, wide, wide, tall, wide, tall, dp, dp, dp, dp),
        check_vma=False,
    )
```

time: 2050 us -> 528 us (0.26)
  waiting for transfers between devices: 1240 us -> 323 us
  matrix products: 340 us -> 0 us
  Pallas kernels: 0 us -> 167 us
  local copies, waits for them, and re-layouts: 167 us -> 13.2 us
  blocking collectives: 151 us -> 0 us
  other arithmetic: 116 us -> 8.93 us
    reduce_scatter x10 -> x2, waiting for transfers between devices: 846 us -> 236 us  [scatter(): return lax.psum_scatter(flat, ('mp', 'dp'), scatter_dimension=0, tiled=True)]
    dot_general x24 -> x0, matrix products: 340 us -> none  [the longest x6 101 us: times_transposed(): lax.dot_general(left, right, (((1,), (1,)), ((), ())), preferred_element_...]
    all_gather x6 -> x2, waiting for transfers between devices: 396 us -> 86.2 us  [gather(): out = lax.all_gather(block, ('mp', 'dp'), axis=0, tiled=True)]
    pallas_call x0 -> x3, Pallas kernels: none -> 167 us  [the longest x1 88.2 us: feed_forward(): pl.pallas_call(feed_forward_kernel, grid_spec=pltpu.PrefetchScalarGridSpe...]
    reshape x8 -> x0, local copies, waits for them, and re-layouts: 114 us -> none  [the longest x3 42.9 us: split_heads(): value.astype(jnp.bfloat16).reshape(seqs_here, seqlen, heads_here, HEAD)]
    all_gather x4 -> x0, blocking collectives: 76.9 us -> none  [the longest x1 21.1 us: shards(): lax.all_gather(w_out, 'dp', axis=1, tiled=True)]
    reduce_sum x9 -> x0, other arithmetic: 69.9 us -> none  [the longest x3 23.7 us: layer_norm(): return centered * lax.rsqrt(spread + EPS) * gain + shift]
    unnamed x2 -> x0, blocking collectives: 68.7 us -> none
  transfers between devices with their start and end apart: 16 -> 4, of which waited for: 15 -> 4; matrix products, arithmetic and copies ran while one was open for 9% -> 2% of each run, Pallas kernels for 0% -> 6%
where the time goes in v1:
time: 528 us; the launch traced here: 527 us
  waiting for transfers between devices  323 us (61%)
  Pallas kernels  167 us (32%)
  between operations  14.5 us (3%)
  local copies, waits for them, and re-layouts  13.2 us (2%)
  other arithmetic  8.93 us (2%)
    reduce_scatter x2, waiting for transfers between devices, scatter(): return lax.psum_scatter(flat, ('mp', 'dp'), scatter_dimension=0, tiled=True)  236 us
    pallas_call x1, Pallas kernels, feed_forward(): pl.pallas_call(feed_forward_kernel, grid_spec=pltpu.PrefetchScalarGridSpe...  88.2 us
    all_gather x2, waiting for transfers between devices, gather(): out = lax.all_gather(block, ('mp', 'dp'), axis=0, tiled=True)  86.2 us
    pallas_call x1, Pallas kernels, attn_backward(): pl.pallas_call(attn_backward_kernel, grid=(rows // ROWS,), in_specs=[row_...  48.9 us
    pallas_call x1, Pallas kernels, attn_forward(): pl.pallas_call(attn_forward_kernel, grid_spec=pltpu.PrefetchScalarGridSpe...  30 us
  transfers between devices with their start and end apart: 4, of which 4 were waited for; matrix products, arithmetic and copies ran while one was open for 2% of the time, Pallas kernels for 6%

profile of v1, /device:TPU:0, one launch (start us, length us, event | category | flops | bytes accessed | tf_op | source)
XLA Modules:
  0.0 526.9 jit_solution(769912844461370683)
XLA Ops:
  7.2 0.0 all-gather.3.cloned.1.call-start
  7.2 0.7 pad_maximum_fusion.2
  7.9 0.1 copy.34
  8.0 0.7 constant_dynamic-update-slice_fusion.3
  8.8 0.7 constant_dynamic-update-slice_fusion.2
  9.5 0.7 constant_dynamic-update-slice_fusion.1
  10.2 0.7 bitcast_dynamic-update-slice_fusion
  10.9 0.0 copy-start
  10.9 0.6 copy-done
  11.6 0.0 all-gather.3.cloned.1.call-update
  11.6 0.0 all-gather.5.cloned.1.call-start
  11.6 1.5 pad_maximum_fusion.1
  13.2 0.0 all-gather.5.cloned.1.call-update
  13.2 0.0 reduce-scatter.3.cloned.1.call-start
  13.9 1.3 dynamic_slice.3.frames
  15.2 56.5 %all-gather.3.cloned.1.call-done = bf16[1024,1152]{1,0:T(8,128)(2,1)} async-done(((bf16[32,1152]{1,0:T(8,128)(2,1)}), bf16[1024,1152]{1,0:T(8,128)(2,1)}) %all-gather.3.cloned.1.call-update) | async-done | bytes 2359312 | tf_op jit(solution)/shard_map/all_gather | solution.py:325
  71.6 3.1 slice.53.wa_ref
  74.7 0.9 slice_convert_fusion
  75.7 0.1 copy.36
  75.8 0.6 bitcast_bitcast_fusion.vec_ref
  76.4 30.0 %attn_forward.1 = (bf16[4608,512]{1,0:T(8,128)(2,1)}, bf16[4608,512]{1,0:T(8,128)(2,1)}, bf16[4608,512]{1,0:T(8,128)(2,1)}, bf16[4608,512]{1,0:T(8,128)(2,1)}, b...) custom-call(s32[96]{0:T(128)} %dynamic_slice.3.frames, bf16[4608,512]{1,0:T(8,128)(2,1)} %x_ref.3, ...), custom_call_target="tpu_custom_call" | custom-call | tf_op jit(solution)/shard_map/attn_forward/pallas_call | solution.py:240
  106.4 29.7 %all-gather.5.cloned.1.call-done = bf16[1024,2048]{1,0:T(8,128)(2,1)} async-done(((bf16[32,2048]{1,0:T(8,128)(2,1)}), bf16[1024,2048]{1,0:T(8,128)(2,1)}) %all-gather.5.cloned.1.call-update) | async-done | bytes 4194320 | tf_op jit(solution)/shard_map/all_gather | solution.py:325
  136.1 88.2 %feed_forward.1 = (bf16[4608,512]{1,0:T(8,128)(2,1)}, f32[4608,512]{1,0:T(8,128)}, bf16[2,512,2048]{2,1,0:T(8,128)(2,1)}, f32[2,512]{1,0:T(2,128)}) custom-call(s32[1]{0:T(128)S(6)} %sub.7.live, f32[4608,512]{1,0:T(8,128)} %get-tuple-element.25.hidden_ref, bf16[4608,512]{1,0:T(8,128)(2,1)} %cot_ref.1, bf16[2,512,2048]{2,1,0:T(8,128)(2,1)} %bitcast.25, ...), custom_call_target="tpu_custom_call" | custom-call | tf_op jit(solution)/shard_map/feed_forward/pallas_call | solution.py:257
  224.3 0.0 copy-start.1
  224.3 48.9 %attn_backward.1 = (f32[4608,512]{1,0:T(8,128)}, bf16[2,512,1024]{2,1,0:T(8,128)(2,1)}, f32[2,512]{1,0:T(2,128)}) custom-call(bf16[4608,512]{1,0:T(8,128)(2,1)} %x_ref.3, f32[4608,512]{1,0:T(8,128)} %get-tuple-element.27.gh_ref, bf16[4608,512]{1,0:T(8,128)(2,1)} %get-tuple-element.28.q_ref, bf16[4608,512]{1,0:T(8,128)(2,1)} %get-tuple-element.29.k_ref, ...), custom_call_target="tpu_custom_call" | custom-call | tf_op jit(solution)/shard_map/attn_backward/pallas_call | solution.py:285
  273.2 0.7 convert.8
  273.8 0.0 copy-done.1
  273.9 0.2 copy.35
  274.1 3.2 pad_maximum_fusion
  277.4 0.0 reduce-scatter.3.cloned.1.call-update
  277.4 0.0 reduce-scatter.5.cloned.1.call-start
  277.4 0.5 reduce-scatter.5.cloned.1.call-update
  278.0 97.1 %reduce-scatter.3.cloned.1.call-done = bf16[32,1152]{1,0:T(8,128)(2,1)} async-done(((bf16[1024,1152]{1,0:T(8,128)(2,1)}), bf16[32,1152]{1,0:T(8,128)(2,1)}) %reduce-scatter.3.cloned.1.call-update) | async-done | bytes 73744 | tf_op jit(solution)/shard_map/reduce_scatter | solution.py:330
  375.1 0.9 convert_element_type.25
  376.0 0.7 slice_reduce_fusion
  376.7 1.4 fusion
  378.1 139.2 %reduce-scatter.5.cloned.1.call-done = bf16[32,2048]{1,0:T(8,128)(2,1)} async-done(((bf16[1024,2048]{1,0:T(8,128)(2,1)}), bf16[32,2048]{1,0:T(8,128)(2,1)}) %reduce-scatter.5.cloned.1.call-update) | async-done | bytes 131088 | tf_op jit(solution)/shard_map/reduce_scatter | solution.py:330
  517.3 0.9 convert_element_type.26
  518.2 0.7 slice_bitcast_fusion
  518.9 1.5 slice.59
  (5 shorter events, 0.1 us)
Async XLA Ops:
  7.2 64.5 %all-gather.3.cloned.1.call-start = ((), (), s32[]{:S(2)}) async-start(), calls=%async_computation.2 | async-start | bytes 2433024 | tf_op jit(solution)/shard_map/all_gather | solution.py:325
  10.9 0.6 copy-start
  11.6 124.5 %all-gather.5.cloned.1.call-start = ((), (), s32[]{:S(2)}) async-start(), calls=%async_computation.3 | async-start | bytes 4325376 | tf_op jit(solution)/shard_map/all_gather | solution.py:325
  13.2 361.9 %reduce-scatter.3.cloned.1.call-start = ((), (), s32[]{:S(2)}) async-start(), calls=%async_computation.4 | async-start | bytes 2433024 | tf_op jit(solution)/shard_map/reduce_scatter | solution.py:330
  224.3 49.6 %copy-start.1 = (f32[2,512]{1,0:T(2,128)S(1)}, f32[2,512]{1,0:T(2,128)}, u32[]{:S(2)}) copy-start(f32[2,512]{1,0:T(2,128)} %get-tuple-element.36) | copy-start | bytes 12292
  277.4 239.9 %reduce-scatter.5.cloned.1.call-start = ((), (), s32[]{:S(2)}) async-start(), calls=%async_computation.5 | async-start | bytes 4325376 | tf_op jit(solution)/shard_map/reduce_scatter | solution.py:330
Sparse Core Ops, SparseCore 0:
  11.7 59.8 all-gather.2
  75.1 60.9 all-gather.4
  277.5 97.5 reduce-scatter.2
  377.3 139.9 reduce-scatter.4

commit v2 on v1

v2 whole, which is shorter than its diff:
```python
import jax
import jax.numpy as jnp
from jax import lax
from jax.experimental import pallas as pl
from jax.experimental.pallas import tpu as pltpu
from jax.sharding import PartitionSpec as P

D = 512
FF = 2048
HEAD = 64
FTOK = 8
SEQ = 48
HALVES = 2
HW = D // HALVES
FW = FF // HALVES
GC = 128
EPS = 1e-05
SEQS_STEP = 8
ROWS = SEQS_STEP * SEQ
BF = jnp.bfloat16
F32 = jnp.float32


def nn(a, b):
    return lax.dot_general(a, b, (((1,), (0,)), ((), ())), preferred_element_type=F32)


def nt(a, b):
    return lax.dot_general(a, b, (((1,), (1,)), ((), ())), preferred_element_type=F32)


def tn(a, b):
    return lax.dot_general(a, b, (((0,), (0,)), ((), ())), preferred_element_type=F32)


def norm_parts(rows):
    mean = jnp.mean(rows, axis=-1, keepdims=True)
    centered = rows - mean
    spread = jnp.mean(centered * centered, axis=-1, keepdims=True)
    rstd = lax.rsqrt(spread + EPS)
    return centered * rstd, rstd


def norm_back(n, rstd, gain, gy):
    gg = gy * gain
    first = jnp.mean(gg, axis=-1, keepdims=True)
    second = jnp.mean(gg * n, axis=-1, keepdims=True)
    return rstd * (gg - first - n * second)


def fold_rows(value):
    return jnp.sum(value.reshape(value.shape[0] // 8, 8, value.shape[1]), axis=0)


def per_head(rows):
    width = rows.shape[1]
    lane = lax.broadcasted_iota(jnp.int32, rows.shape, 1) // HEAD
    pad = jnp.zeros((HEAD - SEQ, width), rows.dtype)
    parts = []
    for h in range(width // HEAD):
        parts.append(jnp.where(lane == h, rows, jnp.zeros_like(rows)))
        parts.append(pad)
    return jnp.concatenate(parts, axis=0)


def pair_blocks(product):
    lane = lax.broadcasted_iota(jnp.int32, (SEQ, 2 * HEAD), 1)
    return jnp.where(lane < HEAD, product[:SEQ], product[HEAD : HEAD + SEQ])


def seq_slice(s, c, width):
    return (slice(s * SEQ, (s + 1) * SEQ), slice(c * width, (c + 1) * width))


def block_place(place, cr, xr, yr, zr):
    z, x, c, y = place[0], place[1], place[2], place[3]
    z = lax.rem(z - zr + place[4], place[4])
    return (y ^ yr, z * 4 + (x ^ xr) * 2 + (c ^ cr))


def load_pieces(place, pieces, metas, dst, sems):
    copies = []
    for piece, meta in zip(pieces, metas):
        depth = piece.shape[0] // len(meta)
        n_dp = D // depth
        for b, rel in enumerate(meta):
            m, dp = block_place(place, *rel)
            row = pl.multiple_of((m * n_dp + dp) * depth, depth)
            copy = pltpu.make_async_copy(
                piece.at[pl.ds(b * depth, depth), :], dst.at[pl.ds(row, depth), :], sems.at[len(copies)]
            )
            copy.start()
            copies.append(copy)
    return copies


def wait_all(copies):
    for copy in copies:
        copy.wait()


def store_blocks(place, acc, start, own_ref, other_ref):
    slots, n_z, depth, width = own_ref.shape
    n_dp = n_z * 4
    for core in range(2):

        @pl.when(place[2] == core)
        def _():
            for m in range(HALVES):
                for dp in range(n_dp):
                    z, x, c = dp // 4, (dp // 2) % 2, dp % 2
                    slot = (place[1] ^ x) + 2 * (place[3] ^ m)
                    back = lax.rem(z - place[0] + n_z, n_z)
                    rows = slice(dp * depth, (dp + 1) * depth)
                    ref = own_ref if c == core else other_ref
                    ref[slot, back, :, start : start + acc.shape[2]] = acc[m, rows, :].astype(BF)


def attn_scores_kernel(place, frames, metas, x_ref, *refs):
    n = len(metas)
    pieces, (normed_ref, q_ref, k_ref, p_ref, vec_ref, w_ref, s_ref, sems) = refs[:n], refs[n:]
    step = pl.program_id(0)

    @pl.when(step == 0)
    def _():
        wait_all(load_pieces(place, pieces, metas, w_ref, sems))
        vec_ref[...] = w_ref[:D, 2 * HW :].astype(F32).T[:8]

    x = x_ref[...].astype(F32)
    n, _ = norm_parts(x)
    normed = (n * vec_ref[0:1] + vec_ref[1:2]).astype(BF)
    normed_ref[...] = normed
    for m in range(HALVES):
        qk = nn(normed, w_ref[m * D : (m + 1) * D, : 2 * HW]).astype(BF)
        cols = slice(m * HW, (m + 1) * HW)
        q_ref[:, cols] = qk[:, :HW]
        k_ref[:, cols] = qk[:, HW:]
    for s in range(SEQS_STEP):
        for m in range(HALVES):
            at = seq_slice(s, m, HW)
            s_ref[at] = nt(k_ref[at], per_head(q_ref[at]))
    key = lax.broadcasted_iota(jnp.int32, (SEQ, 2 * HEAD), 0)
    query = lax.broadcasted_iota(jnp.int32, (SEQ, 2 * HEAD), 1) % HEAD
    for s in range(SEQS_STEP):
        allowed = (key <= query) & (key < frames[step * SEQS_STEP + s] * FTOK)
        for c in range(D // (2 * HEAD)):
            at = seq_slice(s, c, 2 * HEAD)
            scores = jnp.where(allowed, s_ref[at] * HEAD**-0.5, -1000000000.0)
            expd = jnp.exp(scores - jnp.max(scores, axis=0, keepdims=True))
            p_ref[at] = (expd * (1.0 / jnp.sum(expd, axis=0, keepdims=True))).astype(BF)


def attn_output_kernel(place, metas, x_ref, normed_ref, p_ref, *refs):
    n = len(metas)
    pieces, (v_ref, ho_ref, hidden_ref, w_ref, sems) = refs[:n], refs[n:]

    @pl.when(pl.program_id(0) == 0)
    def _():
        wait_all(load_pieces(place, pieces, metas, w_ref, sems))

    for m in range(HALVES):
        v_ref[:, m * HW : (m + 1) * HW] = nn(normed_ref[...], w_ref[m * D : (m + 1) * D, :HW]).astype(BF)
    for s in range(SEQS_STEP):
        for c in range(D // (2 * HEAD)):
            at = seq_slice(s, c, 2 * HEAD)
            ho_ref[at] = pair_blocks(tn(p_ref[at], v_ref[at])).astype(BF)
    attended = nt(ho_ref[:, :HW], w_ref[:D, HW:]) + nt(ho_ref[:, HW:], w_ref[D:, HW:])
    hidden_ref[...] = x_ref[...].astype(F32) + attended


GELU_A = (2.0 / jnp.pi) ** 0.5
GELU_B = 0.044715


def feed_forward_kernel(place, live, metas_u, metas_d, hidden_ref, cot_ref, vec_ref, *refs):
    n, n_all = len(metas_u), len(metas_u) + len(metas_d)
    (
        mixed_ref, gh_ref, own_ref, other_ref, gv_ref,
        wu_ref, wd_ref, accu_ref, accd_ref, gvacc_ref, act_ref, gup_ref, go_ref, sems_u, sems_d,
    ) = refs[n_all:]
    step = pl.program_id(0)
    last = pl.num_programs(0) - 1

    @pl.when(step == 0)
    def _():
        copies = load_pieces(place, refs[:n], metas_u, wu_ref, sems_u)
        copies += load_pieces(place, refs[n:n_all], metas_d, wd_ref, sems_d)
        accu_ref[...] = jnp.zeros_like(accu_ref)
        accd_ref[...] = jnp.zeros_like(accd_ref)
        gvacc_ref[...] = jnp.zeros_like(gvacc_ref)
        wait_all(copies)

    hidden = hidden_ref[...]
    n, rstd = norm_parts(hidden)
    normed = (n * vec_ref[2:3] + vec_ref[3:4]).astype(BF)
    row = lax.broadcasted_iota(jnp.int32, (ROWS, 1), 0) + step * ROWS
    go = jnp.where(row < live[0] * SEQ, cot_ref[...].astype(F32), 0.0)
    go_ref[...] = go.astype(BF)
    for m in range(HALVES):
        cols = slice(m * FW, (m + 1) * FW)
        up = nn(normed, wu_ref[m * D : (m + 1) * D])
        ga = nn(go_ref[...], wd_ref[m * D : (m + 1) * D])
        sq = up * up
        th = jnp.tanh(up * (GELU_A + (GELU_A * GELU_B) * sq))
        half = 0.5 + 0.5 * th
        act_ref[:, cols] = (up * half).astype(BF)
        slope = half + (0.5 * up) * (1.0 - th * th) * (GELU_A + (3.0 * GELU_A * GELU_B) * sq)
        gup_ref[:, cols] = (ga * slope).astype(BF)
    down = jnp.zeros((ROWS, D), F32)
    gy = jnp.zeros((ROWS, D), F32)
    for m in range(HALVES):
        cols = slice(m * FW, (m + 1) * FW)
        down += nt(act_ref[:, cols], wd_ref[m * D : (m + 1) * D])
        gy += nt(gup_ref[:, cols], wu_ref[m * D : (m + 1) * D])
        accu_ref[m] += tn(normed, gup_ref[:, cols])
        accd_ref[m] += tn(go_ref[...], act_ref[:, cols])
    mixed_ref[...] = (hidden + down).astype(BF)
    gh_ref[...] = go + norm_back(n, rstd, vec_ref[2:3], gy)
    gvacc_ref[0] += fold_rows(gy * n)
    gvacc_ref[1] += fold_rows(gy)

    @pl.when(step == last)
    def _():
        store_blocks(place, accu_ref, 0, own_ref, other_ref)
        store_blocks(place, accd_ref, FW, own_ref, other_ref)
        gv_ref[0:1] = jnp.sum(gvacc_ref[0], axis=0, keepdims=True)
        gv_ref[1:2] = jnp.sum(gvacc_ref[1], axis=0, keepdims=True)


def attn_backward_kernel(
    place, metas_qk, metas_vo, x_ref, gh_ref, q_ref, k_ref, v_ref, p_ref, ho_ref, vec_ref, gvtwo_ref, *refs
):
    n, n_all = len(metas_qk), len(metas_qk) + len(metas_vo)
    (
        gi_ref, own_ref, other_ref,
        wqk_ref, wvo_ref, acc_ref, gvacc_ref, gvec_ref, s_ref, ds_ref, dh_ref, dqkv_ref, sems_qk, sems_vo,
    ) = refs[n_all:]
    step = pl.program_id(0)
    last = pl.num_programs(0) - 1

    @pl.when(step == 0)
    def _():
        copies = load_pieces(place, refs[:n], metas_qk, wqk_ref, sems_qk)
        copies += load_pieces(place, refs[n:n_all], metas_vo, wvo_ref, sems_vo)
        acc_ref[...] = jnp.zeros_like(acc_ref)
        gvacc_ref[...] = jnp.zeros_like(gvacc_ref)
        wait_all(copies)

    x = x_ref[...].astype(F32)
    n, rstd = norm_parts(x)
    normed = (n * vec_ref[0:1] + vec_ref[1:2]).astype(BF)
    gh = gh_ref[...]
    gat = gh.astype(BF)
    for m in range(HALVES):
        cols = slice(m * HW, (m + 1) * HW)
        wo = slice(3 * HW, 4 * HW)
        dh_ref[:, cols] = nn(gat, wvo_ref[m * D : (m + 1) * D, HW:]).astype(BF)
        acc_ref[m, :, wo] += tn(gat, ho_ref[:, cols])
    for s in range(SEQS_STEP):
        for m in range(HALVES):
            at = seq_slice(s, m, HW)
            s_ref[at] = nt(v_ref[at], per_head(dh_ref[at]))
    for s in range(SEQS_STEP):
        for c in range(D // (2 * HEAD)):
            at = seq_slice(s, c, 2 * HEAD)
            probs = p_ref[at].astype(F32)
            gp = s_ref[at]
            delta = jnp.sum(probs * gp, axis=0, keepdims=True)
            ds_ref[at] = (probs * ((gp - delta) * HEAD**-0.5)).astype(BF)
    for s in range(SEQS_STEP):
        for m in range(HALVES):
            at = seq_slice(s, m, HW)
            rows = at[0]
            base = 3 * HW * m
            dqkv_ref[rows, base + 2 * HW : base + 3 * HW] = nn(p_ref[at], per_head(dh_ref[at])).astype(BF)
            dqkv_ref[rows, base + HW : base + 2 * HW] = nn(ds_ref[at], per_head(q_ref[at])).astype(BF)
    for s in range(SEQS_STEP):
        for c in range(D // (2 * HEAD)):
            at = seq_slice(s, c, 2 * HEAD)
            base = 3 * HW * (c // 2) + 2 * HEAD * (c % 2)
            dqkv_ref[at[0], base : base + 2 * HEAD] = pair_blocks(tn(ds_ref[at], k_ref[at])).astype(BF)
    gy = jnp.zeros((ROWS, D), F32)
    for m in range(HALVES):
        cols = slice(3 * HW * m, 3 * HW * (m + 1))
        gy += nt(dqkv_ref[:, cols.start : cols.start + 2 * HW], wqk_ref[m * D : (m + 1) * D, : 2 * HW])
        gy += nt(dqkv_ref[:, cols.start + 2 * HW : cols.stop], wvo_ref[m * D : (m + 1) * D, :HW])
        acc_ref[m, :, : 3 * HW] += tn(normed, dqkv_ref[:, cols])
    gi_ref[...] = gh + norm_back(n, rstd, vec_ref[0:1], gy)
    gvacc_ref[0] += fold_rows(gy * n)
    gvacc_ref[1] += fold_rows(gy)

    @pl.when(step == last)
    def _():
        store_blocks(place, acc_ref, 0, own_ref, other_ref)
        one = jnp.concatenate([jnp.sum(gvacc_ref[i], axis=0, keepdims=True) for i in range(2)], axis=0)
        rows = jnp.concatenate([one, gvtwo_ref[...], jnp.zeros((GC - 4, D), F32)], axis=0)
        for m in range(HALVES):
            gvec_ref[m] = rows.T
        store_blocks(place, gvec_ref, 4 * HW, own_ref, other_ref)


def row_block(width):
    return pl.BlockSpec((ROWS, width), lambda i, *_: (i, 0))


def held(shape):
    return pl.BlockSpec(shape, lambda i, *_: (0,) * len(shape), pipeline_mode=pl.Buffered(1))


def shape(dims, dtype):
    return jax.ShapeDtypeStruct(dims, dtype)


PARAMS = pltpu.CompilerParams(vmem_limit_bytes=56 * 1024 * 1024)
HBM = pl.BlockSpec(memory_space=pl.ANY)


def weight_scratch(pieces, metas):
    copies = sum(len(meta) for meta in metas)
    return pltpu.VMEM((HALVES * D, pieces[0].shape[1]), BF), pltpu.SemaphoreType.DMA((copies,))


def cost(flops, nbytes):
    return pl.CostEstimate(flops=flops, bytes_accessed=nbytes, transcendentals=0)


def attn_scores(place, frames, tokens, group):
    rows = tokens.shape[0]
    pieces, metas = group
    w, sems = weight_scratch(pieces, metas)
    return pl.pallas_call(
        lambda place, frames, *refs: attn_scores_kernel(place, frames, metas, *refs),
        grid_spec=pltpu.PrefetchScalarGridSpec(
            num_scalar_prefetch=2,
            grid=(rows // ROWS,),
            in_specs=[row_block(D)] + [HBM] * len(pieces),
            out_specs=[row_block(D)] * 4 + [held((8, D))],
            scratch_shapes=[w, pltpu.VMEM((ROWS, D), F32), sems],
        ),
        out_shape=[shape((rows, D), BF)] * 4 + [shape((8, D), F32)],
        compiler_params=PARAMS,
        cost_estimate=cost(rows * D * 2 * D * 2 * 2, rows * D * 10),
        name="attn_scores",
    )(place, frames, tokens, *pieces)


def attn_output(place, tokens, normed, p, group):
    rows = tokens.shape[0]
    pieces, metas = group
    w, sems = weight_scratch(pieces, metas)
    return pl.pallas_call(
        lambda place, *refs: attn_output_kernel(place, metas, *refs),
        grid_spec=pltpu.PrefetchScalarGridSpec(
            num_scalar_prefetch=1,
            grid=(rows // ROWS,),
            in_specs=[row_block(D)] * 3 + [HBM] * len(pieces),
            out_specs=[row_block(D)] * 3,
            scratch_shapes=[w, sems],
        ),
        out_shape=[shape((rows, D), BF)] * 2 + [shape((rows, D), F32)],
        compiler_params=PARAMS,
        cost_estimate=cost(rows * D * 2 * D * 2 * 2, rows * D * 14),
        name="attn_output",
    )(place, tokens, normed, p, *pieces)


def feed_forward(place, live, hidden, cotangent, vec, up, down, out_dims):
    rows = hidden.shape[0]
    wu, sems_u = weight_scratch(*up)
    wd, sems_d = weight_scratch(*down)
    grads = out_dims + (2 * FW,)
    return pl.pallas_call(
        lambda place, live, *refs: feed_forward_kernel(place, live, up[1], down[1], *refs),
        grid_spec=pltpu.PrefetchScalarGridSpec(
            num_scalar_prefetch=2,
            grid=(rows // ROWS,),
            in_specs=[row_block(D), row_block(D), held((8, D))] + [HBM] * (len(up[0]) + len(down[0])),
            out_specs=[row_block(D), row_block(D), held(grads), held(grads), held((2, D))],
            scratch_shapes=[
                wu,
                wd,
                pltpu.VMEM((HALVES, D, FW), F32),
                pltpu.VMEM((HALVES, D, FW), F32),
                pltpu.VMEM((2, 8, D), F32),
                pltpu.VMEM((ROWS, FF), BF),
                pltpu.VMEM((ROWS, FF), BF),
                pltpu.VMEM((ROWS, D), BF),
                sems_u,
                sems_d,
            ],
        ),
        out_shape=[
            shape((rows, D), BF),
            shape((rows, D), F32),
            shape(grads, BF),
            shape(grads, BF),
            shape((2, D), F32),
        ],
        compiler_params=PARAMS,
        cost_estimate=cost(rows * D * FF * 12, rows * D * 12),
        name="feed_forward",
    )(place, live, hidden, cotangent, vec, *up[0], *down[0])


def attn_backward(place, tokens, gh, q, k, v, p, ho, vec, gv_two, qk, vo, out_dims):
    rows = tokens.shape[0]
    wqk, sems_qk = weight_scratch(*qk)
    wvo, sems_vo = weight_scratch(*vo)
    grads = out_dims + (4 * HW + GC,)
    return pl.pallas_call(
        lambda place, *refs: attn_backward_kernel(place, qk[1], vo[1], *refs),
        grid_spec=pltpu.PrefetchScalarGridSpec(
            num_scalar_prefetch=1,
            grid=(rows // ROWS,),
            in_specs=[row_block(D)] * 7 + [held((8, D)), held((2, D))] + [HBM] * (len(qk[0]) + len(vo[0])),
            out_specs=[row_block(D), held(grads), held(grads)],
            scratch_shapes=[
                wqk,
                wvo,
                pltpu.VMEM((HALVES, D, 4 * HW), F32),
                pltpu.VMEM((2, 8, D), F32),
                pltpu.VMEM((HALVES, D, GC), F32),
                pltpu.VMEM((ROWS, D), F32),
                pltpu.VMEM((ROWS, D), BF),
                pltpu.VMEM((ROWS, D), BF),
                pltpu.VMEM((ROWS, 3 * D), BF),
                sems_qk,
                sems_vo,
            ],
        ),
        out_shape=[shape((rows, D), F32), shape(grads, BF), shape(grads, BF)],
        compiler_params=PARAMS,
        cost_estimate=cost(rows * D * 4 * D * 8, rows * D * 20),
        name="attn_backward",
    )(place, tokens, gh, q, k, v, p, ho, vec, gv_two, *qk[0], *vo[0])


def build(mesh):
    n_dp, n_mp = mesh.shape["dp"], mesh.shape["mp"]
    n_z = n_dp // 4
    depth = D // n_dp
    staged = n_mp == HALVES
    both = ("dp", "mp")
    PLANE = ((0, 0), (1, 0), (0, 1), (1, 1))

    def send(value, zr=0, xr=0, yr=0, cr=0):
        pairs = []
        for z in range(n_z):
            for x in range(2):
                for c in range(2):
                    for y in range(n_mp):
                        here = ((z * 2 + x) * 2 + c) * n_mp + y
                        there = ((((z + zr) % n_z) * 2 + (x ^ xr)) * 2 + (c ^ cr)) * n_mp + (y ^ yr)
                        pairs.append((here, there))
        return lax.ppermute(value, both, pairs)

    def along_z(value):
        return [value] + [send(value, zr=r) for r in range(1, n_z)]

    def across_plane(value):
        return [value] + [send(value, xr=x, yr=y) for x, y in PLANE[1:]]

    def both_cores(pieces):
        return pieces + [send(piece, cr=1) for piece in pieces]

    def stack(blocks):
        return jnp.concatenate(blocks, axis=0)

    Z_FIRST = tuple(tuple((c, x, y, z) for z in range(n_z)) for c in range(2) for x, y in PLANE)
    PLANE_FIRST = tuple(tuple((c, x, y, z) for x, y in PLANE) for c in range(2) for z in range(n_z))

    def after(value, *others):
        return lax.optimization_barrier((value,) + others)[0]

    def gather_staged(qk, vo, up, down):
        down_plane = across_plane(down)
        qk_z = along_z(qk)
        vo_z = along_z(after(vo, qk_z[-1]))
        qk_plane = across_plane(stack(qk_z))
        qk_all = both_cores(qk_plane)
        up_z = along_z(after(up, vo_z[-1]))
        vo_all = both_cores(across_plane(after(stack(vo_z), qk_plane[-1])))
        down_all = both_cores(along_z(after(stack(down_plane), up_z[-1])))
        up_all = both_cores(across_plane(after(stack(up_z), vo_all[3])))
        return (qk_all, Z_FIRST), (vo_all, Z_FIRST), (up_all, Z_FIRST), (down_all, PLANE_FIRST)

    def gather_plain(block, parts):
        out = lax.all_gather(block, ("mp", "dp"), axis=0, tiled=True)
        out = out.reshape(HALVES, n_mp // HALVES, D, parts, -1)
        return out.transpose(0, 2, 3, 1, 4).reshape(HALVES * D, -1)

    def plain_pieces(whole):
        z, x, c = lax.axis_index("dp") // 4, (lax.axis_index("dp") // 2) % 2, lax.axis_index("dp") % 2
        y = lax.axis_index("mp") % HALVES
        blocks = whole.reshape(HALVES, n_z, 2, 2, depth, -1)
        index = lambda n, at: (at - jnp.arange(n)) % n
        blocks = blocks[:, index(n_z, z)]
        blocks = blocks[y ^ jnp.arange(2)][:, :, x ^ jnp.arange(2)][:, :, :, c ^ jnp.arange(2)]
        blocks = blocks.transpose(3, 0, 2, 1, 4, 5).reshape(8, n_z * depth, -1)
        return [blocks[i] for i in range(8)], Z_FIRST

    def scatter_staged(own, other):
        mine = own.astype(F32) + send(other, cr=1).astype(F32)
        mine = mine.astype(BF)
        got = [send(mine[x + 2 * y], xr=x, yr=y).astype(F32) for x, y in PLANE[1:]]
        mine = ((mine[0].astype(F32) + got[0]) + (got[1] + got[2])).astype(BF)
        total = mine[0].astype(F32)
        for r in range(1, n_z):
            total += send(mine[r], zr=r).astype(F32)
        return total

    def scatter_plain(own, other, parts):
        z, x, c = lax.axis_index("dp") // 4, (lax.axis_index("dp") // 2) % 2, lax.axis_index("dp") % 2
        y = lax.axis_index("mp") % HALVES
        blocks = jnp.stack([own, other]).reshape(2, 2, 2, n_z, depth, -1)
        blocks = blocks[c ^ jnp.arange(2)][:, y ^ jnp.arange(2)][:, :, x ^ jnp.arange(2)]
        blocks = blocks[:, :, :, (jnp.arange(n_z) - z) % n_z]
        blocks = blocks.transpose(1, 3, 2, 0, 4, 5).reshape(HALVES, D, -1)
        wide = sum(parts)
        main, tail = blocks[:, :, :wide], blocks[:, :, wide:]
        main = main.reshape(HALVES, D, len(parts), n_mp // HALVES, -1).transpose(0, 3, 1, 2, 4)
        main = main.reshape(n_mp, D, -1)
        tail = jnp.broadcast_to(tail[:1], (n_mp, D, tail.shape[2]))
        flat = jnp.concatenate([main, tail], axis=2).reshape(n_mp * D, -1)
        return lax.psum_scatter(flat, ("mp", "dp"), scatter_dimension=0, tiled=True).astype(F32)

    def shards(
        tokens, cotangent, frame_count, live_count, w_query, w_key, w_value, w_out, w_up, w_down,
        gain_one, shift_one, gain_two, shift_two,
    ):
        dp, mp = lax.axis_index("dp"), lax.axis_index("mp")
        place = jnp.stack([dp // 4, (dp // 2) % 2, dp % 2, mp % HALVES, jnp.int32(n_z)]).astype(jnp.int32)
        seqs = tokens.shape[0] // SEQ
        frames = lax.dynamic_slice(frame_count, (mp * seqs,), (seqs,))
        live = live_count - mp * seqs
        vec = jnp.stack([gain_one, shift_one, gain_two, shift_two], axis=1)
        vec = jnp.pad(vec, ((0, 0), (0, GC - 4)))
        if staged:
            qk, vo, up, down = gather_staged(
                jnp.concatenate([w_query, w_key, vec], axis=1),
                jnp.concatenate([w_value, w_out.T], axis=1),
                w_up,
                w_down.T,
            )
        else:
            vec = lax.all_gather(vec, "dp", axis=0, tiled=True)
            whole = gather_plain(jnp.concatenate([w_query, w_key], axis=1), 2)
            qk = plain_pieces(jnp.concatenate([whole, jnp.concatenate([vec] * HALVES)], axis=1))
            vo = plain_pieces(gather_plain(jnp.concatenate([w_value, w_out.T], axis=1), 2))
            up = plain_pieces(gather_plain(w_up, 1))
            down = plain_pieces(gather_plain(w_down.T, 1))
        out_dims = (4, n_z, depth)
        normed, q, k, p, vec = attn_scores(place, frames, tokens, qk)
        v, ho, hidden = attn_output(place, tokens, normed, p, vo)
        mixed, gh, f_own, f_other, gv_two = feed_forward(
            place, live, hidden, cotangent, vec, up, down, out_dims
        )
        grad_input, a_own, a_other = attn_backward(
            place, tokens, gh, q, k, v, p, ho, vec, gv_two, qk, vo, out_dims
        )
        if staged:
            gf = scatter_staged(f_own, f_other)
            ga = scatter_staged(a_own, a_other)
        else:
            gf = scatter_plain(f_own, f_other, (FW, FW))
            ga = scatter_plain(a_own, a_other, (HW,) * 4)
        wide = w_query.shape[1]
        tall = w_up.shape[1]
        gains = ga[:, 4 * wide :]
        return (
            mixed,
            grad_input,
            ga[:, :wide],
            ga[:, wide : 2 * wide],
            ga[:, 2 * wide : 3 * wide],
            ga[:, 3 * wide : 4 * wide].T,
            gf[:, :tall],
            gf[:, tall:].T,
            gains[:, 0],
            gains[:, 1],
            gains[:, 2],
            gains[:, 3],
        )

    return shards


def solution(mesh):
    rows = P(("dp", "mp"), None)
    wide, tall, dp = P("dp", "mp"), P("mp", "dp"), P("dp")
    return jax.shard_map(
        build(mesh),
        mesh=mesh,
        in_specs=(rows, rows, dp, dp, wide, wide, wide, tall, wide, tall, dp, dp, dp, dp),
        out_specs=(rows, rows, wide, wide, wide, tall, wide, tall, dp, dp, dp, dp),
        check_vma=False,
    )
```

time: 528 us -> 327 us (0.62)
  waiting for transfers between devices: 323 us -> 79.5 us
  starting transfers between devices: 0.16 us -> 48.1 us
  Pallas kernels: 167 us -> 184 us
  between operations: 14.5 us -> 1.88 us
  local copies, waits for them, and re-layouts: 13.2 us -> 5.44 us
    reduce_scatter x2 -> x0, waiting for transfers between devices: 236 us -> none  [scatter(): return lax.psum_scatter(flat, ('mp', 'dp'), scatter_dimension=0, tiled=True)]
    all_gather x2 -> x0, waiting for transfers between devices: 86.2 us -> none  [gather(): out = lax.all_gather(block, ('mp', 'dp'), axis=0, tiled=True)]
    ppermute x0 -> x54, waiting for transfers between devices: none -> 79.5 us  [send(): return lax.ppermute(value, both, pairs)]
    ppermute x0 -> x54, starting transfers between devices: none -> 48.1 us  [send(): return lax.ppermute(value, both, pairs)]
    pallas_call x3 -> x4, Pallas kernels: 167 us -> 184 us  [the longest x1 90.3 us: feed_forward(): pl.pallas_call(lambda place, live, *refs: feed_forward_kernel(place, live...]
    slice x3 -> x0, local copies, waits for them, and re-layouts: 6 us -> none  [the longest x1 3.09 us: shards(): wa = merge_parts(got_a[:, :, :-GC], 4)]
  transfers between devices with their start and end apart: 4 -> 54, of which waited for: 4 -> 22; matrix products, arithmetic and copies ran while one was open for 2% -> 3% of each run, Pallas kernels for 6% -> 13%
where the time goes in v2:
time: 327 us; the launch traced here: 326 us
  Pallas kernels  184 us (56%)
  waiting for transfers between devices  79.5 us (24%)
  starting transfers between devices  48.1 us (15%)
  other arithmetic  7.71 us (2%)
  local copies, waits for them, and re-layouts  5.44 us (2%)
    pallas_call x1, Pallas kernels, feed_forward(): pl.pallas_call(lambda place, live, *refs: feed_forward_kernel(place, live...  90.3 us
    ppermute x54, waiting for transfers between devices, send(): return lax.ppermute(value, both, pairs)  79.5 us
    pallas_call x1, Pallas kernels, attn_backward(): pl.pallas_call(lambda place, *refs: attn_backward_kernel(place, qk[1], vo...  51.2 us
    ppermute x54, starting transfers between devices, send(): return lax.ppermute(value, both, pairs)  48.1 us
    pallas_call x1, Pallas kernels, attn_scores(): pl.pallas_call(lambda place, frames, *refs: attn_scores_kernel(place, fra...  22.5 us
    pallas_call x1, Pallas kernels, attn_output(): pl.pallas_call(lambda place, *refs: attn_output_kernel(place, metas, *ref...  19.6 us
  transfers between devices with their start and end apart: 54, of which 22 were waited for; matrix products, arithmetic and copies ran while one was open for 3% of the time, Pallas kernels for 13%

profile of v2, /device:TPU:0, one launch (start us, length us, event | category | flops | bytes accessed | tf_op | source)
XLA Modules:
  0.0 326.2 jit_solution(12984572725588736299)
XLA Ops:
  0.6 0.7 pad_maximum_fusion.6
  1.5 0.7 pad_maximum_fusion.4
  2.2 5.0 %collective-permute-start.2 = (bf16[32,640]{1,0:T(8,128)(2,1)S(1)}, bf16[32,640]{1,0:T(8,128)(2,1)S(1)}, u32[]{:S(2)}, u32[]{:S(2)}) collective-permute-start(bf16[32,640]{1,0:T(8,128)(2,1)S(1)} %pad_maximum_fusion.4), channel_id=1, source_target_pairs={{0,24},{1,25},{2,26},{3,27},{4,28},{5,29},{6,30},{7,31},{8,0},{9,1... | collective-permute-start | bytes 122888 | tf_op jit(solution)/shard_map/ppermute | solution.py:455
  7.3 1.0 collective-permute-start
  8.3 2.4 collective-permute-start.32
  12.2 0.9 collective-permute-done
  13.1 0.8 pad_maximum_fusion.2.refs_1_.refs_9_
  13.8 2.5 collective-permute-start.5
  16.3 0.7 pad_maximum_fusion.5
  17.1 1.5 collective-permute-start.12
  18.6 1.1 collective-permute-start.11
  19.7 1.3 collective-permute-done.12
  21.0 1.2 collective-permute-start.10
  22.2 0.6 collective-permute-start.4
  22.8 0.9 collective-permute-done.11
  24.3 2.6 collective-permute-done.10
  26.8 1.5 collective-permute-start.22
  28.4 3.2 collective-permute-done.22
  31.6 2.7 collective-permute-done.21
  34.4 6.3 %collective-permute-done.20 = bf16[32,1024]{1,0:T(8,128)(2,1)S(1)} collective-permute-done((bf16[32,1024]{1,0:T(8,128)(2,1)}, bf16[32,1024]{1,0:T(8,128)(2,1)S(1)}, u32[]{:S(2)}, u32[]{:S(2)}) %collective-permute-start.20) | collective-permute-done | bytes 65568 | tf_op jit(solution)/shard_map/ppermute | solution.py:455
  41.0 1.5 collective-permute-start.14
  42.5 1.6 collective-permute-start.13
  44.7 0.9 pad_maximum_fusion.1.refs_11_
  45.5 1.1 collective-permute-done.15.refs_6_.refs_20_
  46.6 0.8 collective-permute-done.14.refs_5_.refs_19_
  47.4 0.8 collective-permute-start.35
  48.3 1.5 collective-permute-start.33
  50.3 6.1 %collective-permute-done.35.refs_14_ = bf16[128,1024]{1,0:T(8,128)(2,1)S(1)} collective-permute-done((bf16[128,1024]{1,0:T(8,128)(2,1)S(1)}, bf16[128,1024]{1,0:T(8,128)(2,1)S(1)}, u32[]{:S(2)}, u32[]{:S(2)}) %collective-permute-start.35) | collective-permute-done | bytes 262176 | tf_op jit(solution)/shard_map/ppermute | solution.py:455
  57.1 1.3 dynamic_slice.3.frames
  58.3 0.6 stack.34.place
  58.9 0.9 pad_maximum_fusion.refs_3_
  59.8 10.0 %collective-permute-done.34.refs_13_ = bf16[128,1024]{1,0:T(8,128)(2,1)S(1)} collective-permute-done((bf16[128,1024]{1,0:T(8,128)(2,1)S(1)}, bf16[128,1024]{1,0:T(8,128)(2,1)S(1)}, u32[]{:S(2)}, u32[]{:S(2)}) %collective-permute-start.34) | collective-permute-done | bytes 262176 | tf_op jit(solution)/shard_map/ppermute | solution.py:455
  69.9 0.7 collective-permute-start.25
  70.6 1.2 collective-permute-start.24
  71.8 1.6 collective-permute-start.23
  73.5 22.5 %attn_scores.1 = (bf16[4608,512]{1,0:T(8,128)(2,1)}, bf16[4608,512]{1,0:T(8,128)(2,1)}, bf16[4608,512]{1,0:T(8,128)(2,1)}, bf16[4608,512]{1,0:T(8,128)(2,1)}, f32[8,512]{1,0:T(8,128)}) custom-call(s32[5]{0:T(128)} %stack.34.place, s32[96]{0:T(128)} %dynamic_slice.3.frames, bf16[4608,512]{1,0:T(8,128)(2,1)} %refs_0_.5, bf16[128,640]{1,0:T(8,128)(2,1)} %copy-done.3, ...), custom_call_target="tpu_custom_call" | custom-call | flops 9663676416 | bytes 23592960 | tf_op jit(solution)/shard_map/attn_scores/pallas_call | solution.py:331
  96.2 0.6 collective-permute-start.38
  97.8 19.6 %attn_output.1 = (bf16[4608,512]{1,0:T(8,128)(2,1)}, bf16[4608,512]{1,0:T(8,128)(2,1)}, f32[4608,512]{1,0:T(8,128)}) custom-call(s32[5]{0:T(128)} %stack.34.place, bf16[4608,512]{1,0:T(8,128)(2,1)} %refs_0_.5, bf16[4608,512]{1,0:T(8,128)(2,1)} %get-tuple-element.33.refs_1_, bf16[4608,512]{1,0:T(8,128)(2,1)} %get-tuple-element.34.refs_2_.refs_5_, ...), custom_call_target="tpu_custom_call" | custom-call | flops 9663676416 | bytes 33030144 | tf_op jit(solution)/shard_map/attn_output/pallas_call | solution.py:351
  117.6 0.6 copy-done.15
  118.6 90.3 %feed_forward.1 = (bf16[4608,512]{1,0:T(8,128)(2,1)}, f32[4608,512]{1,0:T(8,128)}, bf16[4,4,32,2048]{3,2,1,0:T(8,128)(2,1)}, bf16[4,4,32,2048]{3,2,1,0:T(8,128)(2,1)}, f32[2,512]{1,0:T(2,128)}) custom-call(s32[5]{0:T(128)} %stack.34.place, s32[1]{0:T(128)S(6)} %sub.16.live, f32[4608,512]{1,0:T(8,128)} %get-tuple-element.37.refs_0_, ...), custom_call_target="tpu_custom_call" | custom-call | flops 57982058496 | bytes 28311552 | tf_op jit(solution)/shard_map/feed_forward/pallas_call | solution.py:372
  209.0 51.2 %attn_backward.1 = (f32[4608,512]{1,0:T(8,128)}, bf16[4,4,32,1152]{3,2,1,0:T(8,128)(2,1)}, bf16[4,4,32,1152]{3,2,1,0:T(8,128)(2,1)}) custom-call(s32[5]{0:T(128)} %stack.34.place, bf16[4608,512]{1,0:T(8,128)(2,1)} %refs_0_.5, f32[4608,512]{1,0:T(8,128)} %get-tuple-element.43.refs_1_, bf16[4608,512]{1,0:T(8,128)(2,1)} %get-tuple-element.44.refs_2_, ...), custom_call_target="tpu_custom_call" | custom-call | flops 38654705664 | bytes 47185920 | tf_op jit(solution)/shard_map/attn_backward/pallas_call | solution.py:410
  260.8 3.3 %collective-permute-done.40 = bf16[4,4,32,1152]{3,2,1,0:T(8,128)(2,1)S(1)} collective-permute-done((bf16[4,4,32,1152]{3,2,1,0:T(8,128)(2,1)}, bf16[4,4,32,1152]{3,2,1,0:T(8,128)(2,1)S(1)}, u32[]{:S(2)}, u32[]{:S(2)}) %collective-permute-start.40) | collective-permute-done | bytes 1179680 | tf_op jit(solution)/shard_map/ppermute | solution.py:455
  264.1 1.6 add_convert_fusion.1
  266.3 1.4 collective-permute-start.43
  267.7 1.7 collective-permute-start.42
  269.3 6.4 %collective-permute-done.41 = bf16[4,32,1152]{2,1,0:T(8,128)(2,1)S(1)} collective-permute-done((bf16[4,32,1152]{2,1,0:T(8,128)(2,1)S(1)}, bf16[4,32,1152]{2,1,0:T(8,128)(2,1)S(1)}, u32[]{:S(2)}, u32[]{:S(2)}) %collective-permute-start.41) | collective-permute-done | bytes 294944 | tf_op jit(solution)/shard_map/ppermute | solution.py:455
  275.7 5.4 %collective-permute-done.43 = bf16[4,32,1152]{2,1,0:T(8,128)(2,1)S(1)} collective-permute-done((bf16[4,32,1152]{2,1,0:T(8,128)(2,1)S(1)}, bf16[4,32,1152]{2,1,0:T(8,128)(2,1)S(1)}, u32[]{:S(2)}, u32[]{:S(2)}) %collective-permute-start.43) | collective-permute-done | bytes 294944 | tf_op jit(solution)/shard_map/ppermute | solution.py:455
  281.1 1.4 collective-permute-done.42
  282.7 2.0 collective-permute-start.44
  284.7 1.9 collective-permute-start.46
  286.5 2.0 collective-permute-start.45
  288.6 0.9 add_convert_fusion
  289.6 1.4 collective-permute-start.48
  291.0 1.5 collective-permute-start.50
  292.5 0.7 collective-permute-start.49
  293.2 11.3 %collective-permute-done.48 = bf16[4,32,2048]{2,1,0:T(8,128)(2,1)S(1)} collective-permute-done((bf16[4,32,2048]{2,1,0:T(8,128)(2,1)S(1)}, bf16[4,32,2048]{2,1,0:T(8,128)(2,1)S(1)}, u32[]{:S(2)}, u32[]{:S(2)}) %collective-permute-start.48) | collective-permute-done | bytes 524320 | tf_op jit(solution)/shard_map/ppermute | solution.py:455
  304.5 8.1 %collective-permute-done.50 = bf16[4,32,2048]{2,1,0:T(8,128)(2,1)S(1)} collective-permute-done((bf16[4,32,2048]{2,1,0:T(8,128)(2,1)S(1)}, bf16[4,32,2048]{2,1,0:T(8,128)(2,1)S(1)}, u32[]{:S(2)}, u32[]{:S(2)}) %collective-permute-start.50) | collective-permute-done | bytes 524320 | tf_op jit(solution)/shard_map/ppermute | solution.py:455
  312.6 1.4 collective-permute-done.49
  314.8 3.5 %collective-permute-start.53 = (bf16[32,2048]{1,0:T(8,128)(2,1)S(1)}, bf16[32,2048]{1,0:T(8,128)(2,1)S(1)}, u32[]{:S(2)}, u32[]{:S(2)}) collective-permute-start(bf16[32,2048]{1,0:T(8,128)(2,1)S(1)} %get-tuple-element.65), channel_id=1, source_target_pairs={{0,24},{1,25},{2,26},{3,27},{4,28},{5,29},{6,30},{7,31},{8,0},{9,1... | collective-permute-start | bytes 393224 | tf_op jit(solution)/shard_map/ppermute | solution.py:455
  318.3 0.7 slice_bitcast_fusion.17
  318.9 0.7 slice_reduce_fusion
  319.6 1.7 collective-permute-done.51
  321.5 3.9 %collective-permute-done.52 = bf16[32,2048]{1,0:T(8,128)(2,1)S(1)} collective-permute-done((bf16[32,2048]{1,0:T(8,128)(2,1)S(1)}, bf16[32,2048]{1,0:T(8,128)(2,1)S(1)}, u32[]{:S(2)}, u32[]{:S(2)}) %collective-permute-start.52) | collective-permute-done | bytes 131104 | tf_op jit(solution)/shard_map/ppermute | solution.py:455
  325.5 0.7 slice_bitcast_fusion.8
  (134 shorter events, 7.7 us)
Async XLA Ops:
  2.2 9.0 %collective-permute-start.2 = (bf16[32,640]{1,0:T(8,128)(2,1)S(1)}, bf16[32,640]{1,0:T(8,128)(2,1)S(1)}, u32[]{:S(2)}, u32[]{:S(2)}) collective-permute-start(bf16[32,640]{1,0:T(8,128)(2,1)S(1)} %pad_maximum_fusion.4), channel_id=1, source_target_pairs={{0,24},{1,25},{2,26},{3,27},{4,28},{5,29},{6,30},{7,31},{8,0},{9,1... | collective-permute-start | bytes 122888 | tf_op jit(solution)/shard_map/ppermute | solution.py:455
  7.3 4.9 %collective-permute-start.1 = (bf16[32,640]{1,0:T(8,128)(2,1)S(1)}, bf16[32,640]{1,0:T(8,128)(2,1)S(1)}, u32[]{:S(2)}, u32[]{:S(2)}) collective-permute-start(bf16[32,640]{1,0:T(8,128)(2,1)S(1)} %pad_maximum_fusion.4), channel_id=1, source_target_pairs={{0,16},{1,17},{2,18},{3,19},{4,20},{5,21},{6,22},{7,23},{8,24},{9,... | collective-permute-start | bytes 122888 | tf_op jit(solution)/shard_map/ppermute | solution.py:455
  7.3 5.8 %collective-permute-start = (bf16[32,640]{1,0:T(8,128)(2,1)S(1)}, bf16[32,640]{1,0:T(8,128)(2,1)S(1)}, u32[]{:S(2)}, u32[]{:S(2)}) collective-permute-start(bf16[32,640]{1,0:T(8,128)(2,1)S(1)} %pad_maximum_fusion.4), channel_id=1, source_target_pairs={{0,8},{1,9},{2,10},{3,11},{4,12},{5,13},{6,14},{7,15},{8,16},{9,17... | collective-permute-start | bytes 122888 | tf_op jit(solution)/shard_map/ppermute | solution.py:455
  8.3 10.3 %collective-permute-start.32 = (bf16[32,1024]{1,0:T(8,128)(2,1)}, bf16[32,1024]{1,0:T(8,128)(2,1)S(1)}, u32[]{:S(2)}, u32[]{:S(2)}) collective-permute-start(bf16[32,1024]{1,0:T(8,128)(2,1)} %bitcast.59), channel_id=1, source_target_pairs={{0,5},{1,4},{2,7},{3,6},{4,1},{5,0},{6,3},{7,2},{8,13},{9,12},{10,... | collective-permute-start | bytes 196616 | tf_op jit(solution)/shard_map/ppermute | solution.py:455
  10.7 11.5 %collective-permute-start.31 = (bf16[32,1024]{1,0:T(8,128)(2,1)}, bf16[32,1024]{1,0:T(8,128)(2,1)S(1)}, u32[]{:S(2)}, u32[]{:S(2)}) collective-permute-start(bf16[32,1024]{1,0:T(8,128)(2,1)} %bitcast.60), channel_id=1, source_target_pairs={{0,1},{1,0},{2,3},{3,2},{4,5},{5,4},{6,7},{7,6},{8,9},{9,8},{10,11... | collective-permute-start | bytes 196616 | tf_op jit(solution)/shard_map/ppermute | solution.py:455
  11.2 11.0 %collective-permute-start.30 = (bf16[32,1024]{1,0:T(8,128)(2,1)}, bf16[32,1024]{1,0:T(8,128)(2,1)S(1)}, u32[]{:S(2)}, u32[]{:S(2)}) collective-permute-start(bf16[32,1024]{1,0:T(8,128)(2,1)} %bitcast.61), channel_id=1, source_target_pairs={{0,4},{1,5},{2,6},{3,7},{4,0},{5,1},{6,2},{7,3},{8,12},{9,13},{10,... | collective-permute-start | bytes 196616 | tf_op jit(solution)/shard_map/ppermute | solution.py:455
  13.8 59.6 %copy-start.3 = (bf16[128,640]{1,0:T(8,128)(2,1)}, bf16[128,640]{1,0:T(8,128)(2,1)S(1)}, u32[]{:S(2)}) copy-start(bf16[128,640]{1,0:T(8,128)(2,1)S(1)} %pad_maximum_fusion.2.refs_1_.refs_9_) | copy-start | bytes 491524
  13.8 14.5 %collective-permute-start.5 = (bf16[128,640]{1,0:T(8,128)(2,1)S(1)}, bf16[128,640]{1,0:T(8,128)(2,1)S(1)}, u32[]{:S(2)}, u32[]{:S(2)}) collective-permute-start(bf16[128,640]{1,0:T(8,128)(2,1)S(1)} %pad_maximum_fusion.2.refs_1_.refs_9_), channel_id=1, source_target_pairs={{0,5},{1,4},{2,7},{3,6},{4,1},{5,0},{6,3},{7,2},{8,13},{9,12},{10,... | collective-permute-start | bytes 491528 | tf_op jit(solution)/shard_map/ppermute | solution.py:455
  17.1 3.9 %collective-permute-start.12 = (bf16[32,512]{1,0:T(8,128)(2,1)S(1)}, bf16[32,512]{1,0:T(8,128)(2,1)S(1)}, u32[]{:S(2)}, u32[]{:S(2)}) collective-permute-start(bf16[32,512]{1,0:T(8,128)(2,1)S(1)} %pad_maximum_fusion.5), channel_id=1, source_target_pairs={{0,24},{1,25},{2,26},{3,27},{4,28},{5,29},{6,30},{7,31},{8,0},{9,1... | collective-permute-start | bytes 98312 | tf_op jit(solution)/shard_map/ppermute | solution.py:455
  18.6 5.1 %collective-permute-start.11 = (bf16[32,512]{1,0:T(8,128)(2,1)S(1)}, bf16[32,512]{1,0:T(8,128)(2,1)S(1)}, u32[]{:S(2)}, u32[]{:S(2)}) collective-permute-start(bf16[32,512]{1,0:T(8,128)(2,1)S(1)} %pad_maximum_fusion.5), channel_id=1, source_target_pairs={{0,16},{1,17},{2,18},{3,19},{4,20},{5,21},{6,22},{7,23},{8,24},{9,... | collective-permute-start | bytes 98312 | tf_op jit(solution)/shard_map/ppermute | solution.py:455
  21.0 5.8 %collective-permute-start.10 = (bf16[32,512]{1,0:T(8,128)(2,1)S(1)}, bf16[32,512]{1,0:T(8,128)(2,1)S(1)}, u32[]{:S(2)}, u32[]{:S(2)}) collective-permute-start(bf16[32,512]{1,0:T(8,128)(2,1)S(1)} %pad_maximum_fusion.5), channel_id=1, source_target_pairs={{0,8},{1,9},{2,10},{3,11},{4,12},{5,13},{6,14},{7,15},{8,16},{9,17... | collective-permute-start | bytes 98312 | tf_op jit(solution)/shard_map/ppermute | solution.py:455
  22.2 18.8 %collective-permute-start.6 = (bf16[128,640]{1,0:T(8,128)(2,1)S(1)}, bf16[128,640]{1,0:T(8,128)(2,1)S(1)}, u32[]{:S(2)}, u32[]{:S(2)}) collective-permute-start(bf16[128,640]{1,0:T(8,128)(2,1)S(1)} %pad_maximum_fusion.2.refs_1_.refs_9_), channel_id=1, source_target_pairs={{0,2},{1,3},{2,0},{3,1},{4,6},{5,7},{6,4},{7,5},{8,10},{9,11},{10,... | collective-permute-start | bytes 491528 | tf_op jit(solution)/shard_map/ppermute | solution.py:455
  22.2 20.3 %collective-permute-start.4 = (bf16[128,640]{1,0:T(8,128)(2,1)S(1)}, bf16[128,640]{1,0:T(8,128)(2,1)S(1)}, u32[]{:S(2)}, u32[]{:S(2)}) collective-permute-start(bf16[128,640]{1,0:T(8,128)(2,1)S(1)} %pad_maximum_fusion.2.refs_1_.refs_9_), channel_id=1, source_target_pairs={{0,1},{1,0},{2,3},{3,2},{4,5},{5,4},{6,7},{7,6},{8,9},{9,8},{10,11... | collective-permute-start | bytes 491528 | tf_op jit(solution)/shard_map/ppermute | solution.py:455
  23.7 20.4 %collective-permute-start.3 = (bf16[128,640]{1,0:T(8,128)(2,1)S(1)}, bf16[128,640]{1,0:T(8,128)(2,1)S(1)}, u32[]{:S(2)}, u32[]{:S(2)}) collective-permute-start(bf16[128,640]{1,0:T(8,128)(2,1)S(1)} %pad_maximum_fusion.2.refs_1_.refs_9_), channel_id=1, source_target_pairs={{0,4},{1,5},{2,6},{3,7},{4,0},{5,1},{6,2},{7,3},{8,12},{9,13},{10,... | collective-permute-start | bytes 491528 | tf_op jit(solution)/shard_map/ppermute | solution.py:455
  26.8 4.8 %collective-permute-start.22 = (bf16[32,1024]{1,0:T(8,128)(2,1)}, bf16[32,1024]{1,0:T(8,128)(2,1)S(1)}, u32[]{:S(2)}, u32[]{:S(2)}) collective-permute-start(bf16[32,1024]{1,0:T(8,128)(2,1)} %param.22), channel_id=1, source_target_pairs={{0,24},{1,25},{2,26},{3,27},{4,28},{5,29},{6,30},{7,31},{8,0},{9,1... | collective-permute-start | bytes 196616 | tf_op jit(solution)/shard_map/ppermute | solution.py:455
  28.4 45.1 %copy-start.20 = (bf16[128,640]{1,0:T(8,128)(2,1)}, bf16[128,640]{1,0:T(8,128)(2,1)S(1)}, u32[]{:S(2)}) copy-start(bf16[128,640]{1,0:T(8,128)(2,1)S(1)} %collective-permute-done.5.refs_4_.refs_12_) | copy-start | bytes 491524
  28.4 6.0 %collective-permute-start.21 = (bf16[32,1024]{1,0:T(8,128)(2,1)}, bf16[32,1024]{1,0:T(8,128)(2,1)S(1)}, u32[]{:S(2)}, u32[]{:S(2)}) collective-permute-start(bf16[32,1024]{1,0:T(8,128)(2,1)} %param.22), channel_id=1, source_target_pairs={{0,16},{1,17},{2,18},{3,19},{4,20},{5,21},{6,22},{7,23},{8,24},{9,... | collective-permute-start | bytes 196616 | tf_op jit(solution)/shard_map/ppermute | solution.py:455
  28.4 67.7 %copy-start.4 = (bf16[128,512]{1,0:T(8,128)(2,1)}, bf16[128,512]{1,0:T(8,128)(2,1)S(1)}, u32[]{:S(2)}) copy-start(bf16[128,512]{1,0:T(8,128)(2,1)S(1)} %pad_maximum_fusion.3.refs_3_.refs_17_) | copy-start | bytes 393220
  31.6 12.5 %collective-permute-start.16 = (bf16[128,512]{1,0:T(8,128)(2,1)S(1)}, bf16[128,512]{1,0:T(8,128)(2,1)S(1)}, u32[]{:S(2)}, u32[]{:S(2)}) collective-permute-start(bf16[128,512]{1,0:T(8,128)(2,1)S(1)} %pad_maximum_fusion.3.refs_3_.refs_17_), channel_id=1, source_target_pairs={{0,2},{1,3},{2,0},{3,1},{4,6},{5,7},{6,4},{7,5},{8,10},{9,11},{10,... | collective-permute-start | bytes 393224 | tf_op jit(solution)/shard_map/ppermute | solution.py:455
  34.4 6.3 %collective-permute-start.20 = (bf16[32,1024]{1,0:T(8,128)(2,1)}, bf16[32,1024]{1,0:T(8,128)(2,1)S(1)}, u32[]{:S(2)}, u32[]{:S(2)}) collective-permute-start(bf16[32,1024]{1,0:T(8,128)(2,1)} %param.22), channel_id=1, source_target_pairs={{0,8},{1,9},{2,10},{3,11},{4,12},{5,13},{6,14},{7,15},{8,16},{9,17... | collective-permute-start | bytes 196616 | tf_op jit(solution)/shard_map/ppermute | solution.py:455
  40.6 6.0 %collective-permute-start.15 = (bf16[128,512]{1,0:T(8,128)(2,1)S(1)}, bf16[128,512]{1,0:T(8,128)(2,1)S(1)}, u32[]{:S(2)}, u32[]{:S(2)}) collective-permute-start(bf16[128,512]{1,0:T(8,128)(2,1)S(1)} %pad_maximum_fusion.3.refs_3_.refs_17_), channel_id=1, source_target_pairs={{0,5},{1,4},{2,7},{3,6},{4,1},{5,0},{6,3},{7,2},{8,13},{9,12},{10,... | collective-permute-start | bytes 393224 | tf_op jit(solution)/shard_map/ppermute | solution.py:455
  41.0 6.4 %collective-permute-start.14 = (bf16[128,512]{1,0:T(8,128)(2,1)S(1)}, bf16[128,512]{1,0:T(8,128)(2,1)S(1)}, u32[]{:S(2)}, u32[]{:S(2)}) collective-permute-start(bf16[128,512]{1,0:T(8,128)(2,1)S(1)} %pad_maximum_fusion.3.refs_3_.refs_17_), channel_id=1, source_target_pairs={{0,1},{1,0},{2,3},{3,2},{4,5},{5,4},{6,7},{7,6},{8,9},{9,8},{10,11... | collective-permute-start | bytes 393224 | tf_op jit(solution)/shard_map/ppermute | solution.py:455
  42.5 5.6 %collective-permute-start.13 = (bf16[128,512]{1,0:T(8,128)(2,1)S(1)}, bf16[128,512]{1,0:T(8,128)(2,1)S(1)}, u32[]{:S(2)}, u32[]{:S(2)}) collective-permute-start(bf16[128,512]{1,0:T(8,128)(2,1)S(1)} %pad_maximum_fusion.3.refs_3_.refs_17_), channel_id=1, source_target_pairs={{0,4},{1,5},{2,6},{3,7},{4,0},{5,1},{6,2},{7,3},{8,12},{9,13},{10,... | collective-permute-start | bytes 393224 | tf_op jit(solution)/shard_map/ppermute | solution.py:455
  44.1 4.0 %collective-permute-start.9 = (bf16[128,640]{1,0:T(8,128)(2,1)S(1)}, bf16[128,640]{1,0:T(8,128)(2,1)S(1)}, u32[]{:S(2)}, u32[]{:S(2)}) collective-permute-start(bf16[128,640]{1,0:T(8,128)(2,1)S(1)} %collective-permute-done.5.refs_4_.refs_12_), channel_id=1, source_target_pairs={{0,2},{1,3},{2,0},{3,1},{4,6},{5,7},{6,4},{7,5},{8,10},{9,11},{10,... | collective-permute-start | bytes 491528 | tf_op jit(solution)/shard_map/ppermute | solution.py:455
  44.2 51.9 %copy-start.27 = (bf16[128,512]{1,0:T(8,128)(2,1)}, bf16[128,512]{1,0:T(8,128)(2,1)S(1)}, u32[]{:S(2)}) copy-start(bf16[128,512]{1,0:T(8,128)(2,1)S(1)} %collective-permute-done.16.refs_7_.refs_21_) | copy-start | bytes 393220
  44.2 4.1 %collective-permute-start.8 = (bf16[128,640]{1,0:T(8,128)(2,1)S(1)}, bf16[128,640]{1,0:T(8,128)(2,1)S(1)}, u32[]{:S(2)}, u32[]{:S(2)}) collective-permute-start(bf16[128,640]{1,0:T(8,128)(2,1)S(1)} %collective-permute-done.4.refs_3_.refs_11_), channel_id=1, source_target_pairs={{0,2},{1,3},{2,0},{3,1},{4,6},{5,7},{6,4},{7,5},{8,10},{9,11},{10,... | collective-permute-start | bytes 491528 | tf_op jit(solution)/shard_map/ppermute | solution.py:455
  45.5 50.5 %copy-start.1 = (bf16[128,1024]{1,0:T(8,128)(2,1)}, bf16[128,1024]{1,0:T(8,128)(2,1)S(1)}, u32[]{:S(2)}) copy-start(bf16[128,1024]{1,0:T(8,128)(2,1)S(1)} %pad_maximum_fusion.1.refs_11_) | copy-start | bytes 786436
  46.6 49.5 %copy-start.28 = (bf16[128,512]{1,0:T(8,128)(2,1)}, bf16[128,512]{1,0:T(8,128)(2,1)S(1)}, u32[]{:S(2)}) copy-start(bf16[128,512]{1,0:T(8,128)(2,1)S(1)} %collective-permute-done.15.refs_6_.refs_20_) | copy-start | bytes 393220
  46.6 3.3 %collective-permute-start.36 = (bf16[128,1024]{1,0:T(8,128)(2,1)S(1)}, bf16[128,1024]{1,0:T(8,128)(2,1)S(1)}, u32[]{:S(2)}, u32[]{:S(2)}) collective-permute-start(bf16[128,1024]{1,0:T(8,128)(2,1)S(1)} %pad_maximum_fusion.1.refs_11_), channel_id=1, source_target_pairs={{0,2},{1,3},{2,0},{3,1},{4,6},{5,7},{6,4},{7,5},{8,10},{9,11},{10,... | collective-permute-start | bytes 786440 | tf_op jit(solution)/shard_map/ppermute | solution.py:455
  47.4 48.7 %copy-start.29 = (bf16[128,512]{1,0:T(8,128)(2,1)}, bf16[128,512]{1,0:T(8,128)(2,1)S(1)}, u32[]{:S(2)}) copy-start(bf16[128,512]{1,0:T(8,128)(2,1)S(1)} %collective-permute-done.14.refs_5_.refs_19_) | copy-start | bytes 393220
  47.4 9.0 %collective-permute-start.35 = (bf16[128,1024]{1,0:T(8,128)(2,1)S(1)}, bf16[128,1024]{1,0:T(8,128)(2,1)S(1)}, u32[]{:S(2)}, u32[]{:S(2)}) collective-permute-start(bf16[128,1024]{1,0:T(8,128)(2,1)S(1)} %pad_maximum_fusion.1.refs_11_), channel_id=1, source_target_pairs={{0,24},{1,25},{2,26},{3,27},{4,28},{5,29},{6,30},{7,31},{8,0},{9,1... | collective-permute-start | bytes 786440 | tf_op jit(solution)/shard_map/ppermute | solution.py:455
  48.2 47.9 %copy-start.30 = (bf16[128,512]{1,0:T(8,128)(2,1)}, bf16[128,512]{1,0:T(8,128)(2,1)S(1)}, u32[]{:S(2)}) copy-start(bf16[128,512]{1,0:T(8,128)(2,1)S(1)} %collective-permute-done.13.refs_4_.refs_18_) | copy-start | bytes 393220
  48.2 1.6 collective-permute-start.7
  48.2 21.6 %collective-permute-start.34 = (bf16[128,1024]{1,0:T(8,128)(2,1)S(1)}, bf16[128,1024]{1,0:T(8,128)(2,1)S(1)}, u32[]{:S(2)}, u32[]{:S(2)}) collective-permute-start(bf16[128,1024]{1,0:T(8,128)(2,1)S(1)} %pad_maximum_fusion.1.refs_11_), channel_id=1, source_target_pairs={{0,16},{1,17},{2,18},{3,19},{4,20},{5,21},{6,22},{7,23},{8,24},{9,... | collective-permute-start | bytes 786440 | tf_op jit(solution)/shard_map/ppermute | solution.py:455
  48.3 21.5 %collective-permute-start.33 = (bf16[128,1024]{1,0:T(8,128)(2,1)S(1)}, bf16[128,1024]{1,0:T(8,128)(2,1)S(1)}, u32[]{:S(2)}, u32[]{:S(2)}) collective-permute-start(bf16[128,1024]{1,0:T(8,128)(2,1)S(1)} %pad_maximum_fusion.1.refs_11_), channel_id=1, source_target_pairs={{0,8},{1,9},{2,10},{3,11},{4,12},{5,13},{6,14},{7,15},{8,16},{9,17... | collective-permute-start | bytes 786440 | tf_op jit(solution)/shard_map/ppermute | solution.py:455
  49.8 20.8 %collective-permute-start.19 = (bf16[128,512]{1,0:T(8,128)(2,1)S(1)}, bf16[128,512]{1,0:T(8,128)(2,1)}, u32[]{:S(2)}, u32[]{:S(2)}) collective-permute-start(bf16[128,512]{1,0:T(8,128)(2,1)S(1)} %collective-permute-done.15.refs_6_.refs_20_), channel_id=1, source_target_pairs={{0,2},{1,3},{2,0},{3,1},{4,6},{5,7},{6,4},{7,5},{8,10},{9,11},{10,... | collective-permute-start | bytes 393224 | tf_op jit(solution)/shard_map/ppermute | solution.py:455
  49.9 46.2 %copy-start.6 = (bf16[128,1024]{1,0:T(8,128)(2,1)}, bf16[128,1024]{1,0:T(8,128)(2,1)S(1)}, u32[]{:S(2)}) copy-start(bf16[128,1024]{1,0:T(8,128)(2,1)S(1)} %collective-permute-done.36.refs_15_) | copy-start | bytes 786436
  49.9 21.9 %collective-permute-start.18 = (bf16[128,512]{1,0:T(8,128)(2,1)S(1)}, bf16[128,512]{1,0:T(8,128)(2,1)}, u32[]{:S(2)}, u32[]{:S(2)}) collective-permute-start(bf16[128,512]{1,0:T(8,128)(2,1)S(1)} %collective-permute-done.14.refs_5_.refs_19_), channel_id=1, source_target_pairs={{0,2},{1,3},{2,0},{3,1},{4,6},{5,7},{6,4},{7,5},{8,10},{9,11},{10,... | collective-permute-start | bytes 393224 | tf_op jit(solution)/shard_map/ppermute | solution.py:455
  56.4 17.0 %collective-permute-start.17 = (bf16[128,512]{1,0:T(8,128)(2,1)S(1)}, bf16[128,512]{1,0:T(8,128)(2,1)}, u32[]{:S(2)}, u32[]{:S(2)}) collective-permute-start(bf16[128,512]{1,0:T(8,128)(2,1)S(1)} %collective-permute-done.13.refs_4_.refs_18_), channel_id=1, source_target_pairs={{0,2},{1,3},{2,0},{3,1},{4,6},{5,7},{6,4},{7,5},{8,10},{9,11},{10,... | collective-permute-start | bytes 393224 | tf_op jit(solution)/shard_map/ppermute | solution.py:455
  69.8 26.3 %collective-permute-start.26 = (bf16[128,1024]{1,0:T(8,128)(2,1)S(1)}, bf16[128,1024]{1,0:T(8,128)(2,1)S(1)}, u32[]{:S(2)}, u32[]{:S(2)}) collective-permute-start(bf16[128,1024]{1,0:T(8,128)(2,1)S(1)} %pad_maximum_fusion.refs_3_), channel_id=1, source_target_pairs={{0,2},{1,3},{2,0},{3,1},{4,6},{5,7},{6,4},{7,5},{8,10},{9,11},{10,... | collective-permute-start | bytes 786440 | tf_op jit(solution)/shard_map/ppermute | solution.py:455
  69.9 26.9 %collective-permute-start.25 = (bf16[128,1024]{1,0:T(8,128)(2,1)S(1)}, bf16[128,1024]{1,0:T(8,128)(2,1)S(1)}, u32[]{:S(2)}, u32[]{:S(2)}) collective-permute-start(bf16[128,1024]{1,0:T(8,128)(2,1)S(1)} %pad_maximum_fusion.refs_3_), channel_id=1, source_target_pairs={{0,5},{1,4},{2,7},{3,6},{4,1},{5,0},{6,3},{7,2},{8,13},{9,12},{10,... | collective-permute-start | bytes 786440 | tf_op jit(solution)/shard_map/ppermute | solution.py:455
  70.6 26.2 %collective-permute-start.24 = (bf16[128,1024]{1,0:T(8,128)(2,1)S(1)}, bf16[128,1024]{1,0:T(8,128)(2,1)S(1)}, u32[]{:S(2)}, u32[]{:S(2)}) collective-permute-start(bf16[128,1024]{1,0:T(8,128)(2,1)S(1)} %pad_maximum_fusion.refs_3_), channel_id=1, source_target_pairs={{0,1},{1,0},{2,3},{3,2},{4,5},{5,4},{6,7},{7,6},{8,9},{9,8},{10,11... | collective-permute-start | bytes 786440 | tf_op jit(solution)/shard_map/ppermute | solution.py:455
  71.8 25.5 %collective-permute-start.23 = (bf16[128,1024]{1,0:T(8,128)(2,1)S(1)}, bf16[128,1024]{1,0:T(8,128)(2,1)S(1)}, u32[]{:S(2)}, u32[]{:S(2)}) collective-permute-start(bf16[128,1024]{1,0:T(8,128)(2,1)S(1)} %pad_maximum_fusion.refs_3_), channel_id=1, source_target_pairs={{0,4},{1,5},{2,6},{3,7},{4,0},{5,1},{6,2},{7,3},{8,12},{9,13},{10,... | collective-permute-start | bytes 786440 | tf_op jit(solution)/shard_map/ppermute | solution.py:455
  73.4 24.0 %collective-permute-start.39 = (bf16[128,1024]{1,0:T(8,128)(2,1)S(1)}, bf16[128,1024]{1,0:T(8,128)(2,1)S(1)}, u32[]{:S(2)}, u32[]{:S(2)}) collective-permute-start(bf16[128,1024]{1,0:T(8,128)(2,1)S(1)} %collective-permute-done.35.refs_14_), channel_id=1, source_target_pairs={{0,2},{1,3},{2,0},{3,1},{4,6},{5,7},{6,4},{7,5},{8,10},{9,11},{10,... | collective-permute-start | bytes 786440 | tf_op jit(solution)/shard_map/ppermute | solution.py:455
  96.2 21.4 %collective-permute-start.38 = (bf16[128,1024]{1,0:T(8,128)(2,1)S(1)}, bf16[128,1024]{1,0:T(8,128)(2,1)S(1)}, u32[]{:S(2)}, u32[]{:S(2)}) collective-permute-start(bf16[128,1024]{1,0:T(8,128)(2,1)S(1)} %collective-permute-done.34.refs_13_), channel_id=1, source_target_pairs={{0,2},{1,3},{2,0},{3,1},{4,6},{5,7},{6,4},{7,5},{8,10},{9,11},{10,... | collective-permute-start | bytes 786440 | tf_op jit(solution)/shard_map/ppermute | solution.py:455
  96.7 20.8 %collective-permute-start.37 = (bf16[128,1024]{1,0:T(8,128)(2,1)S(1)}, bf16[128,1024]{1,0:T(8,128)(2,1)S(1)}, u32[]{:S(2)}, u32[]{:S(2)}) collective-permute-start(bf16[128,1024]{1,0:T(8,128)(2,1)S(1)} %collective-permute-done.33.refs_12_), channel_id=1, source_target_pairs={{0,2},{1,3},{2,0},{3,1},{4,6},{5,7},{6,4},{7,5},{8,10},{9,11},{10,... | collective-permute-start | bytes 786440 | tf_op jit(solution)/shard_map/ppermute | solution.py:455
  96.8 20.7 %collective-permute-start.29 = (bf16[128,1024]{1,0:T(8,128)(2,1)S(1)}, bf16[128,1024]{1,0:T(8,128)(2,1)S(1)}, u32[]{:S(2)}, u32[]{:S(2)}) collective-permute-start(bf16[128,1024]{1,0:T(8,128)(2,1)S(1)} %collective-permute-done.25.refs_6_), channel_id=1, source_target_pairs={{0,2},{1,3},{2,0},{3,1},{4,6},{5,7},{6,4},{7,5},{8,10},{9,11},{10,... | collective-permute-start | bytes 786440 | tf_op jit(solution)/shard_map/ppermute | solution.py:455
  97.3 20.3 %collective-permute-start.28 = (bf16[128,1024]{1,0:T(8,128)(2,1)S(1)}, bf16[128,1024]{1,0:T(8,128)(2,1)S(1)}, u32[]{:S(2)}, u32[]{:S(2)}) collective-permute-start(bf16[128,1024]{1,0:T(8,128)(2,1)S(1)} %collective-permute-done.24.refs_5_), channel_id=1, source_target_pairs={{0,2},{1,3},{2,0},{3,1},{4,6},{5,7},{6,4},{7,5},{8,10},{9,11},{10,... | collective-permute-start | bytes 786440 | tf_op jit(solution)/shard_map/ppermute | solution.py:455
  97.4 20.2 %collective-permute-start.27 = (bf16[128,1024]{1,0:T(8,128)(2,1)S(1)}, bf16[128,1024]{1,0:T(8,128)(2,1)S(1)}, u32[]{:S(2)}, u32[]{:S(2)}) collective-permute-start(bf16[128,1024]{1,0:T(8,128)(2,1)S(1)} %collective-permute-done.23.refs_4_), channel_id=1, source_target_pairs={{0,2},{1,3},{2,0},{3,1},{4,6},{5,7},{6,4},{7,5},{8,10},{9,11},{10,... | collective-permute-start | bytes 786440 | tf_op jit(solution)/shard_map/ppermute | solution.py:455
  209.0 51.4 %copy-start.5 = (bf16[4,4,32,2048]{3,2,1,0:T(8,128)(2,1)S(1)}, bf16[4,4,32,2048]{3,2,1,0:T(8,128)(2,1)}, u32[]{:S(2)}) copy-start(bf16[4,4,32,2048]{3,2,1,0:T(8,128)(2,1)} %get-tuple-element.53) | copy-start | bytes 6291460
  260.2 3.9 %collective-permute-start.40 = (bf16[4,4,32,1152]{3,2,1,0:T(8,128)(2,1)}, bf16[4,4,32,1152]{3,2,1,0:T(8,128)(2,1)S(1)}, u32[]{:S(2)}, u32[]{:S(2)}) collective-permute-start(bf16[4,4,32,1152]{3,2,1,0:T(8,128)(2,1)} %get-tuple-element.51), channel_id=1, source_target_pairs={{0,2},{1,3},{2,0},{3,1},{4,6},{5,7},{6,4},{7,5},{8,10},{9,11},{10,... | collective-permute-start | bytes 3538952 | tf_op jit(solution)/shard_map/ppermute | solution.py:455
  260.3 28.3 %collective-permute-start.47 = (bf16[4,4,32,2048]{3,2,1,0:T(8,128)(2,1)S(1)}, bf16[4,4,32,2048]{3,2,1,0:T(8,128)(2,1)S(1)}, u32[]{:S(2)}, u32[]{:S(2)}) collective-permute-start(bf16[4,4,32,2048]{3,2,1,0:T(8,128)(2,1)S(1)} %copy-done.5), channel_id=1, source_target_pairs={{0,2},{1,3},{2,0},{3,1},{4,6},{5,7},{6,4},{7,5},{8,10},{9,11},{10,... | collective-permute-start | bytes 6291464 | tf_op jit(solution)/shard_map/ppermute | solution.py:455
  265.8 9.9 %collective-permute-start.41 = (bf16[4,32,1152]{2,1,0:T(8,128)(2,1)S(1)}, bf16[4,32,1152]{2,1,0:T(8,128)(2,1)S(1)}, u32[]{:S(2)}, u32[]{:S(2)}) collective-permute-start(bf16[4,32,1152]{2,1,0:T(8,128)(2,1)S(1)} %get-tuple-element.61), channel_id=1, source_target_pairs={{0,4},{1,5},{2,6},{3,7},{4,0},{5,1},{6,2},{7,3},{8,12},{9,13},{10,... | collective-permute-start | bytes 884744 | tf_op jit(solution)/shard_map/ppermute | solution.py:455
  266.3 14.9 %collective-permute-start.43 = (bf16[4,32,1152]{2,1,0:T(8,128)(2,1)S(1)}, bf16[4,32,1152]{2,1,0:T(8,128)(2,1)S(1)}, u32[]{:S(2)}, u32[]{:S(2)}) collective-permute-start(bf16[4,32,1152]{2,1,0:T(8,128)(2,1)S(1)} %get-tuple-element.62), channel_id=1, source_target_pairs={{0,5},{1,4},{2,7},{3,6},{4,1},{5,0},{6,3},{7,2},{8,13},{9,12},{10,... | collective-permute-start | bytes 884744 | tf_op jit(solution)/shard_map/ppermute | solution.py:455
  267.7 14.8 %collective-permute-start.42 = (bf16[4,32,1152]{2,1,0:T(8,128)(2,1)S(1)}, bf16[4,32,1152]{2,1,0:T(8,128)(2,1)S(1)}, u32[]{:S(2)}, u32[]{:S(2)}) collective-permute-start(bf16[4,32,1152]{2,1,0:T(8,128)(2,1)S(1)} %get-tuple-element.63), channel_id=1, source_target_pairs={{0,1},{1,0},{2,3},{3,2},{4,5},{5,4},{6,7},{7,6},{8,9},{9,8},{10,11... | collective-permute-start | bytes 884744 | tf_op jit(solution)/shard_map/ppermute | solution.py:455
  282.7 9.8 %collective-permute-start.44 = (bf16[32,1152]{1,0:T(8,128)(2,1)S(1)}, bf16[32,1152]{1,0:T(8,128)(2,1)S(1)}, u32[]{:S(2)}, u32[]{:S(2)}) collective-permute-start(bf16[32,1152]{1,0:T(8,128)(2,1)S(1)} %get-tuple-element.67), channel_id=1, source_target_pairs={{0,8},{1,9},{2,10},{3,11},{4,12},{5,13},{6,14},{7,15},{8,16},{9,17... | collective-permute-start | bytes 221192 | tf_op jit(solution)/shard_map/ppermute | solution.py:455
  284.7 8.5 %collective-permute-start.46 = (bf16[32,1152]{1,0:T(8,128)(2,1)S(1)}, bf16[32,1152]{1,0:T(8,128)(2,1)S(1)}, u32[]{:S(2)}, u32[]{:S(2)}) collective-permute-start(bf16[32,1152]{1,0:T(8,128)(2,1)S(1)} %get-tuple-element.68), channel_id=1, source_target_pairs={{0,24},{1,25},{2,26},{3,27},{4,28},{5,29},{6,30},{7,31},{8,0},{9,1... | collective-permute-start | bytes 221192 | tf_op jit(solution)/shard_map/ppermute | solution.py:455
  286.5 6.6 %collective-permute-start.45 = (bf16[32,1152]{1,0:T(8,128)(2,1)S(1)}, bf16[32,1152]{1,0:T(8,128)(2,1)S(1)}, u32[]{:S(2)}, u32[]{:S(2)}) collective-permute-start(bf16[32,1152]{1,0:T(8,128)(2,1)S(1)} %get-tuple-element.69), channel_id=1, source_target_pairs={{0,16},{1,17},{2,18},{3,19},{4,20},{5,21},{6,22},{7,23},{8,24},{9,... | collective-permute-start | bytes 221192 | tf_op jit(solution)/shard_map/ppermute | solution.py:455
  289.6 14.9 %collective-permute-start.48 = (bf16[4,32,2048]{2,1,0:T(8,128)(2,1)S(1)}, bf16[4,32,2048]{2,1,0:T(8,128)(2,1)S(1)}, u32[]{:S(2)}, u32[]{:S(2)}) collective-permute-start(bf16[4,32,2048]{2,1,0:T(8,128)(2,1)S(1)} %get-tuple-element.58), channel_id=1, source_target_pairs={{0,4},{1,5},{2,6},{3,7},{4,0},{5,1},{6,2},{7,3},{8,12},{9,13},{10,... | collective-permute-start | bytes 1572872 | tf_op jit(solution)/shard_map/ppermute | solution.py:455
  291.0 21.7 %collective-permute-start.50 = (bf16[4,32,2048]{2,1,0:T(8,128)(2,1)S(1)}, bf16[4,32,2048]{2,1,0:T(8,128)(2,1)S(1)}, u32[]{:S(2)}, u32[]{:S(2)}) collective-permute-start(bf16[4,32,2048]{2,1,0:T(8,128)(2,1)S(1)} %get-tuple-element.59), channel_id=1, source_target_pairs={{0,5},{1,4},{2,7},{3,6},{4,1},{5,0},{6,3},{7,2},{8,13},{9,12},{10,... | collective-permute-start | bytes 1572872 | tf_op jit(solution)/shard_map/ppermute | solution.py:455
  292.5 21.6 %collective-permute-start.49 = (bf16[4,32,2048]{2,1,0:T(8,128)(2,1)S(1)}, bf16[4,32,2048]{2,1,0:T(8,128)(2,1)S(1)}, u32[]{:S(2)}, u32[]{:S(2)}) collective-permute-start(bf16[4,32,2048]{2,1,0:T(8,128)(2,1)S(1)} %get-tuple-element.60), channel_id=1, source_target_pairs={{0,1},{1,0},{2,3},{3,2},{4,5},{5,4},{6,7},{7,6},{8,9},{9,8},{10,11... | collective-permute-start | bytes 1572872 | tf_op jit(solution)/shard_map/ppermute | solution.py:455
  314.4 7.0 %collective-permute-start.51 = (bf16[32,2048]{1,0:T(8,128)(2,1)S(1)}, bf16[32,2048]{1,0:T(8,128)(2,1)S(1)}, u32[]{:S(2)}, u32[]{:S(2)}) collective-permute-start(bf16[32,2048]{1,0:T(8,128)(2,1)S(1)} %get-tuple-element.64), channel_id=1, source_target_pairs={{0,8},{1,9},{2,10},{3,11},{4,12},{5,13},{6,14},{7,15},{8,16},{9,17... | collective-permute-start | bytes 393224 | tf_op jit(solution)/shard_map/ppermute | solution.py:455
  314.8 6.7 %collective-permute-start.53 = (bf16[32,2048]{1,0:T(8,128)(2,1)S(1)}, bf16[32,2048]{1,0:T(8,128)(2,1)S(1)}, u32[]{:S(2)}, u32[]{:S(2)}) collective-permute-start(bf16[32,2048]{1,0:T(8,128)(2,1)S(1)} %get-tuple-element.65), channel_id=1, source_target_pairs={{0,24},{1,25},{2,26},{3,27},{4,28},{5,29},{6,30},{7,31},{8,0},{9,1... | collective-permute-start | bytes 393224 | tf_op jit(solution)/shard_map/ppermute | solution.py:455
  318.3 7.2 %collective-permute-start.52 = (bf16[32,2048]{1,0:T(8,128)(2,1)S(1)}, bf16[32,2048]{1,0:T(8,128)(2,1)S(1)}, u32[]{:S(2)}, u32[]{:S(2)}) collective-permute-start(bf16[32,2048]{1,0:T(8,128)(2,1)S(1)} %get-tuple-element.66), channel_id=1, source_target_pairs={{0,16},{1,17},{2,18},{3,19},{4,20},{5,21},{6,22},{7,23},{8,24},{9,... | collective-permute-start | bytes 393224 | tf_op jit(solution)/shard_map/ppermute | solution.py:455
  (21 other events, 426.3 us)

commit v3 on v2

v3 whole, which is shorter than its diff:
```python
import jax
import jax.numpy as jnp
from jax import lax
from jax.experimental import pallas as pl
from jax.experimental.pallas import tpu as pltpu
from jax.sharding import PartitionSpec as P

D = 512
FF = 2048
HEAD = 64
FTOK = 8
SEQ = 48
HALVES = 2
HW = D // HALVES
FW = FF // HALVES
PAIR = 2 * HEAD
GC = 128
EPS = 1e-05
CHUNK = 256
BF = jnp.bfloat16
F32 = jnp.float32


def nn(a, b):
    return lax.dot_general(a, b, (((1,), (0,)), ((), ())), preferred_element_type=F32)


def nt(a, b):
    return lax.dot_general(a, b, (((1,), (1,)), ((), ())), preferred_element_type=F32)


def tn(a, b):
    return lax.dot_general(a, b, (((0,), (0,)), ((), ())), preferred_element_type=F32)


def norm_parts(rows):
    mean = jnp.mean(rows, axis=-1, keepdims=True)
    centered = rows - mean
    spread = jnp.mean(centered * centered, axis=-1, keepdims=True)
    rstd = lax.rsqrt(spread + EPS)
    return centered * rstd, rstd


def norm_back(n, rstd, gain, gy):
    gg = gy * gain
    first = jnp.mean(gg, axis=-1, keepdims=True)
    second = jnp.mean(gg * n, axis=-1, keepdims=True)
    return rstd * (gg - first - n * second)


def fold_rows(value):
    return jnp.sum(value.reshape(value.shape[0] // 8, 8, value.shape[1]), axis=0)


def per_head(rows):
    width = rows.shape[1]
    lane = lax.broadcasted_iota(jnp.int32, rows.shape, 1) // HEAD
    pad = jnp.zeros((HEAD - SEQ, width), rows.dtype)
    parts = []
    for h in range(width // HEAD):
        parts.append(jnp.where(lane == h, rows, jnp.zeros_like(rows)))
        parts.append(pad)
    return jnp.concatenate(parts, axis=0)


def pair_blocks(product):
    lane = lax.broadcasted_iota(jnp.int32, (SEQ, PAIR), 1)
    return jnp.where(lane < HEAD, product[:SEQ], product[HEAD : HEAD + SEQ])


def seq_slice(s, c, width):
    return (slice(s * SEQ, (s + 1) * SEQ), slice(c * width, (c + 1) * width))


def block_place(place, cr, xr, yr, zr):
    z, x, c, y = place[0], place[1], place[2], place[3]
    z = lax.rem(z - zr + place[4], place[4])
    return (y ^ yr, z * 4 + (x ^ xr) * 2 + (c ^ cr))


def load_pieces(place, pieces, metas, dst, sems):
    copies = []
    for piece, meta in zip(pieces, metas):
        depth = piece.shape[0] // len(meta)
        n_dp = D // depth
        for b, rel in enumerate(meta):
            m, dp = block_place(place, *rel)
            row = pl.multiple_of((m * n_dp + dp) * depth, depth)
            copy = pltpu.make_async_copy(
                piece.at[pl.ds(b * depth, depth), :], dst.at[pl.ds(row, depth), :], sems.at[len(copies)]
            )
            copy.start()
            copies.append(copy)
    return copies


def wait_all(copies):
    for copy in copies:
        copy.wait()


def store_blocks(place, acc, start, own_ref, other_ref):
    slots, n_z, depth, width = own_ref.shape
    n_dp = n_z * 4
    for core in range(2):

        @pl.when(place[2] == core)
        def _():
            for m in range(HALVES):
                for dp in range(n_dp):
                    z, x, c = dp // 4, (dp // 2) % 2, dp % 2
                    slot = (place[1] ^ x) + 2 * (place[3] ^ m)
                    back = lax.rem(z - place[0] + n_z, n_z)
                    rows = slice(dp * depth, (dp + 1) * depth)
                    ref = own_ref if c == core else other_ref
                    ref[slot, back, :, start : start + acc.shape[2]] = acc[m, rows, :].astype(BF)


def attn_forward_kernel(place, frames, metas, x_ref, *refs):
    n = len(metas)
    pieces = refs[:n]
    q_ref, k_ref, v_ref, p_ref, ho_ref, hidden_ref, vec_ref, w_ref, s_ref, sems = refs[n:]
    step = pl.program_id(0)
    seqs = x_ref.shape[0] // SEQ

    @pl.when(step == 0)
    def _():
        wait_all(load_pieces(place, pieces, metas, w_ref, sems))
        vec_ref[...] = w_ref[:D, 4 * HW :].astype(F32).T[:8]

    x = x_ref[...].astype(F32)
    n, _ = norm_parts(x)
    normed = (n * vec_ref[0:1] + vec_ref[1:2]).astype(BF)
    for m in range(HALVES):
        qkv = nn(normed, w_ref[m * D : (m + 1) * D, : 3 * HW]).astype(BF)
        cols = slice(m * HW, (m + 1) * HW)
        q_ref[:, cols] = qkv[:, :HW]
        k_ref[:, cols] = qkv[:, HW : 2 * HW]
        v_ref[:, cols] = qkv[:, 2 * HW :]
    for s in range(seqs):
        for m in range(HALVES):
            at = seq_slice(s, m, HW)
            s_ref[at] = nt(k_ref[at], per_head(q_ref[at]))
    key = lax.broadcasted_iota(jnp.int32, (SEQ, PAIR), 0)
    query = lax.broadcasted_iota(jnp.int32, (SEQ, PAIR), 1) % HEAD
    for s in range(seqs):
        allowed = (key <= query) & (key < frames[step * seqs + s] * FTOK)
        for c in range(D // PAIR):
            at = seq_slice(s, c, PAIR)
            scores = jnp.where(allowed, s_ref[at] * HEAD**-0.5, -1000000000.0)
            expd = jnp.exp(scores - jnp.max(scores, axis=0, keepdims=True))
            p_ref[at] = (expd * (1.0 / jnp.sum(expd, axis=0, keepdims=True))).astype(BF)
    for s in range(seqs):
        for c in range(D // PAIR):
            at = seq_slice(s, c, PAIR)
            ho_ref[at] = pair_blocks(tn(p_ref[at], v_ref[at])).astype(BF)
    attended = nt(ho_ref[:, :HW], w_ref[:D, 3 * HW : 4 * HW]) + nt(ho_ref[:, HW:], w_ref[D:, 3 * HW : 4 * HW])
    hidden_ref[...] = x + attended


GELU_A = (2.0 / jnp.pi) ** 0.5
GELU_B = 0.044715


def feed_forward_kernel(place, live, metas, hidden_ref, cot_ref, ho_ref, vec_ref, *refs):
    n = len(metas)
    (
        mixed_ref, gh_ref, own_ref, other_ref, gv_ref,
        w_ref, accu_ref, accd_ref, acco_ref, gvacc_ref, act_ref, gup_ref, go_ref, sems,
    ) = refs[n:]
    step = pl.program_id(0)
    last = pl.num_programs(0) - 1
    rows = hidden_ref.shape[0]

    @pl.when(step == 0)
    def _():
        copies = load_pieces(place, refs[:n], metas, w_ref, sems)
        accu_ref[...] = jnp.zeros_like(accu_ref)
        accd_ref[...] = jnp.zeros_like(accd_ref)
        acco_ref[...] = jnp.zeros_like(acco_ref)
        gvacc_ref[...] = jnp.zeros_like(gvacc_ref)
        wait_all(copies)

    hidden = hidden_ref[...]
    n, rstd = norm_parts(hidden)
    normed = (n * vec_ref[2:3] + vec_ref[3:4]).astype(BF)
    row = lax.broadcasted_iota(jnp.int32, (rows, 1), 0) + step * rows
    go = jnp.where(row < live[0] * SEQ, cot_ref[...].astype(F32), 0.0)
    go_ref[...] = go.astype(BF)
    for m in range(HALVES):
        for c in range(FW // CHUNK):
            depth = slice(m * D, (m + 1) * D)
            cols = slice(m * FW + c * CHUNK, m * FW + (c + 1) * CHUNK)
            up = nn(normed, w_ref[depth, c * CHUNK : (c + 1) * CHUNK])
            ga = nn(go_ref[...], w_ref[depth, FW + c * CHUNK : FW + (c + 1) * CHUNK])
            sq = up * up
            th = jnp.tanh(up * (GELU_A + (GELU_A * GELU_B) * sq))
            half = 0.5 + 0.5 * th
            act_ref[:, cols] = (up * half).astype(BF)
            slope = half + (0.5 * up) * (1.0 - th * th) * (GELU_A + (3.0 * GELU_A * GELU_B) * sq)
            gup_ref[:, cols] = (ga * slope).astype(BF)
    down = jnp.zeros((rows, D), F32)
    gy = jnp.zeros((rows, D), F32)
    for m in range(HALVES):
        cols = slice(m * FW, (m + 1) * FW)
        down += nt(act_ref[:, cols], w_ref[m * D : (m + 1) * D, FW:])
        gy += nt(gup_ref[:, cols], w_ref[m * D : (m + 1) * D, :FW])
        accu_ref[m] += tn(normed, gup_ref[:, cols])
        accd_ref[m] += tn(go_ref[...], act_ref[:, cols])
    mixed_ref[...] = (hidden + down).astype(BF)
    gh = go + norm_back(n, rstd, vec_ref[2:3], gy)
    gh_ref[...] = gh
    for m in range(HALVES):
        acco_ref[m] += tn(gh.astype(BF), ho_ref[:, m * HW : (m + 1) * HW])
    gvacc_ref[0] += fold_rows(gy * n)
    gvacc_ref[1] += fold_rows(gy)

    @pl.when(step == last)
    def _():
        store_blocks(place, accu_ref, 0, own_ref, other_ref)
        store_blocks(place, accd_ref, FW, own_ref, other_ref)
        store_blocks(place, acco_ref, 2 * FW, own_ref, other_ref)
        gv_ref[0:1] = jnp.sum(gvacc_ref[0], axis=0, keepdims=True)
        gv_ref[1:2] = jnp.sum(gvacc_ref[1], axis=0, keepdims=True)


def attn_backward_kernel(
    place, x_ref, gh_ref, q_ref, k_ref, v_ref, p_ref, w_ref, vec_ref, gvtwo_ref,
    gi_ref, own_ref, other_ref, acc_ref, gvacc_ref, gvec_ref, s_ref, ds_ref, dh_ref, dqkv_ref,
):
    step = pl.program_id(0)
    last = pl.num_programs(0) - 1
    seqs = x_ref.shape[0] // SEQ

    @pl.when(step == 0)
    def _():
        acc_ref[...] = jnp.zeros_like(acc_ref)
        gvacc_ref[...] = jnp.zeros_like(gvacc_ref)

    gh = gh_ref[...]
    gat = gh.astype(BF)
    for m in range(HALVES):
        dh_ref[:, m * HW : (m + 1) * HW] = nn(gat, w_ref[m * D : (m + 1) * D, 3 * HW : 4 * HW]).astype(BF)
    for s in range(seqs):
        for c in range(D // PAIR):
            at = seq_slice(s, c, PAIR)
            s_ref[at] = nt(v_ref[at], per_head(dh_ref[at]))
    for s in range(seqs):
        for c in range(D // PAIR):
            at = seq_slice(s, c, PAIR)
            probs = p_ref[at].astype(F32)
            gp = s_ref[at]
            delta = jnp.sum(probs * gp, axis=0, keepdims=True)
            ds_ref[at] = (probs * ((gp - delta) * HEAD**-0.5)).astype(BF)
    for s in range(seqs):
        for c in range(D // PAIR):
            at = seq_slice(s, c, PAIR)
            base = 3 * HW * (c * PAIR // HW) + c * PAIR % HW
            dqkv_ref[at[0], base + 2 * HW : base + 2 * HW + PAIR] = nn(p_ref[at], per_head(dh_ref[at])).astype(BF)
            dqkv_ref[at[0], base + HW : base + HW + PAIR] = nn(ds_ref[at], per_head(q_ref[at])).astype(BF)
    for s in range(seqs):
        for c in range(D // PAIR):
            at = seq_slice(s, c, PAIR)
            base = 3 * HW * (c * PAIR // HW) + c * PAIR % HW
            dqkv_ref[at[0], base : base + PAIR] = pair_blocks(tn(ds_ref[at], k_ref[at])).astype(BF)
    n, rstd = norm_parts(x_ref[...].astype(F32))
    normed = (n * vec_ref[0:1] + vec_ref[1:2]).astype(BF)
    gy = jnp.zeros(x_ref.shape, F32)
    for m in range(HALVES):
        cols = slice(3 * HW * m, 3 * HW * (m + 1))
        gy += nt(dqkv_ref[:, cols], w_ref[m * D : (m + 1) * D, : 3 * HW])
        acc_ref[m] += tn(normed, dqkv_ref[:, cols])
    gi_ref[...] = gh + norm_back(n, rstd, vec_ref[0:1], gy)
    gvacc_ref[0] += fold_rows(gy * n)
    gvacc_ref[1] += fold_rows(gy)

    @pl.when(step == last)
    def _():
        store_blocks(place, acc_ref, 0, own_ref, other_ref)
        one = jnp.concatenate([jnp.sum(gvacc_ref[i], axis=0, keepdims=True) for i in range(2)], axis=0)
        rows = jnp.concatenate([one, gvtwo_ref[...], jnp.zeros((GC - 4, D), F32)], axis=0)
        for m in range(HALVES):
            gvec_ref[m] = rows.T
        store_blocks(place, gvec_ref, 3 * HW, own_ref, other_ref)


def step_rows(rows):
    return 16 * SEQ if rows % (16 * SEQ) == 0 else 8 * SEQ


def row_block(rows, width):
    return pl.BlockSpec((step_rows(rows), width), lambda i, *_: (i, 0))


def held(shape):
    return pl.BlockSpec(shape, lambda i, *_: (0,) * len(shape), pipeline_mode=pl.Buffered(1))


def shape(dims, dtype):
    return jax.ShapeDtypeStruct(dims, dtype)


PARAMS = pltpu.CompilerParams(vmem_limit_bytes=60 * 1024 * 1024)
HBM = pl.BlockSpec(memory_space=pl.ANY)


def weight_dims(group):
    return (HALVES * D, group[0][0].shape[1])


def copy_sems(group):
    return pltpu.SemaphoreType.DMA((sum(len(meta) for meta in group[1]),))


def cost(flops, nbytes):
    return pl.CostEstimate(flops=flops, bytes_accessed=nbytes, transcendentals=0)


def attn_forward(place, frames, tokens, group):
    rows = tokens.shape[0]
    dims = weight_dims(group)
    return pl.pallas_call(
        lambda place, frames, *refs: attn_forward_kernel(place, frames, group[1], *refs),
        grid_spec=pltpu.PrefetchScalarGridSpec(
            num_scalar_prefetch=2,
            grid=(rows // step_rows(rows),),
            in_specs=[row_block(rows, D)] + [HBM] * len(group[0]),
            out_specs=[row_block(rows, D)] * 6 + [held((8, D)), held(dims)],
            scratch_shapes=[pltpu.VMEM((step_rows(rows), D), F32), copy_sems(group)],
        ),
        out_shape=[shape((rows, D), BF)] * 5 + [shape((rows, D), F32), shape((8, D), F32), shape(dims, BF)],
        compiler_params=PARAMS,
        cost_estimate=cost(rows * D * D * 24, rows * D * 18),
        name="attn_forward",
    )(place, frames, tokens, *group[0])


def feed_forward(place, live, hidden, cotangent, ho, vec, group, out_dims):
    rows = hidden.shape[0]
    grads = out_dims + (2 * FW + HW,)
    dims = weight_dims(group)
    return pl.pallas_call(
        lambda place, live, *refs: feed_forward_kernel(place, live, group[1], *refs),
        grid_spec=pltpu.PrefetchScalarGridSpec(
            num_scalar_prefetch=2,
            grid=(rows // step_rows(rows),),
            in_specs=[row_block(rows, D)] * 3 + [held((8, D))] + [HBM] * len(group[0]),
            out_specs=[row_block(rows, D), row_block(rows, D), held(grads), held(grads), held((2, D))],
            scratch_shapes=[
                pltpu.VMEM(dims, BF),
                pltpu.VMEM((HALVES, D, FW), F32),
                pltpu.VMEM((HALVES, D, FW), F32),
                pltpu.VMEM((HALVES, D, HW), F32),
                pltpu.VMEM((2, 8, D), F32),
                pltpu.VMEM((step_rows(rows), FF), BF),
                pltpu.VMEM((step_rows(rows), FF), BF),
                pltpu.VMEM((step_rows(rows), D), BF),
                copy_sems(group),
            ],
        ),
        out_shape=[
            shape((rows, D), BF),
            shape((rows, D), F32),
            shape(grads, BF),
            shape(grads, BF),
            shape((2, D), F32),
        ],
        compiler_params=PARAMS,
        cost_estimate=cost(rows * D * FF * 12, rows * D * 12),
        name="feed_forward",
    )(place, live, hidden, cotangent, ho, vec, *group[0])


def attn_backward(place, tokens, gh, q, k, v, p, w, vec, gv_two, out_dims):
    rows = tokens.shape[0]
    grads = out_dims + (3 * HW + GC,)
    return pl.pallas_call(
        attn_backward_kernel,
        grid_spec=pltpu.PrefetchScalarGridSpec(
            num_scalar_prefetch=1,
            grid=(rows // step_rows(rows),),
            in_specs=[row_block(rows, D)] * 6 + [held(w.shape), held((8, D)), held((2, D))],
            out_specs=[row_block(rows, D), held(grads), held(grads)],
            scratch_shapes=[
                pltpu.VMEM((HALVES, D, 3 * HW), F32),
                pltpu.VMEM((2, 8, D), F32),
                pltpu.VMEM((HALVES, D, GC), F32),
                pltpu.VMEM((step_rows(rows), D), F32),
                pltpu.VMEM((step_rows(rows), D), BF),
                pltpu.VMEM((step_rows(rows), D), BF),
                pltpu.VMEM((step_rows(rows), 3 * D), BF),
            ],
        ),
        out_shape=[shape((rows, D), F32), shape(grads, BF), shape(grads, BF)],
        compiler_params=PARAMS,
        cost_estimate=cost(rows * D * D * 36, rows * D * 18),
        name="attn_backward",
    )(place, tokens, gh, q, k, v, p, w, vec, gv_two)


def build(mesh):
    n_dp, n_mp = mesh.shape["dp"], mesh.shape["mp"]
    n_z = n_dp // 4
    depth = D // n_dp
    staged = n_mp == HALVES
    both = ("dp", "mp")
    PLANE = ((0, 0), (1, 0), (0, 1), (1, 1))

    def send(value, zr=0, xr=0, yr=0, cr=0):
        pairs = []
        for z in range(n_z):
            for x in range(2):
                for c in range(2):
                    for y in range(n_mp):
                        here = ((z * 2 + x) * 2 + c) * n_mp + y
                        there = ((((z + zr) % n_z) * 2 + (x ^ xr)) * 2 + (c ^ cr)) * n_mp + (y ^ yr)
                        pairs.append((here, there))
        return lax.ppermute(value, both, pairs)

    def along_z(value):
        return [value] + [send(value, zr=r) for r in range(1, n_z)]

    def across_plane(value):
        return [value] + [send(value, xr=x, yr=y) for x, y in PLANE[1:]]

    def both_cores(pieces):
        return pieces + [send(piece, cr=1) for piece in pieces]

    def stack(blocks):
        return jnp.concatenate(blocks, axis=0)

    Z_FIRST = tuple(tuple((c, x, y, z) for z in range(n_z)) for c in range(2) for x, y in PLANE)
    PLANE_FIRST = tuple(tuple((c, x, y, z) for x, y in PLANE) for c in range(2) for z in range(n_z))

    def after(value, *others):
        return lax.optimization_barrier((value,) + others)[0]

    def gather_first(attn, ff):
        attn_z = along_z(attn)
        attn_plane = across_plane(stack(attn_z))
        ff_z = along_z(after(ff, attn_z[-1]))
        ff_plane = across_plane(after(stack(ff_z), attn_plane[-1]))
        return (both_cores(attn_plane), Z_FIRST), ff_plane

    def gather_last(ff_plane, done):
        ff_plane = [after(piece, done) for piece in ff_plane]
        return both_cores(ff_plane), Z_FIRST

    def gather_plain(block, parts):
        out = lax.all_gather(block, ("mp", "dp"), axis=0, tiled=True)
        out = out.reshape(HALVES, n_mp // HALVES, D, parts, -1)
        return out.transpose(0, 2, 3, 1, 4).reshape(HALVES * D, -1)

    def plain_pieces(whole):
        z, x, c = lax.axis_index("dp") // 4, (lax.axis_index("dp") // 2) % 2, lax.axis_index("dp") % 2
        y = lax.axis_index("mp") % HALVES
        blocks = whole.reshape(HALVES, n_z, 2, 2, depth, -1)
        index = lambda n, at: (at - jnp.arange(n)) % n
        blocks = blocks[:, index(n_z, z)]
        blocks = blocks[y ^ jnp.arange(2)][:, :, x ^ jnp.arange(2)][:, :, :, c ^ jnp.arange(2)]
        blocks = blocks.transpose(3, 0, 2, 1, 4, 5).reshape(8, n_z * depth, -1)
        return [blocks[i] for i in range(8)], Z_FIRST

    def scatter_core(own, other):
        return (own.astype(F32) + send(other, cr=1).astype(F32)).astype(BF)

    def scatter_plane(mine):
        return mine[0], [send(mine[x + 2 * y], xr=x, yr=y) for x, y in PLANE[1:]]

    def scatter_add(mine, got):
        got = [part.astype(F32) for part in got]
        return ((mine.astype(F32) + got[0]) + (got[1] + got[2])).astype(BF)

    def scatter_z(mine):
        return mine[0], [send(mine[r], zr=r) for r in range(1, n_z)]

    def scatter_sum(mine, got):
        total = mine.astype(F32)
        for part in got:
            total += part.astype(F32)
        return total

    def scatter_plain(own, other, parts):
        z, x, c = lax.axis_index("dp") // 4, (lax.axis_index("dp") // 2) % 2, lax.axis_index("dp") % 2
        y = lax.axis_index("mp") % HALVES
        blocks = jnp.stack([own, other]).reshape(2, 2, 2, n_z, depth, -1)
        blocks = blocks[c ^ jnp.arange(2)][:, y ^ jnp.arange(2)][:, :, x ^ jnp.arange(2)]
        blocks = blocks[:, :, :, (jnp.arange(n_z) - z) % n_z]
        blocks = blocks.transpose(1, 3, 2, 0, 4, 5).reshape(HALVES, D, -1)
        main, start = [], 0
        for part in parts:
            cut = blocks[:, :, start : start + part].reshape(HALVES, D, n_mp // HALVES, -1)
            main.append(cut.transpose(0, 2, 1, 3).reshape(n_mp, D, -1))
            start += part
        main = jnp.concatenate(main, axis=2)
        tail = jnp.broadcast_to(blocks[:1, :, start:], (n_mp, D, blocks.shape[2] - start))
        flat = jnp.concatenate([main, tail], axis=2).reshape(n_mp * D, -1)
        return lax.psum_scatter(flat, ("mp", "dp"), scatter_dimension=0, tiled=True).astype(F32)

    def shards(
        tokens, cotangent, frame_count, live_count, w_query, w_key, w_value, w_out, w_up, w_down,
        gain_one, shift_one, gain_two, shift_two,
    ):
        dp, mp = lax.axis_index("dp"), lax.axis_index("mp")
        place = jnp.stack([dp // 4, (dp // 2) % 2, dp % 2, mp % HALVES, jnp.int32(n_z)]).astype(jnp.int32)
        seqs = tokens.shape[0] // SEQ
        frames = lax.dynamic_slice(frame_count, (mp * seqs,), (seqs,))
        live = live_count - mp * seqs
        vec = jnp.stack([gain_one, shift_one, gain_two, shift_two], axis=1)
        vec = jnp.pad(vec, ((0, 0), (0, GC - 4)))
        attn = jnp.concatenate([w_query, w_key, w_value, w_out.T], axis=1)
        ff = jnp.concatenate([w_up, w_down.T], axis=1)
        out_dims = (4, n_z, depth)
        if staged:
            attn, ff = gather_first(jnp.concatenate([attn, vec], axis=1), ff)
        else:
            vec = lax.all_gather(vec, "dp", axis=0, tiled=True)
            attn = jnp.concatenate([gather_plain(attn, 4), jnp.concatenate([vec] * HALVES)], axis=1)
            attn = plain_pieces(attn)
            ff = plain_pieces(gather_plain(ff, 2))
        q, k, v, p, ho, hidden, vec, wa = attn_forward(place, frames, tokens, attn)
        if staged:
            ff = gather_last(ff, vec)
        mixed, gh, f_own, f_other, gv_two = feed_forward(
            place, live, hidden, cotangent, ho, vec, ff, out_dims
        )
        if staged:
            f_mine = scatter_core(f_own, f_other)
            gh = after(gh, f_mine)
            f_mine, f_got = scatter_plane(f_mine)
        grad_input, a_own, a_other = attn_backward(
            place, tokens, gh, q, k, v, p, wa, vec, gv_two, out_dims
        )
        if staged:
            a_mine = scatter_core(a_own, a_other)
            f_mine = after(scatter_add(f_mine, f_got), a_mine)
            f_mine, f_got = scatter_z(f_mine)
            a_mine, a_got = scatter_plane(a_mine)
            a_mine = after(scatter_add(a_mine, a_got), *f_got)
            gf = scatter_sum(f_mine, f_got)
            ga = scatter_sum(*scatter_z(a_mine))
        else:
            gf = scatter_plain(f_own, f_other, (FW, FW, HW))
            ga = scatter_plain(a_own, a_other, (HW,) * 3)
        wide = w_query.shape[1]
        tall = w_up.shape[1]
        gains = ga[:, 3 * wide :]
        return (
            mixed,
            grad_input,
            ga[:, :wide],
            ga[:, wide : 2 * wide],
            ga[:, 2 * wide : 3 * wide],
            gf[:, 2 * tall :].T,
            gf[:, :tall],
            gf[:, tall : 2 * tall].T,
            gains[:, 0],
            gains[:, 1],
            gains[:, 2],
            gains[:, 3],
        )

    return shards


def solution(mesh):
    rows = P(("dp", "mp"), None)
    wide, tall, dp = P("dp", "mp"), P("mp", "dp"), P("dp")
    return jax.shard_map(
        build(mesh),
        mesh=mesh,
        in_specs=(rows, rows, dp, dp, wide, wide, wide, tall, wide, tall, dp, dp, dp, dp),
        out_specs=(rows, rows, wide, wide, wide, tall, wide, tall, dp, dp, dp, dp),
        check_vma=False,
    )
```

time: 327 us -> 241 us (0.74)
  waiting for transfers between devices: 79.5 us -> 33 us
  Pallas kernels: 184 us -> 154 us
  starting transfers between devices: 48.1 us -> 36.8 us
  local copies, waits for them, and re-layouts: 5.44 us -> 8.77 us
    ppermute x54 -> x34, waiting for transfers between devices: 79.5 us -> 33 us  [send(): return lax.ppermute(value, both, pairs)]
    pallas_call x3 -> x2, Pallas kernels: 93.4 us -> 75 us  [the longest x1 44.9 us: attn_backward(): pl.pallas_call(attn_backward_kernel, grid_spec=pltpu.PrefetchScalarGridSp...]
    pallas_call x1, Pallas kernels: 90.3 us -> 78.6 us  [feed_forward(): pl.pallas_call(lambda place, live, *refs: feed_forward_kernel(place, live...]
    ppermute x54 -> x34, starting transfers between devices: 48.1 us -> 36.8 us  [send(): return lax.ppermute(value, both, pairs)]
  transfers between devices with their start and end apart: 54 -> 34, of which waited for: 22 -> 17; matrix products, arithmetic and copies ran while one was open for 3% -> 3% of each run, Pallas kernels for 13% -> 31%
where the time goes in v3:
time: 241 us; the launch traced here: 240 us
  Pallas kernels  154 us (64%)
  starting transfers between devices  36.8 us (15%)
  waiting for transfers between devices  33 us (14%)
  local copies, waits for them, and re-layouts  8.77 us (4%)
  other arithmetic  6.17 us (3%)
    pallas_call x1, Pallas kernels, feed_forward(): pl.pallas_call(lambda place, live, *refs: feed_forward_kernel(place, live...  78.6 us
    pallas_call x1, Pallas kernels, attn_backward(): pl.pallas_call(attn_backward_kernel, grid_spec=pltpu.PrefetchScalarGridSp...  44.9 us
    ppermute x34, starting transfers between devices, send(): return lax.ppermute(value, both, pairs)  36.8 us
    ppermute x34, waiting for transfers between devices, send(): return lax.ppermute(value, both, pairs)  33 us
    pallas_call x1, Pallas kernels, attn_forward(): pl.pallas_call(lambda place, frames, *refs: attn_forward_kernel(place, fr...  30.1 us
  transfers between devices with their start and end apart: 34, of which 17 were waited for; matrix products, arithmetic and copies ran while one was open for 3% of the time, Pallas kernels for 31%

profile of v3, /device:TPU:0, one launch (start us, length us, event | category | flops | bytes accessed | tf_op | source)
XLA Modules:
  0.0 239.9 jit_solution(8675819512975445781)
XLA Ops:
  0.6 0.7 pad_maximum_fusion.3
  1.5 0.7 constant_dynamic-update-slice_fusion.3
  2.2 0.7 constant_dynamic-update-slice_fusion.2
  2.9 0.7 constant_dynamic-update-slice_fusion.1
  3.6 0.7 bitcast_dynamic-update-slice_fusion
  4.4 5.1 %collective-permute-start.2 = (bf16[32,1152]{1,0:T(8,128)(2,1)S(1)}, bf16[32,1152]{1,0:T(8,128)(2,1)S(1)}, u32[]{:S(2)}, u32[]{:S(2)}) collective-permute-start(bf16[32,1152]{1,0:T(8,128)(2,1)S(1)} %constant_dynamic-update-slice_fusion), channel_id=1, source_target_pairs={{0,24},{1,25},{2,26},{3,27},{4,28},{5,29},{6,30},{7,31},{8,0},{9,1... | collective-permute-start | bytes 221192 | tf_op jit(solution)/shard_map/ppermute | solution.py:418
  9.5 1.0 collective-permute-start
  10.5 1.7 collective-permute-done.2
  12.2 4.3 %collective-permute-done.1 = bf16[32,1152]{1,0:T(8,128)(2,1)S(1)} collective-permute-done((bf16[32,1152]{1,0:T(8,128)(2,1)S(1)}, bf16[32,1152]{1,0:T(8,128)(2,1)S(1)}, u32[]{:S(2)}, u32[]{:S(2)}) %collective-permute-start.1) | collective-permute-done | bytes 73760 | tf_op jit(solution)/shard_map/ppermute | solution.py:418
  16.5 2.5 %collective-permute-start.5 = (bf16[128,1152]{1,0:T(8,128)(2,1)S(1)}, bf16[128,1152]{1,0:T(8,128)(2,1)S(1)}, u32[]{:S(2)}, u32[]{:S(2)}) collective-permute-start(bf16[128,1152]{1,0:T(8,128)(2,1)S(1)} %pad_maximum_fusion.1.refs_1_), channel_id=1, source_target_pairs={{0,5},{1,4},{2,7},{3,6},{4,1},{5,0},{6,3},{7,2},{8,13},{9,12},{10,... | collective-permute-start | bytes 884744 | tf_op jit(solution)/shard_map/ppermute | solution.py:418
  19.0 0.5 collective-permute-start.4
  19.5 0.5 collective-permute-start.3
  20.1 0.9 pad_maximum_fusion.2
  20.9 2.0 collective-permute-start.12
  23.0 3.7 %collective-permute-done.12 = bf16[32,2048]{1,0:T(8,128)(2,1)S(1)} collective-permute-done((bf16[32,2048]{1,0:T(8,128)(2,1)S(1)}, bf16[32,2048]{1,0:T(8,128)(2,1)S(1)}, u32[]{:S(2)}, u32[]{:S(2)}) %collective-permute-start.12) | collective-permute-done | bytes 131104 | tf_op jit(solution)/shard_map/ppermute | solution.py:418
  26.7 3.1 %collective-permute-start.10 = (bf16[32,2048]{1,0:T(8,128)(2,1)S(1)}, bf16[32,2048]{1,0:T(8,128)(2,1)S(1)}, u32[]{:S(2)}, u32[]{:S(2)}) collective-permute-start(bf16[32,2048]{1,0:T(8,128)(2,1)S(1)} %pad_maximum_fusion.2), channel_id=1, source_target_pairs={{0,8},{1,9},{2,10},{3,11},{4,12},{5,13},{6,14},{7,15},{8,16},{9,17... | collective-permute-start | bytes 393224 | tf_op jit(solution)/shard_map/ppermute | solution.py:418
  29.9 2.3 collective-permute-done.11
  32.1 0.5 collective-permute-start.9
  32.7 0.4 collective-permute-start.7
  33.2 1.3 dynamic_slice.3.frames
  34.4 0.6 stack.34.place
  35.1 2.5 %collective-permute-start.15 = (bf16[128,2048]{1,0:T(8,128)(2,1)S(1)}, bf16[128,2048]{1,0:T(8,128)(2,1)S(1)}, u32[]{:S(2)}, u32[]{:S(2)}) collective-permute-start(bf16[128,2048]{1,0:T(8,128)(2,1)S(1)} %pad_maximum_fusion.refs_4_), channel_id=1, source_target_pairs={{0,5},{1,4},{2,7},{3,6},{4,1},{5,0},{6,3},{7,2},{8,13},{9,12},{10,... | collective-permute-start | bytes 1572872 | tf_op jit(solution)/shard_map/ppermute | solution.py:418
  37.6 0.5 collective-permute-start.14
  38.1 0.5 collective-permute-start.13
  38.7 0.1 copy-done.14
  38.8 30.1 %attn_forward.1 = (bf16[4608,512]{1,0:T(8,128)(2,1)}, bf16[4608,512]{1,0:T(8,128)(2,1)}, bf16[4608,512]{1,0:T(8,128)(2,1)}, bf16[4608,512]{1,0:T(8,128)(2,1)}, b...) custom-call(s32[5]{0:T(128)} %stack.34.place, ...), custom_call_target="tpu_custom_call" | custom-call | flops 28991029248 | bytes 42467328 | tf_op jit(solution)/shard_map/attn_forward/pallas_call | solution.py:322
  69.1 0.5 collective-permute-start.17
  69.7 0.4 collective-permute-start.19
  70.8 0.1 collective-permute-done.16.refs_8_
  70.9 0.7 collective-permute-done.17.refs_9_
  71.7 0.7 collective-permute-done.18.refs_10_
  72.4 0.7 collective-permute-done.19.refs_11_
  73.2 0.8 copy-done.9
  74.0 78.6 %feed_forward.1 = (bf16[4608,512]{1,0:T(8,128)(2,1)}, f32[4608,512]{1,0:T(8,128)}, bf16[4,4,32,2304]{3,2,1,0:T(8,128)(2,1)}, bf16[4,4,32,2304]{3,2,1,0:T(8,128)(2,1)}, f32[2,512]{1,0:T(2,128)}) custom-call(s32[5]{0:T(128)} %stack.34.place, s32[1]{0:T(128)S(6)} %sub.16.live, f32[4608,512]{1,0:T(8,128)} %get-tuple-element.37.refs_0_, ...), custom_call_target="tpu_custom_call" | custom-call | flops 57982058496 | bytes 28311552 | tf_op jit(solution)/shard_map/feed_forward/pallas_call | solution.py:342
  152.6 0.2 collective-permute-start.20
  152.8 4.6 %collective-permute-done.20 = bf16[4,4,32,2304]{3,2,1,0:T(8,128)(2,1)S(1)} collective-permute-done((bf16[4,4,32,2304]{3,2,1,0:T(8,128)(2,1)}, bf16[4,4,32,2304]{3,2,1,0:T(8,128)(2,1)S(1)}, u32[]{:S(2)}, u32[]{:S(2)}) %collective-permute-start.20) | collective-permute-done | bytes 2359328 | tf_op jit(solution)/shard_map/ppermute | solution.py:418
  157.4 2.3 add_convert_fusion
  159.8 1.4 collective-permute-start.25
  161.2 1.6 collective-permute-start.27
  162.8 0.5 collective-permute-start.26
  163.3 44.9 %attn_backward.1 = (f32[4608,512]{1,0:T(8,128)}, bf16[4,4,32,896]{3,2,1,0:T(8,128)(2,1)}, bf16[4,4,32,896]{3,2,1,0:T(8,128)(2,1)}) custom-call(s32[5]{0:T(128)} %stack.34.place, bf16[4608,512]{1,0:T(8,128)(2,1)} %x_ref.1, f32[4608,512]{1,0:T(8,128)} %get-tuple-element.50.gh_ref, bf16[4608,512]{1,0:T(8,128)(2,1)} %get-tuple-element.51.q_ref, ...), custom_call_target="tpu_custom_call" | custom-call | flops 43486543872 | bytes 42467328 | tf_op jit(solution)/shard_map/attn_backward/pallas_call | solution.py:377
  208.4 1.8 fusion.1
  210.2 0.9 collective-permute-done.21
  211.0 0.2 add_convert_fusion.1
  211.3 2.0 collective-permute-start.30
  213.4 1.4 collective-permute-start.28
  214.8 1.4 collective-permute-start.22
  216.2 1.5 collective-permute-start.24
  217.7 0.3 collective-permute-done.30
  218.0 1.6 collective-permute-start.23
  219.7 6.7 %collective-permute-done.29 = bf16[32,2304]{1,0:T(8,128)(2,1)S(1)} collective-permute-done((bf16[32,2304]{1,0:T(8,128)(2,1)S(1)}, bf16[32,2304]{1,0:T(8,128)(2,1)S(1)}, u32[]{:S(2)}, u32[]{:S(2)}) %collective-permute-start.29) | collective-permute-done | bytes 147488 | tf_op jit(solution)/shard_map/ppermute | solution.py:418
  226.4 0.7 slice_bitcast_fusion.11
  227.1 0.4 collective-permute-done.24
  227.5 1.5 collective-permute-done.23
  229.0 0.1 fusion.3
  229.1 2.2 collective-permute-start.31
  231.3 1.8 collective-permute-start.33
  233.1 0.5 collective-permute-start.32
  233.6 0.6 slice_bitcast_fusion.15
  234.2 1.4 collective-permute-done.31
  235.6 0.8 collective-permute-done.33
  236.5 2.0 collective-permute-done.32
  238.5 0.7 slice_reduce_fusion
  239.3 0.6 fusion.8
  (63 shorter events, 0.9 us)
Async XLA Ops:
  4.4 7.8 %collective-permute-start.2 = (bf16[32,1152]{1,0:T(8,128)(2,1)S(1)}, bf16[32,1152]{1,0:T(8,128)(2,1)S(1)}, u32[]{:S(2)}, u32[]{:S(2)}) collective-permute-start(bf16[32,1152]{1,0:T(8,128)(2,1)S(1)} %constant_dynamic-update-slice_fusion), channel_id=1, source_target_pairs={{0,24},{1,25},{2,26},{3,27},{4,28},{5,29},{6,30},{7,31},{8,0},{9,1... | collective-permute-start | bytes 221192 | tf_op jit(solution)/shard_map/ppermute | solution.py:418
  9.5 7.0 %collective-permute-start.1 = (bf16[32,1152]{1,0:T(8,128)(2,1)S(1)}, bf16[32,1152]{1,0:T(8,128)(2,1)S(1)}, u32[]{:S(2)}, u32[]{:S(2)}) collective-permute-start(bf16[32,1152]{1,0:T(8,128)(2,1)S(1)} %constant_dynamic-update-slice_fusion), channel_id=1, source_target_pairs={{0,16},{1,17},{2,18},{3,19},{4,20},{5,21},{6,22},{7,23},{8,24},{9,... | collective-permute-start | bytes 221192 | tf_op jit(solution)/shard_map/ppermute | solution.py:418
  9.5 7.0 %collective-permute-start = (bf16[32,1152]{1,0:T(8,128)(2,1)S(1)}, bf16[32,1152]{1,0:T(8,128)(2,1)S(1)}, u32[]{:S(2)}, u32[]{:S(2)}) collective-permute-start(bf16[32,1152]{1,0:T(8,128)(2,1)S(1)} %constant_dynamic-update-slice_fusion), channel_id=1, source_target_pairs={{0,8},{1,9},{2,10},{3,11},{4,12},{5,13},{6,14},{7,15},{8,16},{9,17... | collective-permute-start | bytes 221192 | tf_op jit(solution)/shard_map/ppermute | solution.py:418
  16.5 22.2 %copy-start.2 = (bf16[128,1152]{1,0:T(8,128)(2,1)}, bf16[128,1152]{1,0:T(8,128)(2,1)S(1)}, u32[]{:S(2)}) copy-start(bf16[128,1152]{1,0:T(8,128)(2,1)S(1)} %pad_maximum_fusion.1.refs_1_) | copy-start | bytes 884740
  16.5 15.6 %collective-permute-start.5 = (bf16[128,1152]{1,0:T(8,128)(2,1)S(1)}, bf16[128,1152]{1,0:T(8,128)(2,1)S(1)}, u32[]{:S(2)}, u32[]{:S(2)}) collective-permute-start(bf16[128,1152]{1,0:T(8,128)(2,1)S(1)} %pad_maximum_fusion.1.refs_1_), channel_id=1, source_target_pairs={{0,5},{1,4},{2,7},{3,6},{4,1},{5,0},{6,3},{7,2},{8,13},{9,12},{10,... | collective-permute-start | bytes 884744 | tf_op jit(solution)/shard_map/ppermute | solution.py:418
  19.0 13.6 %collective-permute-start.4 = (bf16[128,1152]{1,0:T(8,128)(2,1)S(1)}, bf16[128,1152]{1,0:T(8,128)(2,1)S(1)}, u32[]{:S(2)}, u32[]{:S(2)}) collective-permute-start(bf16[128,1152]{1,0:T(8,128)(2,1)S(1)} %pad_maximum_fusion.1.refs_1_), channel_id=1, source_target_pairs={{0,1},{1,0},{2,3},{3,2},{4,5},{5,4},{6,7},{7,6},{8,9},{9,8},{10,11... | collective-permute-start | bytes 884744 | tf_op jit(solution)/shard_map/ppermute | solution.py:418
  19.5 13.2 %collective-permute-start.3 = (bf16[128,1152]{1,0:T(8,128)(2,1)S(1)}, bf16[128,1152]{1,0:T(8,128)(2,1)S(1)}, u32[]{:S(2)}, u32[]{:S(2)}) collective-permute-start(bf16[128,1152]{1,0:T(8,128)(2,1)S(1)} %pad_maximum_fusion.1.refs_1_), channel_id=1, source_target_pairs={{0,4},{1,5},{2,6},{3,7},{4,0},{5,1},{6,2},{7,3},{8,12},{9,13},{10,... | collective-permute-start | bytes 884744 | tf_op jit(solution)/shard_map/ppermute | solution.py:418
  20.9 5.8 %collective-permute-start.12 = (bf16[32,2048]{1,0:T(8,128)(2,1)S(1)}, bf16[32,2048]{1,0:T(8,128)(2,1)S(1)}, u32[]{:S(2)}, u32[]{:S(2)}) collective-permute-start(bf16[32,2048]{1,0:T(8,128)(2,1)S(1)} %pad_maximum_fusion.2), channel_id=1, source_target_pairs={{0,24},{1,25},{2,26},{3,27},{4,28},{5,29},{6,30},{7,31},{8,0},{9,1... | collective-permute-start | bytes 393224 | tf_op jit(solution)/shard_map/ppermute | solution.py:418
  23.0 9.1 %collective-permute-start.11 = (bf16[32,2048]{1,0:T(8,128)(2,1)S(1)}, bf16[32,2048]{1,0:T(8,128)(2,1)S(1)}, u32[]{:S(2)}, u32[]{:S(2)}) collective-permute-start(bf16[32,2048]{1,0:T(8,128)(2,1)S(1)} %pad_maximum_fusion.2), channel_id=1, source_target_pairs={{0,16},{1,17},{2,18},{3,19},{4,20},{5,21},{6,22},{7,23},{8,24},{9,... | collective-permute-start | bytes 393224 | tf_op jit(solution)/shard_map/ppermute | solution.py:418
  26.7 8.3 %collective-permute-start.10 = (bf16[32,2048]{1,0:T(8,128)(2,1)S(1)}, bf16[32,2048]{1,0:T(8,128)(2,1)S(1)}, u32[]{:S(2)}, u32[]{:S(2)}) collective-permute-start(bf16[32,2048]{1,0:T(8,128)(2,1)S(1)} %pad_maximum_fusion.2), channel_id=1, source_target_pairs={{0,8},{1,9},{2,10},{3,11},{4,12},{5,13},{6,14},{7,15},{8,16},{9,17... | collective-permute-start | bytes 393224 | tf_op jit(solution)/shard_map/ppermute | solution.py:418
  32.1 5.5 %collective-permute-start.6 = (bf16[128,1152]{1,0:T(8,128)(2,1)S(1)}, bf16[128,1152]{1,0:T(8,128)(2,1)S(1)}, u32[]{:S(2)}, u32[]{:S(2)}) collective-permute-start(bf16[128,1152]{1,0:T(8,128)(2,1)S(1)} %pad_maximum_fusion.1.refs_1_), channel_id=1, source_target_pairs={{0,2},{1,3},{2,0},{3,1},{4,6},{5,7},{6,4},{7,5},{8,10},{9,11},{10,... | collective-permute-start | bytes 884744 | tf_op jit(solution)/shard_map/ppermute | solution.py:418
  32.1 6.5 %copy-start.10 = (bf16[128,1152]{1,0:T(8,128)(2,1)}, bf16[128,1152]{1,0:T(8,128)(2,1)S(1)}, u32[]{:S(2)}) copy-start(bf16[128,1152]{1,0:T(8,128)(2,1)S(1)} %collective-permute-done.5.refs_4_) | copy-start | bytes 884740
  32.1 6.0 %collective-permute-start.9 = (bf16[128,1152]{1,0:T(8,128)(2,1)S(1)}, bf16[128,1152]{1,0:T(8,128)(2,1)S(1)}, u32[]{:S(2)}, u32[]{:S(2)}) collective-permute-start(bf16[128,1152]{1,0:T(8,128)(2,1)S(1)} %collective-permute-done.5.refs_4_), channel_id=1, source_target_pairs={{0,2},{1,3},{2,0},{3,1},{4,6},{5,7},{6,4},{7,5},{8,10},{9,11},{10,... | collective-permute-start | bytes 884744 | tf_op jit(solution)/shard_map/ppermute | solution.py:418
  32.6 6.0 %copy-start.11 = (bf16[128,1152]{1,0:T(8,128)(2,1)}, bf16[128,1152]{1,0:T(8,128)(2,1)S(1)}, u32[]{:S(2)}) copy-start(bf16[128,1152]{1,0:T(8,128)(2,1)S(1)} %collective-permute-done.4.refs_3_) | copy-start | bytes 884740
  32.6 6.0 %collective-permute-start.8 = (bf16[128,1152]{1,0:T(8,128)(2,1)S(1)}, bf16[128,1152]{1,0:T(8,128)(2,1)}, u32[]{:S(2)}, u32[]{:S(2)}) collective-permute-start(bf16[128,1152]{1,0:T(8,128)(2,1)S(1)} %collective-permute-done.4.refs_3_), channel_id=1, source_target_pairs={{0,2},{1,3},{2,0},{3,1},{4,6},{5,7},{6,4},{7,5},{8,10},{9,11},{10,... | collective-permute-start | bytes 884744 | tf_op jit(solution)/shard_map/ppermute | solution.py:418
  32.7 5.9 %copy-start.12 = (bf16[128,1152]{1,0:T(8,128)(2,1)}, bf16[128,1152]{1,0:T(8,128)(2,1)S(1)}, u32[]{:S(2)}) copy-start(bf16[128,1152]{1,0:T(8,128)(2,1)S(1)} %collective-permute-done.3.refs_2_) | copy-start | bytes 884740
  32.7 5.9 %collective-permute-start.7 = (bf16[128,1152]{1,0:T(8,128)(2,1)S(1)}, bf16[128,1152]{1,0:T(8,128)(2,1)}, u32[]{:S(2)}, u32[]{:S(2)}) collective-permute-start(bf16[128,1152]{1,0:T(8,128)(2,1)S(1)} %collective-permute-done.3.refs_2_), channel_id=1, source_target_pairs={{0,2},{1,3},{2,0},{3,1},{4,6},{5,7},{6,4},{7,5},{8,10},{9,11},{10,... | collective-permute-start | bytes 884744 | tf_op jit(solution)/shard_map/ppermute | solution.py:418
  35.1 33.9 %copy-start.1 = (bf16[128,2048]{1,0:T(8,128)(2,1)}, bf16[128,2048]{1,0:T(8,128)(2,1)S(1)}, u32[]{:S(2)}) copy-start(bf16[128,2048]{1,0:T(8,128)(2,1)S(1)} %pad_maximum_fusion.refs_4_) | copy-start | bytes 1572868
  35.1 33.9 %collective-permute-start.15 = (bf16[128,2048]{1,0:T(8,128)(2,1)S(1)}, bf16[128,2048]{1,0:T(8,128)(2,1)S(1)}, u32[]{:S(2)}, u32[]{:S(2)}) collective-permute-start(bf16[128,2048]{1,0:T(8,128)(2,1)S(1)} %pad_maximum_fusion.refs_4_), channel_id=1, source_target_pairs={{0,5},{1,4},{2,7},{3,6},{4,1},{5,0},{6,3},{7,2},{8,13},{9,12},{10,... | collective-permute-start | bytes 1572872 | tf_op jit(solution)/shard_map/ppermute | solution.py:418
  37.6 1.1 copy-start.13
  37.6 31.4 %collective-permute-start.14 = (bf16[128,2048]{1,0:T(8,128)(2,1)S(1)}, bf16[128,2048]{1,0:T(8,128)(2,1)S(1)}, u32[]{:S(2)}, u32[]{:S(2)}) collective-permute-start(bf16[128,2048]{1,0:T(8,128)(2,1)S(1)} %pad_maximum_fusion.refs_4_), channel_id=1, source_target_pairs={{0,1},{1,0},{2,3},{3,2},{4,5},{5,4},{6,7},{7,6},{8,9},{9,8},{10,11... | collective-permute-start | bytes 1572872 | tf_op jit(solution)/shard_map/ppermute | solution.py:418
  38.1 0.7 copy-start.14
  38.1 31.0 %collective-permute-start.13 = (bf16[128,2048]{1,0:T(8,128)(2,1)S(1)}, bf16[128,2048]{1,0:T(8,128)(2,1)S(1)}, u32[]{:S(2)}, u32[]{:S(2)}) collective-permute-start(bf16[128,2048]{1,0:T(8,128)(2,1)S(1)} %pad_maximum_fusion.refs_4_), channel_id=1, source_target_pairs={{0,4},{1,5},{2,6},{3,7},{4,0},{5,1},{6,2},{7,3},{8,12},{9,13},{10,... | collective-permute-start | bytes 1572872 | tf_op jit(solution)/shard_map/ppermute | solution.py:418
  68.9 2.0 collective-permute-start.16
  69.0 4.9 %copy-start.3 = (bf16[128,2048]{1,0:T(8,128)(2,1)}, bf16[128,2048]{1,0:T(8,128)(2,1)S(1)}, u32[]{:S(2)}) copy-start(bf16[128,2048]{1,0:T(8,128)(2,1)S(1)} %collective-permute-done.15.refs_7_) | copy-start | bytes 1572868
  69.0 4.9 %copy-start.4 = (bf16[128,2048]{1,0:T(8,128)(2,1)}, bf16[128,2048]{1,0:T(8,128)(2,1)S(1)}, u32[]{:S(2)}) copy-start(bf16[128,2048]{1,0:T(8,128)(2,1)S(1)} %collective-permute-done.14.refs_6_) | copy-start | bytes 1572868
  69.1 4.9 %copy-start.5 = (bf16[128,2048]{1,0:T(8,128)(2,1)}, bf16[128,2048]{1,0:T(8,128)(2,1)S(1)}, u32[]{:S(2)}) copy-start(bf16[128,2048]{1,0:T(8,128)(2,1)S(1)} %collective-permute-done.13.refs_5_) | copy-start | bytes 1572868
  69.1 2.6 %collective-permute-start.17 = (bf16[128,2048]{1,0:T(8,128)(2,1)S(1)}, bf16[128,2048]{1,0:T(8,128)(2,1)S(1)}, u32[]{:S(2)}, u32[]{:S(2)}) collective-permute-start(bf16[128,2048]{1,0:T(8,128)(2,1)S(1)} %collective-permute-done.13.refs_5_), channel_id=1, source_target_pairs={{0,2},{1,3},{2,0},{3,1},{4,6},{5,7},{6,4},{7,5},{8,10},{9,11},{10,... | collective-permute-start | bytes 1572872 | tf_op jit(solution)/shard_map/ppermute | solution.py:418
  69.6 2.8 %collective-permute-start.18 = (bf16[128,2048]{1,0:T(8,128)(2,1)S(1)}, bf16[128,2048]{1,0:T(8,128)(2,1)S(1)}, u32[]{:S(2)}, u32[]{:S(2)}) collective-permute-start(bf16[128,2048]{1,0:T(8,128)(2,1)S(1)} %collective-permute-done.14.refs_6_), channel_id=1, source_target_pairs={{0,2},{1,3},{2,0},{3,1},{4,6},{5,7},{6,4},{7,5},{8,10},{9,11},{10,... | collective-permute-start | bytes 1572872 | tf_op jit(solution)/shard_map/ppermute | solution.py:418
  69.7 3.5 %collective-permute-start.19 = (bf16[128,2048]{1,0:T(8,128)(2,1)S(1)}, bf16[128,2048]{1,0:T(8,128)(2,1)S(1)}, u32[]{:S(2)}, u32[]{:S(2)}) collective-permute-start(bf16[128,2048]{1,0:T(8,128)(2,1)S(1)} %collective-permute-done.15.refs_7_), channel_id=1, source_target_pairs={{0,2},{1,3},{2,0},{3,1},{4,6},{5,7},{6,4},{7,5},{8,10},{9,11},{10,... | collective-permute-start | bytes 1572872 | tf_op jit(solution)/shard_map/ppermute | solution.py:418
  70.9 3.1 %copy-start.6 = (bf16[128,2048]{1,0:T(8,128)(2,1)}, bf16[128,2048]{1,0:T(8,128)(2,1)S(1)}, u32[]{:S(2)}) copy-start(bf16[128,2048]{1,0:T(8,128)(2,1)S(1)} %collective-permute-done.16.refs_8_) | copy-start | bytes 1572868
  71.7 2.3 copy-start.7
  72.4 1.6 copy-start.8
  73.2 0.8 copy-start.9
  152.6 4.8 %collective-permute-start.20 = (bf16[4,4,32,2304]{3,2,1,0:T(8,128)(2,1)}, bf16[4,4,32,2304]{3,2,1,0:T(8,128)(2,1)S(1)}, u32[]{:S(2)}, u32[]{:S(2)}) collective-permute-start(bf16[4,4,32,2304]{3,2,1,0:T(8,128)(2,1)} %get-tuple-element.49), channel_id=1, source_target_pairs={{0,2},{1,3},{2,0},{3,1},{4,6},{5,7},{6,4},{7,5},{8,10},{9,11},{10,... | collective-permute-start | bytes 7077896 | tf_op jit(solution)/shard_map/ppermute | solution.py:418
  159.8 48.6 %collective-permute-start.25 = (bf16[4,32,2304]{2,1,0:T(8,128)(2,1)S(1)}, bf16[4,32,2304]{2,1,0:T(8,128)(2,1)}, u32[]{:S(2)}, u32[]{:S(2)}) collective-permute-start(bf16[4,32,2304]{2,1,0:T(8,128)(2,1)S(1)} %get-tuple-element.66), channel_id=1, source_target_pairs={{0,4},{1,5},{2,6},{3,7},{4,0},{5,1},{6,2},{7,3},{8,12},{9,13},{10,... | collective-permute-start | bytes 1769480 | tf_op jit(solution)/shard_map/ppermute | solution.py:418
  161.2 47.2 %collective-permute-start.27 = (bf16[4,32,2304]{2,1,0:T(8,128)(2,1)S(1)}, bf16[4,32,2304]{2,1,0:T(8,128)(2,1)}, u32[]{:S(2)}, u32[]{:S(2)}) collective-permute-start(bf16[4,32,2304]{2,1,0:T(8,128)(2,1)S(1)} %get-tuple-element.67), channel_id=1, source_target_pairs={{0,5},{1,4},{2,7},{3,6},{4,1},{5,0},{6,3},{7,2},{8,13},{9,12},{10,... | collective-permute-start | bytes 1769480 | tf_op jit(solution)/shard_map/ppermute | solution.py:418
  162.8 45.6 %collective-permute-start.26 = (bf16[4,32,2304]{2,1,0:T(8,128)(2,1)S(1)}, bf16[4,32,2304]{2,1,0:T(8,128)(2,1)}, u32[]{:S(2)}, u32[]{:S(2)}) collective-permute-start(bf16[4,32,2304]{2,1,0:T(8,128)(2,1)S(1)} %get-tuple-element.68), channel_id=1, source_target_pairs={{0,1},{1,0},{2,3},{3,2},{4,5},{5,4},{6,7},{7,6},{8,9},{9,8},{10,11... | collective-permute-start | bytes 1769480 | tf_op jit(solution)/shard_map/ppermute | solution.py:418
  208.3 2.8 %copy-start = (bf16[4,4,32,896]{3,2,1,0:T(8,128)(2,1)S(1)}, bf16[4,4,32,896]{3,2,1,0:T(8,128)(2,1)}, u32[]{:S(2)}) copy-start(bf16[4,4,32,896]{3,2,1,0:T(8,128)(2,1)} %get-tuple-element.58) | copy-start | bytes 2752516
  208.3 2.7 %collective-permute-start.21 = (bf16[4,4,32,896]{3,2,1,0:T(8,128)(2,1)}, bf16[4,4,32,896]{3,2,1,0:T(8,128)(2,1)S(1)}, u32[]{:S(2)}, u32[]{:S(2)}) collective-permute-start(bf16[4,4,32,896]{3,2,1,0:T(8,128)(2,1)} %get-tuple-element.59), channel_id=1, source_target_pairs={{0,2},{1,3},{2,0},{3,1},{4,6},{5,7},{6,4},{7,5},{8,10},{9,11},{10,... | collective-permute-start | bytes 2752520 | tf_op jit(solution)/shard_map/ppermute | solution.py:418
  211.3 6.7 %collective-permute-start.30 = (bf16[32,2304]{1,0:T(8,128)(2,1)S(1)}, bf16[32,2304]{1,0:T(8,128)(2,1)S(1)}, u32[]{:S(2)}, u32[]{:S(2)}) collective-permute-start(bf16[32,2304]{1,0:T(8,128)(2,1)S(1)} %get-tuple-element.72), channel_id=1, source_target_pairs={{0,24},{1,25},{2,26},{3,27},{4,28},{5,29},{6,30},{7,31},{8,0},{9,1... | collective-permute-start | bytes 442376 | tf_op jit(solution)/shard_map/ppermute | solution.py:418
  213.4 13.0 %collective-permute-start.29 = (bf16[32,2304]{1,0:T(8,128)(2,1)S(1)}, bf16[32,2304]{1,0:T(8,128)(2,1)S(1)}, u32[]{:S(2)}, u32[]{:S(2)}) collective-permute-start(bf16[32,2304]{1,0:T(8,128)(2,1)S(1)} %get-tuple-element.73), channel_id=1, source_target_pairs={{0,16},{1,17},{2,18},{3,19},{4,20},{5,21},{6,22},{7,23},{8,24},{9,... | collective-permute-start | bytes 442376 | tf_op jit(solution)/shard_map/ppermute | solution.py:418
  213.4 13.0 %collective-permute-start.28 = (bf16[32,2304]{1,0:T(8,128)(2,1)S(1)}, bf16[32,2304]{1,0:T(8,128)(2,1)S(1)}, u32[]{:S(2)}, u32[]{:S(2)}) collective-permute-start(bf16[32,2304]{1,0:T(8,128)(2,1)S(1)} %get-tuple-element.74), channel_id=1, source_target_pairs={{0,8},{1,9},{2,10},{3,11},{4,12},{5,13},{6,14},{7,15},{8,16},{9,17... | collective-permute-start | bytes 442376 | tf_op jit(solution)/shard_map/ppermute | solution.py:418
  214.8 12.3 %collective-permute-start.22 = (bf16[4,32,896]{2,1,0:T(8,128)(2,1)S(1)}, bf16[4,32,896]{2,1,0:T(8,128)(2,1)S(1)}, u32[]{:S(2)}, u32[]{:S(2)}) collective-permute-start(bf16[4,32,896]{2,1,0:T(8,128)(2,1)S(1)} %get-tuple-element.69), channel_id=1, source_target_pairs={{0,4},{1,5},{2,6},{3,7},{4,0},{5,1},{6,2},{7,3},{8,12},{9,13},{10,... | collective-permute-start | bytes 688136 | tf_op jit(solution)/shard_map/ppermute | solution.py:418
  216.2 11.3 %collective-permute-start.24 = (bf16[4,32,896]{2,1,0:T(8,128)(2,1)S(1)}, bf16[4,32,896]{2,1,0:T(8,128)(2,1)S(1)}, u32[]{:S(2)}, u32[]{:S(2)}) collective-permute-start(bf16[4,32,896]{2,1,0:T(8,128)(2,1)S(1)} %get-tuple-element.70), channel_id=1, source_target_pairs={{0,5},{1,4},{2,7},{3,6},{4,1},{5,0},{6,3},{7,2},{8,13},{9,12},{10,... | collective-permute-start | bytes 688136 | tf_op jit(solution)/shard_map/ppermute | solution.py:418
  218.0 10.9 %collective-permute-start.23 = (bf16[4,32,896]{2,1,0:T(8,128)(2,1)S(1)}, bf16[4,32,896]{2,1,0:T(8,128)(2,1)S(1)}, u32[]{:S(2)}, u32[]{:S(2)}) collective-permute-start(bf16[4,32,896]{2,1,0:T(8,128)(2,1)S(1)} %get-tuple-element.71), channel_id=1, source_target_pairs={{0,1},{1,0},{2,3},{3,2},{4,5},{5,4},{6,7},{7,6},{8,9},{9,8},{10,11... | collective-permute-start | bytes 688136 | tf_op jit(solution)/shard_map/ppermute | solution.py:418
  229.1 6.5 %collective-permute-start.31 = (bf16[32,896]{1,0:T(8,128)(2,1)S(1)}, bf16[32,896]{1,0:T(8,128)(2,1)S(1)}, u32[]{:S(2)}, u32[]{:S(2)}) collective-permute-start(bf16[32,896]{1,0:T(8,128)(2,1)S(1)} %get-tuple-element.77), channel_id=1, source_target_pairs={{0,8},{1,9},{2,10},{3,11},{4,12},{5,13},{6,14},{7,15},{8,16},{9,17... | collective-permute-start | bytes 172040 | tf_op jit(solution)/shard_map/ppermute | solution.py:418
  231.3 5.1 %collective-permute-start.33 = (bf16[32,896]{1,0:T(8,128)(2,1)S(1)}, bf16[32,896]{1,0:T(8,128)(2,1)S(1)}, u32[]{:S(2)}, u32[]{:S(2)}) collective-permute-start(bf16[32,896]{1,0:T(8,128)(2,1)S(1)} %get-tuple-element.78), channel_id=1, source_target_pairs={{0,24},{1,25},{2,26},{3,27},{4,28},{5,29},{6,30},{7,31},{8,0},{9,1... | collective-permute-start | bytes 172040 | tf_op jit(solution)/shard_map/ppermute | solution.py:418
  233.1 5.4 %collective-permute-start.32 = (bf16[32,896]{1,0:T(8,128)(2,1)S(1)}, bf16[32,896]{1,0:T(8,128)(2,1)S(1)}, u32[]{:S(2)}, u32[]{:S(2)}) collective-permute-start(bf16[32,896]{1,0:T(8,128)(2,1)S(1)} %get-tuple-element.79), channel_id=1, source_target_pairs={{0,16},{1,17},{2,18},{3,19},{4,20},{5,21},{6,22},{7,23},{8,24},{9,... | collective-permute-start | bytes 172040 | tf_op jit(solution)/shard_map/ppermute | solution.py:418

commit v4 on v3

--- a/solution.py
+++ b/solution.py
@@ -68,6 +68,18 @@
     return jnp.where(lane < HEAD, product[:SEQ], product[HEAD : HEAD + SEQ])
 
 
+def head_rows(rows):
+    lane = lax.broadcasted_iota(jnp.int32, rows.shape, 1)
+    zero = jnp.zeros_like(rows)
+    return jnp.concatenate([jnp.where(lane < HEAD, rows, zero), jnp.where(lane < HEAD, zero, rows)], axis=0)
+
+
+def pair_scores(left, right):
+    right = jnp.concatenate([right, jnp.zeros((HEAD - SEQ, right.shape[1]), right.dtype)], axis=0)
+    both = nt(head_rows(left), right)
+    return jnp.concatenate([both[:SEQ], both[SEQ:]], axis=1)
+
+
 def seq_slice(s, c, width):
     return (slice(s * SEQ, (s + 1) * SEQ), slice(c * width, (c + 1) * width))
 
@@ -116,10 +128,22 @@
                     ref[slot, back, :, start : start + acc.shape[2]] = acc[m, rows, :].astype(BF)
 
 
+def pack_kernel(q_ref, k_ref, v_ref, o_ref, u_ref, d_ref, vec_ref, attn_ref, ff_ref):
+    at = 0
+    for ref in (q_ref, k_ref, v_ref, o_ref):
+        attn_ref[:, at : at + ref.shape[1]] = ref[...]
+        at += ref.shape[1]
+    vec = jnp.concatenate([vec_ref[...].astype(F32), jnp.zeros((GC - 4, vec_ref.shape[1]), F32)], axis=0)
+    attn_ref[:, at:] = vec.T.astype(BF)
+    ff_ref[:, : u_ref.shape[1]] = u_ref[...]
+    ff_ref[:, u_ref.shape[1] :] = d_ref[...]
+
+
 def attn_forward_kernel(place, frames, metas, x_ref, *refs):
     n = len(metas)
     pieces = refs[:n]
-    q_ref, k_ref, v_ref, p_ref, ho_ref, hidden_ref, vec_ref, w_ref, s_ref, sems = refs[n:]
+    qkvp_ref, ho_ref, hidden_ref, vec_ref, w_ref, s_ref, sems = refs[n:]
+    q_ref, k_ref, v_ref, p_ref = (qkvp_ref.at[:, i * D : (i + 1) * D] for i in range(4))
     step = pl.program_id(0)
     seqs = x_ref.shape[0] // SEQ
 
@@ -144,7 +168,7 @@
     key = lax.broadcasted_iota(jnp.int32, (SEQ, PAIR), 0)
     query = lax.broadcasted_iota(jnp.int32, (SEQ, PAIR), 1) % HEAD
     for s in range(seqs):
-        allowed = (key <= query) & (key < frames[step * seqs + s] * FTOK)
+        allowed = (key <= query) & (key < frames[place[5] + step * seqs + s] * FTOK)
         for c in range(D // PAIR):
             at = seq_slice(s, c, PAIR)
             scores = jnp.where(allowed, s_ref[at] * HEAD**-0.5, -1000000000.0)
@@ -185,7 +209,7 @@
     n, rstd = norm_parts(hidden)
     normed = (n * vec_ref[2:3] + vec_ref[3:4]).astype(BF)
     row = lax.broadcasted_iota(jnp.int32, (rows, 1), 0) + step * rows
-    go = jnp.where(row < live[0] * SEQ, cot_ref[...].astype(F32), 0.0)
+    go = jnp.where(row < (live[0] - place[5]) * SEQ, cot_ref[...].astype(F32), 0.0)
     go_ref[...] = go.astype(BF)
     for m in range(HALVES):
         for c in range(FW // CHUNK):
@@ -225,12 +249,13 @@
 
 
 def attn_backward_kernel(
-    place, x_ref, gh_ref, q_ref, k_ref, v_ref, p_ref, w_ref, vec_ref, gvtwo_ref,
+    place, x_ref, gh_ref, qkvp_ref, w_ref, vec_ref, gvtwo_ref,
     gi_ref, own_ref, other_ref, acc_ref, gvacc_ref, gvec_ref, s_ref, ds_ref, dh_ref, dqkv_ref,
 ):
     step = pl.program_id(0)
     last = pl.num_programs(0) - 1
     seqs = x_ref.shape[0] // SEQ
+    q_ref, k_ref, v_ref, p_ref = (qkvp_ref.at[:, i * D : (i + 1) * D] for i in range(4))
 
     @pl.when(step == 0)
     def _():
@@ -244,7 +269,9 @@
     for s in range(seqs):
         for c in range(D // PAIR):
             at = seq_slice(s, c, PAIR)
-            s_ref[at] = nt(v_ref[at], per_head(dh_ref[at]))
+            base = 3 * HW * (c * PAIR // HW) + c * PAIR % HW
+            s_ref[at] = pair_scores(v_ref[at], dh_ref[at])
+            dqkv_ref[at[0], base + 2 * HW : base + 2 * HW + PAIR] = nn(p_ref[at], per_head(dh_ref[at])).astype(BF)
     for s in range(seqs):
         for c in range(D // PAIR):
             at = seq_slice(s, c, PAIR)
@@ -256,12 +283,7 @@
         for c in range(D // PAIR):
             at = seq_slice(s, c, PAIR)
             base = 3 * HW * (c * PAIR // HW) + c * PAIR % HW
-            dqkv_ref[at[0], base + 2 * HW : base + 2 * HW + PAIR] = nn(p_ref[at], per_head(dh_ref[at])).astype(BF)
             dqkv_ref[at[0], base + HW : base + HW + PAIR] = nn(ds_ref[at], per_head(q_ref[at])).astype(BF)
-    for s in range(seqs):
-        for c in range(D // PAIR):
-            at = seq_slice(s, c, PAIR)
-            base = 3 * HW * (c * PAIR // HW) + c * PAIR % HW
             dqkv_ref[at[0], base : base + PAIR] = pair_blocks(tn(ds_ref[at], k_ref[at])).astype(BF)
     n, rstd = norm_parts(x_ref[...].astype(F32))
     normed = (n * vec_ref[0:1] + vec_ref[1:2]).astype(BF)
@@ -300,7 +322,10 @@
     return jax.ShapeDtypeStruct(dims, dtype)
 
 
-PARAMS = pltpu.CompilerParams(vmem_limit_bytes=60 * 1024 * 1024)
+def vmem(mib):
+    return pltpu.CompilerParams(vmem_limit_bytes=mib * 1024 * 1024)
+
+
 HBM = pl.BlockSpec(memory_space=pl.ANY)
 
 
@@ -314,6 +339,15 @@
 
 def cost(flops, nbytes):
     return pl.CostEstimate(flops=flops, bytes_accessed=nbytes, transcendentals=0)
+
+
+def pack(w_query, w_key, w_value, w_out, w_up, w_down, vec):
+    depth = w_query.shape[0]
+    return pl.pallas_call(
+        pack_kernel,
+        out_shape=[shape((depth, 4 * w_query.shape[1] + GC), BF), shape((depth, 2 * w_up.shape[1]), BF)],
+        name="pack",
+    )(w_query, w_key, w_value, w_out, w_up, w_down, vec)
 
 
 def attn_forward(place, frames, tokens, group):
@@ -325,11 +359,17 @@
             num_scalar_prefetch=2,
             grid=(rows // step_rows(rows),),
             in_specs=[row_block(rows, D)] + [HBM] * len(group[0]),
-            out_specs=[row_block(rows, D)] * 6 + [held((8, D)), held(dims)],
+            out_specs=[row_block(rows, 4 * D), row_block(rows, D), row_block(rows, D), held((8, D)), held(dims)],
             scratch_shapes=[pltpu.VMEM((step_rows(rows), D), F32), copy_sems(group)],
         ),
-        out_shape=[shape((rows, D), BF)] * 5 + [shape((rows, D), F32), shape((8, D), F32), shape(dims, BF)],
-        compiler_params=PARAMS,
+        out_shape=[
+            shape((rows, 4 * D), BF),
+            shape((rows, D), BF),
+            shape((rows, D), F32),
+            shape((8, D), F32),
+            shape(dims, BF),
+        ],
+        compiler_params=vmem(60),
         cost_estimate=cost(rows * D * D * 24, rows * D * 18),
         name="attn_forward",
     )(place, frames, tokens, *group[0])
@@ -365,13 +405,13 @@
             shape(grads, BF),
             shape((2, D), F32),
         ],
-        compiler_params=PARAMS,
+        compiler_params=vmem(54),
         cost_estimate=cost(rows * D * FF * 12, rows * D * 12),
         name="feed_forward",
     )(place, live, hidden, cotangent, ho, vec, *group[0])
 
 
-def attn_backward(place, tokens, gh, q, k, v, p, w, vec, gv_two, out_dims):
+def attn_backward(place, tokens, gh, qkvp, w, vec, gv_two, out_dims):
     rows = tokens.shape[0]
     grads = out_dims + (3 * HW + GC,)
     return pl.pallas_call(
@@ -379,7 +419,7 @@
         grid_spec=pltpu.PrefetchScalarGridSpec(
             num_scalar_prefetch=1,
             grid=(rows // step_rows(rows),),
-            in_specs=[row_block(rows, D)] * 6 + [held(w.shape), held((8, D)), held((2, D))],
+            in_specs=[row_block(rows, D)] * 2 + [row_block(rows, 4 * D), held(w.shape), held((8, D)), held((2, D))],
             out_specs=[row_block(rows, D), held(grads), held(grads)],
             scratch_shapes=[
                 pltpu.VMEM((HALVES, D, 3 * HW), F32),
@@ -392,10 +432,10 @@
             ],
         ),
         out_shape=[shape((rows, D), F32), shape(grads, BF), shape(grads, BF)],
-        compiler_params=PARAMS,
+        compiler_params=vmem(40),
         cost_estimate=cost(rows * D * D * 36, rows * D * 18),
         name="attn_backward",
-    )(place, tokens, gh, q, k, v, p, w, vec, gv_two)
+    )(place, tokens, gh, qkvp, w, vec, gv_two)
 
 
 def build(mesh):
@@ -435,15 +475,15 @@
     def after(value, *others):
         return lax.optimization_barrier((value,) + others)[0]
 
-    def gather_first(attn, ff):
+    def gather_first(attn, ff, place):
         attn_z = along_z(attn)
-        attn_plane = across_plane(stack(attn_z))
+        attn_plane = across_plane(after(stack(attn_z), place))
         ff_z = along_z(after(ff, attn_z[-1]))
         ff_plane = across_plane(after(stack(ff_z), attn_plane[-1]))
         return (both_cores(attn_plane), Z_FIRST), ff_plane
 
     def gather_last(ff_plane, done):
-        ff_plane = [after(piece, done) for piece in ff_plane]
+        ff_plane = ff_plane[:1] + [after(piece, done) for piece in ff_plane[1:]]
         return both_cores(ff_plane), Z_FIRST
 
     def gather_plain(block, parts):
@@ -462,7 +502,8 @@
         return [blocks[i] for i in range(8)], Z_FIRST
 
     def scatter_core(own, other):
-        return (own.astype(F32) + send(other, cr=1).astype(F32)).astype(BF)
+        got = send(other, cr=1)
+        return [(own[slot].astype(F32) + got[slot].astype(F32)).astype(BF) for slot in range(4)]
 
     def scatter_plane(mine):
         return mine[0], [send(mine[x + 2 * y], xr=x, yr=y) for x, y in PLANE[1:]]
@@ -502,38 +543,34 @@
         gain_one, shift_one, gain_two, shift_two,
     ):
         dp, mp = lax.axis_index("dp"), lax.axis_index("mp")
-        place = jnp.stack([dp // 4, (dp // 2) % 2, dp % 2, mp % HALVES, jnp.int32(n_z)]).astype(jnp.int32)
         seqs = tokens.shape[0] // SEQ
-        frames = lax.dynamic_slice(frame_count, (mp * seqs,), (seqs,))
-        live = live_count - mp * seqs
-        vec = jnp.stack([gain_one, shift_one, gain_two, shift_two], axis=1)
-        vec = jnp.pad(vec, ((0, 0), (0, GC - 4)))
-        attn = jnp.concatenate([w_query, w_key, w_value, w_out.T], axis=1)
-        ff = jnp.concatenate([w_up, w_down.T], axis=1)
+        place = jnp.stack([dp // 4, (dp // 2) % 2, dp % 2, mp % HALVES, jnp.int32(n_z), mp * seqs])
+        place = place.astype(jnp.int32)
+        vec = jnp.stack([gain_one, shift_one, gain_two, shift_two])
         out_dims = (4, n_z, depth)
         if staged:
-            attn, ff = gather_first(jnp.concatenate([attn, vec], axis=1), ff)
+            attn, ff = gather_first(*pack(w_query, w_key, w_value, w_out.T, w_up, w_down.T, vec), place)
         else:
-            vec = lax.all_gather(vec, "dp", axis=0, tiled=True)
-            attn = jnp.concatenate([gather_plain(attn, 4), jnp.concatenate([vec] * HALVES)], axis=1)
-            attn = plain_pieces(attn)
-            ff = plain_pieces(gather_plain(ff, 2))
-        q, k, v, p, ho, hidden, vec, wa = attn_forward(place, frames, tokens, attn)
+            vec = lax.all_gather(jnp.pad(vec.T, ((0, 0), (0, GC - 4))), "dp", axis=0, tiled=True)
+            attn = gather_plain(jnp.concatenate([w_query, w_key, w_value, w_out.T], axis=1), 4)
+            attn = plain_pieces(jnp.concatenate([attn, jnp.concatenate([vec] * HALVES)], axis=1))
+            ff = plain_pieces(gather_plain(jnp.concatenate([w_up, w_down.T], axis=1), 2))
+        qkvp, ho, hidden, vec, wa = attn_forward(place, frame_count, tokens, attn)
         if staged:
             ff = gather_last(ff, vec)
         mixed, gh, f_own, f_other, gv_two = feed_forward(
-            place, live, hidden, cotangent, ho, vec, ff, out_dims
+            place, live_count, hidden, cotangent, ho, vec, ff, out_dims
         )
         if staged:
             f_mine = scatter_core(f_own, f_other)
-            gh = after(gh, f_mine)
+            gh = after(gh, *f_mine[1:])
             f_mine, f_got = scatter_plane(f_mine)
         grad_input, a_own, a_other = attn_backward(
-            place, tokens, gh, q, k, v, p, wa, vec, gv_two, out_dims
+            place, tokens, gh, qkvp, wa, vec, gv_two, out_dims
         )
         if staged:
             a_mine = scatter_core(a_own, a_other)
-            f_mine = after(scatter_add(f_mine, f_got), a_mine)
+            f_mine = after(scatter_add(f_mine, f_got), *a_mine[1:])
             f_mine, f_got = scatter_z(f_mine)
             a_mine, a_got = scatter_plane(a_mine)
             a_mine = after(scatter_add(a_mine, a_got), *f_got)

time: 241 us -> 232 us (0.963)
  Pallas kernels: 154 us -> 148 us
  local copies, waits for them, and re-layouts: 8.77 us -> 4.19 us
    pallas_call x1, Pallas kernels: 44.9 us -> 36.9 us  [attn_backward(): pl.pallas_call(attn_backward_kernel, grid_spec=pltpu.PrefetchScalarGridSp...]
    unnamed x34 -> x36, local copies, waits for them, and re-layouts: 3.86 us -> 0.83 us
  transfers between devices with their start and end apart: 34 -> 34, of which waited for: 17 -> 16; matrix products, arithmetic and copies ran while one was open for 3% -> 2% of each run, Pallas kernels for 31% -> 29%
where the time goes in v4:
time: 232 us; the launch traced here: 231 us
  Pallas kernels  148 us (64%)
  starting transfers between devices  36 us (16%)
  waiting for transfers between devices  34 us (15%)
  other arithmetic  7.01 us (3%)
  local copies, waits for them, and re-layouts  4.19 us (2%)
    pallas_call x1, Pallas kernels, feed_forward(): pl.pallas_call(lambda place, live, *refs: feed_forward_kernel(place, live...  78.9 us
    pallas_call x1, Pallas kernels, attn_backward(): pl.pallas_call(attn_backward_kernel, grid_spec=pltpu.PrefetchScalarGridSp...  36.9 us
    ppermute x34, starting transfers between devices, send(): return lax.ppermute(value, both, pairs)  36 us
    ppermute x34, waiting for transfers between devices, send(): return lax.ppermute(value, both, pairs)  34 us
    pallas_call x1, Pallas kernels, attn_forward(): pl.pallas_call(lambda place, frames, *refs: attn_forward_kernel(place, fr...  30.9 us
  transfers between devices with their start and end apart: 34, of which 16 were waited for; matrix products, arithmetic and copies ran while one was open for 2% of the time, Pallas kernels for 29%

profile of v4, /device:TPU:0, one launch (start us, length us, event | category | flops | bytes accessed | tf_op | source)
XLA Modules:
  0.0 231.2 jit_solution(14313270420540131308)
XLA Ops:
  0.6 1.3 pad_maximum_fusion.2.vec_ref
  1.9 1.7 pack.1
  3.6 5.0 %collective-permute-start.2 = (bf16[32,1152]{1,0:T(8,128)(2,1)}, bf16[32,1152]{1,0:T(8,128)(2,1)S(1)}, u32[]{:S(2)}, u32[]{:S(2)}) collective-permute-start(bf16[32,1152]{1,0:T(8,128)(2,1)} %get-tuple-element.36), channel_id=1, source_target_pairs={{0,24},{1,25},{2,26},{3,27},{4,28},{5,29},{6,30},{7,31},{8,0},{9,1... | collective-permute-start | bytes 221192 | tf_op jit(solution)/shard_map/ppermute | solution.py:458
  8.6 1.0 collective-permute-start
  9.6 0.6 stack.38.place
  10.2 1.4 collective-permute-done.2
  11.7 4.2 %collective-permute-done.1 = bf16[32,1152]{1,0:T(8,128)(2,1)S(1)} collective-permute-done((bf16[32,1152]{1,0:T(8,128)(2,1)}, bf16[32,1152]{1,0:T(8,128)(2,1)S(1)}, u32[]{:S(2)}, u32[]{:S(2)}) %collective-permute-start.1) | collective-permute-done | bytes 73760 | tf_op jit(solution)/shard_map/ppermute | solution.py:458
  15.8 0.9 pad_maximum_fusion.1.refs_1_
  16.8 2.5 %collective-permute-start.5 = (bf16[128,1152]{1,0:T(8,128)(2,1)S(1)}, bf16[128,1152]{1,0:T(8,128)(2,1)S(1)}, u32[]{:S(2)}, u32[]{:S(2)}) collective-permute-start(bf16[128,1152]{1,0:T(8,128)(2,1)S(1)} %pad_maximum_fusion.1.refs_1_), channel_id=1, source_target_pairs={{0,5},{1,4},{2,7},{3,6},{4,1},{5,0},{6,3},{7,2},{8,13},{9,12},{10,... | collective-permute-start | bytes 884744 | tf_op jit(solution)/shard_map/ppermute | solution.py:458
  19.3 0.5 collective-permute-start.4
  19.8 0.5 collective-permute-start.3
  20.3 2.0 collective-permute-start.12
  22.3 4.0 %collective-permute-done.12 = bf16[32,2048]{1,0:T(8,128)(2,1)S(1)} collective-permute-done((bf16[32,2048]{1,0:T(8,128)(2,1)}, bf16[32,2048]{1,0:T(8,128)(2,1)S(1)}, u32[]{:S(2)}, u32[]{:S(2)}) %collective-permute-start.12) | collective-permute-done | bytes 131104 | tf_op jit(solution)/shard_map/ppermute | solution.py:458
  26.3 3.1 %collective-permute-start.10 = (bf16[32,2048]{1,0:T(8,128)(2,1)}, bf16[32,2048]{1,0:T(8,128)(2,1)S(1)}, u32[]{:S(2)}, u32[]{:S(2)}) collective-permute-start(bf16[32,2048]{1,0:T(8,128)(2,1)} %get-tuple-element.42), channel_id=1, source_target_pairs={{0,8},{1,9},{2,10},{3,11},{4,12},{5,13},{6,14},{7,15},{8,16},{9,17... | collective-permute-start | bytes 393224 | tf_op jit(solution)/shard_map/ppermute | solution.py:458
  29.4 2.2 collective-permute-done.11
  31.7 0.5 collective-permute-start.9
  32.2 0.7 collective-permute-done.4.refs_3_
  32.9 0.0 collective-permute-start.8
  32.9 0.1 collective-permute-done.3.refs_2_
  33.0 0.4 collective-permute-start.7
  33.4 0.9 pad_maximum_fusion.refs_4_
  34.4 0.2 collective-permute-start.16
  34.6 2.2 collective-permute-start.15
  36.8 0.8 collective-permute-start.14
  37.6 0.5 collective-permute-start.13
  38.1 30.9 %attn_forward.1 = (bf16[4608,2048]{1,0:T(8,128)(2,1)}, bf16[4608,512]{1,0:T(8,128)(2,1)}, f32[4608,512]{1,0:T(8,128)}, f32[8,512]{1,0:T(8,128)}, bf16[1024,1152]{1,0:T(8,128)(2,1)}) custom-call(s32[6]{0:T(128)} %stack.38.place, s32[192]{0:T(256)} %frames.1, bf16[4608,512]{1,0:T(8,128)(2,1)} %x_ref.1, bf16[128,1152]{1,0:T(8,128)(2,1)} %copy-done.5, ...), custom_call_target="tpu_custom_call" | custom-call | flops 28991029248 | bytes 42467328 | tf_op jit(solution)/shard_map/attn_forward/pallas_call | solution.py:356
  69.1 0.1 collective-permute-start.17
  69.2 0.5 collective-permute-start.18
  69.7 0.1 collective-permute-start.19
  70.4 0.6 collective-permute-done.17.refs_9_
  71.1 0.7 collective-permute-done.18.refs_10_
  71.8 0.7 collective-permute-done.19.refs_11_
  72.6 0.8 copy-done.12
  73.4 78.9 %feed_forward.1 = (bf16[4608,512]{1,0:T(8,128)(2,1)}, f32[4608,512]{1,0:T(8,128)}, bf16[4,4,32,2304]{3,2,1,0:T(8,128)(2,1)}, bf16[4,4,32,2304]{3,2,1,0:T(8,128)(2,1)}, f32[2,512]{1,0:T(2,128)}) custom-call(s32[6]{0:T(128)} %stack.38.place, s32[1]{0:T(128)S(6)} %copy.26.live, f32[4608,512]{1,0:T(8,128)} %get-tuple-element.38.refs_0_, ...), custom_call_target="tpu_custom_call" | custom-call | flops 57982058496 | bytes 28311552 | tf_op jit(solution)/shard_map/feed_forward/pallas_call | solution.py:382
  152.3 0.2 collective-permute-start.20
  152.5 4.6 %collective-permute-done.20 = bf16[4,4,32,2304]{3,2,1,0:T(8,128)(2,1)S(1)} collective-permute-done((bf16[4,4,32,2304]{3,2,1,0:T(8,128)(2,1)}, bf16[4,4,32,2304]{3,2,1,0:T(8,128)(2,1)S(1)}, u32[]{:S(2)}, u32[]{:S(2)}) %collective-permute-start.20) | collective-permute-done | bytes 2359328 | tf_op jit(solution)/shard_map/ppermute | solution.py:458
  157.1 2.0 fusion.4
  159.2 2.3 collective-permute-start.27
  161.4 0.7 collective-permute-start.26
  162.2 0.5 collective-permute-start.25
  162.8 36.9 %attn_backward.1 = (f32[4608,512]{1,0:T(8,128)}, bf16[4,4,32,896]{3,2,1,0:T(8,128)(2,1)S(1)}, bf16[4,4,32,896]{3,2,1,0:T(8,128)(2,1)S(1)}) custom-call(s32[6]{0:T(128)S(1)} %copy-done, bf16[4608,512]{1,0:T(8,128)(2,1)S(1)} %bitcast.56, f32[4608,512]{1,0:T(8,128)} %get-tuple-element.51.gh_ref, bf16[4608,2048]{1,0:T(8,128)(2,1)} %get-tuple-element.52.qkvp_ref, ...), custom_call_target="tpu_custom_call" | custom-call | flops 43486543872 | bytes 42467328 | tf_op jit(solution)/shard_map/attn_backward/pallas_call | solution.py:417
  199.7 1.5 fusion.1
  201.2 1.0 collective-permute-done.21
  202.1 0.2 fusion.11
  202.4 1.5 collective-permute-start.30
  203.8 1.2 collective-permute-start.29
  205.0 0.8 collective-permute-start.28
  205.8 1.5 collective-permute-start.22
  207.3 1.5 collective-permute-start.24
  208.8 1.3 collective-permute-start.23
  210.0 8.3 %collective-permute-done.29 = bf16[32,2304]{1,0:T(8,128)(2,1)S(1)} collective-permute-done((bf16[32,2304]{1,0:T(8,128)(2,1)S(1)}, bf16[32,2304]{1,0:T(8,128)(2,1)S(1)}, u32[]{:S(2)}, u32[]{:S(2)}) %collective-permute-start.29) | collective-permute-done | bytes 147488 | tf_op jit(solution)/shard_map/ppermute | solution.py:458
  218.4 0.1 fusion.9
  218.4 0.7 slice_bitcast_fusion.3
  219.2 0.9 collective-permute-done.23
  220.0 0.1 fusion.7
  220.2 2.6 %collective-permute-start.31 = (bf16[32,896]{1,0:T(8,128)(2,1)S(1)}, bf16[32,896]{1,0:T(8,128)(2,1)S(1)}, u32[]{:S(2)}, u32[]{:S(2)}) collective-permute-start(bf16[32,896]{1,0:T(8,128)(2,1)S(1)} %get-tuple-element.75), channel_id=1, source_target_pairs={{0,8},{1,9},{2,10},{3,11},{4,12},{5,13},{6,14},{7,15},{8,16},{9,17... | collective-permute-start | bytes 172040 | tf_op jit(solution)/shard_map/ppermute | solution.py:458
  222.8 1.3 collective-permute-start.33
  224.1 0.7 collective-permute-start.32
  224.8 0.6 slice_bitcast_fusion.7
  225.4 0.9 collective-permute-done.31
  226.3 1.0 collective-permute-done.33
  227.3 2.4 %collective-permute-done.32 = bf16[32,896]{1,0:T(8,128)(2,1)S(1)} collective-permute-done((bf16[32,896]{1,0:T(8,128)(2,1)S(1)}, bf16[32,896]{1,0:T(8,128)(2,1)S(1)}, u32[]{:S(2)}, u32[]{:S(2)}) %collective-permute-start.32) | collective-permute-done | bytes 57376 | tf_op jit(solution)/shard_map/ppermute | solution.py:458
  229.8 0.7 slice_reduce_fusion
  230.5 0.6 fusion.16
  (61 shorter events, 0.2 us)
Async XLA Ops:
  3.6 8.1 %collective-permute-start.2 = (bf16[32,1152]{1,0:T(8,128)(2,1)}, bf16[32,1152]{1,0:T(8,128)(2,1)S(1)}, u32[]{:S(2)}, u32[]{:S(2)}) collective-permute-start(bf16[32,1152]{1,0:T(8,128)(2,1)} %get-tuple-element.36), channel_id=1, source_target_pairs={{0,24},{1,25},{2,26},{3,27},{4,28},{5,29},{6,30},{7,31},{8,0},{9,1... | collective-permute-start | bytes 221192 | tf_op jit(solution)/shard_map/ppermute | solution.py:458
  8.6 7.2 %collective-permute-start.1 = (bf16[32,1152]{1,0:T(8,128)(2,1)}, bf16[32,1152]{1,0:T(8,128)(2,1)S(1)}, u32[]{:S(2)}, u32[]{:S(2)}) collective-permute-start(bf16[32,1152]{1,0:T(8,128)(2,1)} %get-tuple-element.36), channel_id=1, source_target_pairs={{0,16},{1,17},{2,18},{3,19},{4,20},{5,21},{6,22},{7,23},{8,24},{9,... | collective-permute-start | bytes 221192 | tf_op jit(solution)/shard_map/ppermute | solution.py:458
  8.6 7.2 %collective-permute-start = (bf16[32,1152]{1,0:T(8,128)(2,1)}, bf16[32,1152]{1,0:T(8,128)(2,1)S(1)}, u32[]{:S(2)}, u32[]{:S(2)}) collective-permute-start(bf16[32,1152]{1,0:T(8,128)(2,1)} %get-tuple-element.36), channel_id=1, source_target_pairs={{0,8},{1,9},{2,10},{3,11},{4,12},{5,13},{6,14},{7,15},{8,16},{9,17... | collective-permute-start | bytes 221192 | tf_op jit(solution)/shard_map/ppermute | solution.py:458
  16.7 21.4 %copy-start.5 = (bf16[128,1152]{1,0:T(8,128)(2,1)}, bf16[128,1152]{1,0:T(8,128)(2,1)S(1)}, u32[]{:S(2)}) copy-start(bf16[128,1152]{1,0:T(8,128)(2,1)S(1)} %pad_maximum_fusion.1.refs_1_) | copy-start | bytes 884740
  16.8 14.9 %collective-permute-start.5 = (bf16[128,1152]{1,0:T(8,128)(2,1)S(1)}, bf16[128,1152]{1,0:T(8,128)(2,1)S(1)}, u32[]{:S(2)}, u32[]{:S(2)}) collective-permute-start(bf16[128,1152]{1,0:T(8,128)(2,1)S(1)} %pad_maximum_fusion.1.refs_1_), channel_id=1, source_target_pairs={{0,5},{1,4},{2,7},{3,6},{4,1},{5,0},{6,3},{7,2},{8,13},{9,12},{10,... | collective-permute-start | bytes 884744 | tf_op jit(solution)/shard_map/ppermute | solution.py:458
  19.3 13.6 %collective-permute-start.4 = (bf16[128,1152]{1,0:T(8,128)(2,1)S(1)}, bf16[128,1152]{1,0:T(8,128)(2,1)S(1)}, u32[]{:S(2)}, u32[]{:S(2)}) collective-permute-start(bf16[128,1152]{1,0:T(8,128)(2,1)S(1)} %pad_maximum_fusion.1.refs_1_), channel_id=1, source_target_pairs={{0,1},{1,0},{2,3},{3,2},{4,5},{5,4},{6,7},{7,6},{8,9},{9,8},{10,11... | collective-permute-start | bytes 884744 | tf_op jit(solution)/shard_map/ppermute | solution.py:458
  19.8 13.2 %collective-permute-start.3 = (bf16[128,1152]{1,0:T(8,128)(2,1)S(1)}, bf16[128,1152]{1,0:T(8,128)(2,1)S(1)}, u32[]{:S(2)}, u32[]{:S(2)}) collective-permute-start(bf16[128,1152]{1,0:T(8,128)(2,1)S(1)} %pad_maximum_fusion.1.refs_1_), channel_id=1, source_target_pairs={{0,4},{1,5},{2,6},{3,7},{4,0},{5,1},{6,2},{7,3},{8,12},{9,13},{10,... | collective-permute-start | bytes 884744 | tf_op jit(solution)/shard_map/ppermute | solution.py:458
  20.3 5.9 %collective-permute-start.12 = (bf16[32,2048]{1,0:T(8,128)(2,1)}, bf16[32,2048]{1,0:T(8,128)(2,1)S(1)}, u32[]{:S(2)}, u32[]{:S(2)}) collective-permute-start(bf16[32,2048]{1,0:T(8,128)(2,1)} %get-tuple-element.42), channel_id=1, source_target_pairs={{0,24},{1,25},{2,26},{3,27},{4,28},{5,29},{6,30},{7,31},{8,0},{9,1... | collective-permute-start | bytes 393224 | tf_op jit(solution)/shard_map/ppermute | solution.py:458
  22.3 9.3 %collective-permute-start.11 = (bf16[32,2048]{1,0:T(8,128)(2,1)}, bf16[32,2048]{1,0:T(8,128)(2,1)S(1)}, u32[]{:S(2)}, u32[]{:S(2)}) collective-permute-start(bf16[32,2048]{1,0:T(8,128)(2,1)} %get-tuple-element.42), channel_id=1, source_target_pairs={{0,16},{1,17},{2,18},{3,19},{4,20},{5,21},{6,22},{7,23},{8,24},{9,... | collective-permute-start | bytes 393224 | tf_op jit(solution)/shard_map/ppermute | solution.py:458
  26.3 7.2 %collective-permute-start.10 = (bf16[32,2048]{1,0:T(8,128)(2,1)}, bf16[32,2048]{1,0:T(8,128)(2,1)S(1)}, u32[]{:S(2)}, u32[]{:S(2)}) collective-permute-start(bf16[32,2048]{1,0:T(8,128)(2,1)} %get-tuple-element.42), channel_id=1, source_target_pairs={{0,8},{1,9},{2,10},{3,11},{4,12},{5,13},{6,14},{7,15},{8,16},{9,17... | collective-permute-start | bytes 393224 | tf_op jit(solution)/shard_map/ppermute | solution.py:458
  31.6 2.9 %collective-permute-start.6 = (bf16[128,1152]{1,0:T(8,128)(2,1)S(1)}, bf16[128,1152]{1,0:T(8,128)(2,1)}, u32[]{:S(2)}, u32[]{:S(2)}) collective-permute-start(bf16[128,1152]{1,0:T(8,128)(2,1)S(1)} %pad_maximum_fusion.1.refs_1_), channel_id=1, source_target_pairs={{0,2},{1,3},{2,0},{3,1},{4,6},{5,7},{6,4},{7,5},{8,10},{9,11},{10,... | collective-permute-start | bytes 884744 | tf_op jit(solution)/shard_map/ppermute | solution.py:458
  31.6 6.5 %copy-start.13 = (bf16[128,1152]{1,0:T(8,128)(2,1)}, bf16[128,1152]{1,0:T(8,128)(2,1)S(1)}, u32[]{:S(2)}) copy-start(bf16[128,1152]{1,0:T(8,128)(2,1)S(1)} %collective-permute-done.5.refs_4_) | copy-start | bytes 884740
  31.7 5.2 %collective-permute-start.9 = (bf16[128,1152]{1,0:T(8,128)(2,1)S(1)}, bf16[128,1152]{1,0:T(8,128)(2,1)}, u32[]{:S(2)}, u32[]{:S(2)}) collective-permute-start(bf16[128,1152]{1,0:T(8,128)(2,1)S(1)} %collective-permute-done.5.refs_4_), channel_id=1, source_target_pairs={{0,2},{1,3},{2,0},{3,1},{4,6},{5,7},{6,4},{7,5},{8,10},{9,11},{10,... | collective-permute-start | bytes 884744 | tf_op jit(solution)/shard_map/ppermute | solution.py:458
  32.9 5.2 %copy-start.14 = (bf16[128,1152]{1,0:T(8,128)(2,1)}, bf16[128,1152]{1,0:T(8,128)(2,1)S(1)}, u32[]{:S(2)}) copy-start(bf16[128,1152]{1,0:T(8,128)(2,1)S(1)} %collective-permute-done.4.refs_3_) | copy-start | bytes 884740
  32.9 4.7 %collective-permute-start.8 = (bf16[128,1152]{1,0:T(8,128)(2,1)S(1)}, bf16[128,1152]{1,0:T(8,128)(2,1)}, u32[]{:S(2)}, u32[]{:S(2)}) collective-permute-start(bf16[128,1152]{1,0:T(8,128)(2,1)S(1)} %collective-permute-done.4.refs_3_), channel_id=1, source_target_pairs={{0,2},{1,3},{2,0},{3,1},{4,6},{5,7},{6,4},{7,5},{8,10},{9,11},{10,... | collective-permute-start | bytes 884744 | tf_op jit(solution)/shard_map/ppermute | solution.py:458
  33.0 5.1 %copy-start.15 = (bf16[128,1152]{1,0:T(8,128)(2,1)}, bf16[128,1152]{1,0:T(8,128)(2,1)S(1)}, u32[]{:S(2)}) copy-start(bf16[128,1152]{1,0:T(8,128)(2,1)S(1)} %collective-permute-done.3.refs_2_) | copy-start | bytes 884740
  33.0 5.1 %collective-permute-start.7 = (bf16[128,1152]{1,0:T(8,128)(2,1)S(1)}, bf16[128,1152]{1,0:T(8,128)(2,1)}, u32[]{:S(2)}, u32[]{:S(2)}) collective-permute-start(bf16[128,1152]{1,0:T(8,128)(2,1)S(1)} %collective-permute-done.3.refs_2_), channel_id=1, source_target_pairs={{0,2},{1,3},{2,0},{3,1},{4,6},{5,7},{6,4},{7,5},{8,10},{9,11},{10,... | collective-permute-start | bytes 884744 | tf_op jit(solution)/shard_map/ppermute | solution.py:458
  34.4 34.7 %copy-start.4 = (bf16[128,2048]{1,0:T(8,128)(2,1)}, bf16[128,2048]{1,0:T(8,128)(2,1)S(1)}, u32[]{:S(2)}) copy-start(bf16[128,2048]{1,0:T(8,128)(2,1)S(1)} %pad_maximum_fusion.refs_4_) | copy-start | bytes 1572868
  34.4 36.0 %collective-permute-start.16 = (bf16[128,2048]{1,0:T(8,128)(2,1)S(1)}, bf16[128,2048]{1,0:T(8,128)(2,1)S(1)}, u32[]{:S(2)}, u32[]{:S(2)}) collective-permute-start(bf16[128,2048]{1,0:T(8,128)(2,1)S(1)} %pad_maximum_fusion.refs_4_), channel_id=1, source_target_pairs={{0,2},{1,3},{2,0},{3,1},{4,6},{5,7},{6,4},{7,5},{8,10},{9,11},{10,... | collective-permute-start | bytes 1572872 | tf_op jit(solution)/shard_map/ppermute | solution.py:458
  34.6 34.5 %collective-permute-start.15 = (bf16[128,2048]{1,0:T(8,128)(2,1)S(1)}, bf16[128,2048]{1,0:T(8,128)(2,1)S(1)}, u32[]{:S(2)}, u32[]{:S(2)}) collective-permute-start(bf16[128,2048]{1,0:T(8,128)(2,1)S(1)} %pad_maximum_fusion.refs_4_), channel_id=1, source_target_pairs={{0,5},{1,4},{2,7},{3,6},{4,1},{5,0},{6,3},{7,2},{8,13},{9,12},{10,... | collective-permute-start | bytes 1572872 | tf_op jit(solution)/shard_map/ppermute | solution.py:458
  36.8 32.3 %collective-permute-start.14 = (bf16[128,2048]{1,0:T(8,128)(2,1)S(1)}, bf16[128,2048]{1,0:T(8,128)(2,1)S(1)}, u32[]{:S(2)}, u32[]{:S(2)}) collective-permute-start(bf16[128,2048]{1,0:T(8,128)(2,1)S(1)} %pad_maximum_fusion.refs_4_), channel_id=1, source_target_pairs={{0,1},{1,0},{2,3},{3,2},{4,5},{5,4},{6,7},{7,6},{8,9},{9,8},{10,11... | collective-permute-start | bytes 1572872 | tf_op jit(solution)/shard_map/ppermute | solution.py:458
  37.6 31.5 %collective-permute-start.13 = (bf16[128,2048]{1,0:T(8,128)(2,1)S(1)}, bf16[128,2048]{1,0:T(8,128)(2,1)S(1)}, u32[]{:S(2)}, u32[]{:S(2)}) collective-permute-start(bf16[128,2048]{1,0:T(8,128)(2,1)S(1)} %pad_maximum_fusion.refs_4_), channel_id=1, source_target_pairs={{0,4},{1,5},{2,6},{3,7},{4,0},{5,1},{6,2},{7,3},{8,12},{9,13},{10,... | collective-permute-start | bytes 1572872 | tf_op jit(solution)/shard_map/ppermute | solution.py:458
  38.1 124.6 %slice-start = ((s8[4718592]{0:T(1024)(128)(4,1)}), s8[524288]{0:T(1024)(128)(4,1)S(1)}, s32[]{:S(2)}) async-start(s8[4718592]{0:T(1024)(128)(4,1)} %bitcast.55), calls=%async_computation | async-start | bytes 1048576
  69.1 3.5 %copy-start.7 = (bf16[128,2048]{1,0:T(8,128)(2,1)}, bf16[128,2048]{1,0:T(8,128)(2,1)S(1)}, u32[]{:S(2)}) copy-start(bf16[128,2048]{1,0:T(8,128)(2,1)S(1)} %collective-permute-done.15.refs_7_) | copy-start | bytes 1572868
  69.1 3.5 %copy-start.8 = (bf16[128,2048]{1,0:T(8,128)(2,1)}, bf16[128,2048]{1,0:T(8,128)(2,1)S(1)}, u32[]{:S(2)}) copy-start(bf16[128,2048]{1,0:T(8,128)(2,1)S(1)} %collective-permute-done.14.refs_6_) | copy-start | bytes 1572868
  69.1 3.5 %copy-start.9 = (bf16[128,2048]{1,0:T(8,128)(2,1)}, bf16[128,2048]{1,0:T(8,128)(2,1)S(1)}, u32[]{:S(2)}) copy-start(bf16[128,2048]{1,0:T(8,128)(2,1)S(1)} %collective-permute-done.13.refs_5_) | copy-start | bytes 1572868
  69.1 2.0 collective-permute-start.17
  69.2 2.6 %collective-permute-start.18 = (bf16[128,2048]{1,0:T(8,128)(2,1)S(1)}, bf16[128,2048]{1,0:T(8,128)(2,1)S(1)}, u32[]{:S(2)}, u32[]{:S(2)}) collective-permute-start(bf16[128,2048]{1,0:T(8,128)(2,1)S(1)} %collective-permute-done.14.refs_6_), channel_id=1, source_target_pairs={{0,2},{1,3},{2,0},{3,1},{4,6},{5,7},{6,4},{7,5},{8,10},{9,11},{10,... | collective-permute-start | bytes 1572872 | tf_op jit(solution)/shard_map/ppermute | solution.py:458
  69.7 2.9 %collective-permute-start.19 = (bf16[128,2048]{1,0:T(8,128)(2,1)S(1)}, bf16[128,2048]{1,0:T(8,128)(2,1)S(1)}, u32[]{:S(2)}, u32[]{:S(2)}) collective-permute-start(bf16[128,2048]{1,0:T(8,128)(2,1)S(1)} %collective-permute-done.15.refs_7_), channel_id=1, source_target_pairs={{0,2},{1,3},{2,0},{3,1},{4,6},{5,7},{6,4},{7,5},{8,10},{9,11},{10,... | collective-permute-start | bytes 1572872 | tf_op jit(solution)/shard_map/ppermute | solution.py:458
  70.4 2.2 copy-start.6
  71.1 1.5 copy-start.10
  71.8 0.8 copy-start.11
  72.6 0.8 copy-start.12
  73.4 89.3 %slice-start.1 = ((s8[4718592]{0:T(1024)(128)(4,1)}), s8[4194304]{0:T(1024)(128)(4,1)S(1)}, s32[]{:S(2)}) async-start(s8[4718592]{0:T(1024)(128)(4,1)} %bitcast.55), calls=%async_computation.1 | async-start | bytes 8388608
  152.3 4.8 %collective-permute-start.20 = (bf16[4,4,32,2304]{3,2,1,0:T(8,128)(2,1)}, bf16[4,4,32,2304]{3,2,1,0:T(8,128)(2,1)S(1)}, u32[]{:S(2)}, u32[]{:S(2)}) collective-permute-start(bf16[4,4,32,2304]{3,2,1,0:T(8,128)(2,1)} %get-tuple-element.50), channel_id=1, source_target_pairs={{0,2},{1,3},{2,0},{3,1},{4,6},{5,7},{6,4},{7,5},{8,10},{9,11},{10,... | collective-permute-start | bytes 7077896 | tf_op jit(solution)/shard_map/ppermute | solution.py:458
  157.1 5.6 %copy-start = (s32[6]{0:T(128)S(1)}, s32[6]{0:T(128)}, u32[]{:S(2)}) copy-start(s32[6]{0:T(128)} %stack.38.place) | copy-start | bytes 76
  157.1 5.6 %copy-start.1 = (bf16[1024,1152]{1,0:T(8,128)(2,1)S(1)}, bf16[1024,1152]{1,0:T(8,128)(2,1)}, u32[]{:S(2)}) copy-start(bf16[1024,1152]{1,0:T(8,128)(2,1)} %get-tuple-element.53.w_ref) | copy-start | bytes 7077892
  157.1 5.6 %copy-start.2 = (f32[8,512]{1,0:T(8,128)S(1)}, f32[8,512]{1,0:T(8,128)}, u32[]{:S(2)}) copy-start(f32[8,512]{1,0:T(8,128)} %get-tuple-element.40.refs_3_.vec_ref) | copy-start | bytes 49156
  157.1 5.6 %copy-start.3 = (f32[2,512]{1,0:T(2,128)S(1)}, f32[2,512]{1,0:T(2,128)}, u32[]{:S(2)}) copy-start(f32[2,512]{1,0:T(2,128)} %get-tuple-element.54.gvtwo_ref) | copy-start | bytes 12292
  159.2 40.5 %collective-permute-start.27 = (bf16[4,32,2304]{2,1,0:T(8,128)(2,1)S(1)}, bf16[4,32,2304]{2,1,0:T(8,128)(2,1)S(1)}, u32[]{:S(2)}, u32[]{:S(2)}) collective-permute-start(bf16[4,32,2304]{2,1,0:T(8,128)(2,1)S(1)} %get-tuple-element.64), channel_id=1, source_target_pairs={{0,5},{1,4},{2,7},{3,6},{4,1},{5,0},{6,3},{7,2},{8,13},{9,12},{10,... | collective-permute-start | bytes 1769480 | tf_op jit(solution)/shard_map/ppermute | solution.py:458
  161.4 38.2 %collective-permute-start.26 = (bf16[4,32,2304]{2,1,0:T(8,128)(2,1)S(1)}, bf16[4,32,2304]{2,1,0:T(8,128)(2,1)S(1)}, u32[]{:S(2)}, u32[]{:S(2)}) collective-permute-start(bf16[4,32,2304]{2,1,0:T(8,128)(2,1)S(1)} %get-tuple-element.65), channel_id=1, source_target_pairs={{0,1},{1,0},{2,3},{3,2},{4,5},{5,4},{6,7},{7,6},{8,9},{9,8},{10,11... | collective-permute-start | bytes 1769480 | tf_op jit(solution)/shard_map/ppermute | solution.py:458
  162.2 37.5 %collective-permute-start.25 = (bf16[4,32,2304]{2,1,0:T(8,128)(2,1)S(1)}, bf16[4,32,2304]{2,1,0:T(8,128)(2,1)S(1)}, u32[]{:S(2)}, u32[]{:S(2)}) collective-permute-start(bf16[4,32,2304]{2,1,0:T(8,128)(2,1)S(1)} %get-tuple-element.66), channel_id=1, source_target_pairs={{0,4},{1,5},{2,6},{3,7},{4,0},{5,1},{6,2},{7,3},{8,12},{9,13},{10,... | collective-permute-start | bytes 1769480 | tf_op jit(solution)/shard_map/ppermute | solution.py:458
  199.7 2.5 %collective-permute-start.21 = (bf16[4,4,32,896]{3,2,1,0:T(8,128)(2,1)S(1)}, bf16[4,4,32,896]{3,2,1,0:T(8,128)(2,1)S(1)}, u32[]{:S(2)}, u32[]{:S(2)}) collective-permute-start(bf16[4,4,32,896]{3,2,1,0:T(8,128)(2,1)S(1)} %get-tuple-element.57), channel_id=1, source_target_pairs={{0,2},{1,3},{2,0},{3,1},{4,6},{5,7},{6,4},{7,5},{8,10},{9,11},{10,... | collective-permute-start | bytes 2752520 | tf_op jit(solution)/shard_map/ppermute | solution.py:458
  202.4 6.4 %collective-permute-start.30 = (bf16[32,2304]{1,0:T(8,128)(2,1)S(1)}, bf16[32,2304]{1,0:T(8,128)(2,1)S(1)}, u32[]{:S(2)}, u32[]{:S(2)}) collective-permute-start(bf16[32,2304]{1,0:T(8,128)(2,1)S(1)} %get-tuple-element.70), channel_id=1, source_target_pairs={{0,24},{1,25},{2,26},{3,27},{4,28},{5,29},{6,30},{7,31},{8,0},{9,1... | collective-permute-start | bytes 442376 | tf_op jit(solution)/shard_map/ppermute | solution.py:458
  203.8 14.5 %collective-permute-start.29 = (bf16[32,2304]{1,0:T(8,128)(2,1)S(1)}, bf16[32,2304]{1,0:T(8,128)(2,1)S(1)}, u32[]{:S(2)}, u32[]{:S(2)}) collective-permute-start(bf16[32,2304]{1,0:T(8,128)(2,1)S(1)} %get-tuple-element.71), channel_id=1, source_target_pairs={{0,16},{1,17},{2,18},{3,19},{4,20},{5,21},{6,22},{7,23},{8,24},{9,... | collective-permute-start | bytes 442376 | tf_op jit(solution)/shard_map/ppermute | solution.py:458
  205.0 13.3 %collective-permute-start.28 = (bf16[32,2304]{1,0:T(8,128)(2,1)S(1)}, bf16[32,2304]{1,0:T(8,128)(2,1)S(1)}, u32[]{:S(2)}, u32[]{:S(2)}) collective-permute-start(bf16[32,2304]{1,0:T(8,128)(2,1)S(1)} %get-tuple-element.72), channel_id=1, source_target_pairs={{0,8},{1,9},{2,10},{3,11},{4,12},{5,13},{6,14},{7,15},{8,16},{9,17... | collective-permute-start | bytes 442376 | tf_op jit(solution)/shard_map/ppermute | solution.py:458
  205.8 13.4 %collective-permute-start.22 = (bf16[4,32,896]{2,1,0:T(8,128)(2,1)S(1)}, bf16[4,32,896]{2,1,0:T(8,128)(2,1)S(1)}, u32[]{:S(2)}, u32[]{:S(2)}) collective-permute-start(bf16[4,32,896]{2,1,0:T(8,128)(2,1)S(1)} %get-tuple-element.67), channel_id=1, source_target_pairs={{0,4},{1,5},{2,6},{3,7},{4,0},{5,1},{6,2},{7,3},{8,12},{9,13},{10,... | collective-permute-start | bytes 688136 | tf_op jit(solution)/shard_map/ppermute | solution.py:458
  207.3 11.9 %collective-permute-start.24 = (bf16[4,32,896]{2,1,0:T(8,128)(2,1)S(1)}, bf16[4,32,896]{2,1,0:T(8,128)(2,1)S(1)}, u32[]{:S(2)}, u32[]{:S(2)}) collective-permute-start(bf16[4,32,896]{2,1,0:T(8,128)(2,1)S(1)} %get-tuple-element.68), channel_id=1, source_target_pairs={{0,5},{1,4},{2,7},{3,6},{4,1},{5,0},{6,3},{7,2},{8,13},{9,12},{10,... | collective-permute-start | bytes 688136 | tf_op jit(solution)/shard_map/ppermute | solution.py:458
  208.8 11.3 %collective-permute-start.23 = (bf16[4,32,896]{2,1,0:T(8,128)(2,1)S(1)}, bf16[4,32,896]{2,1,0:T(8,128)(2,1)S(1)}, u32[]{:S(2)}, u32[]{:S(2)}) collective-permute-start(bf16[4,32,896]{2,1,0:T(8,128)(2,1)S(1)} %get-tuple-element.69), channel_id=1, source_target_pairs={{0,1},{1,0},{2,3},{3,2},{4,5},{5,4},{6,7},{7,6},{8,9},{9,8},{10,11... | collective-permute-start | bytes 688136 | tf_op jit(solution)/shard_map/ppermute | solution.py:458
  220.2 6.1 %collective-permute-start.31 = (bf16[32,896]{1,0:T(8,128)(2,1)S(1)}, bf16[32,896]{1,0:T(8,128)(2,1)S(1)}, u32[]{:S(2)}, u32[]{:S(2)}) collective-permute-start(bf16[32,896]{1,0:T(8,128)(2,1)S(1)} %get-tuple-element.75), channel_id=1, source_target_pairs={{0,8},{1,9},{2,10},{3,11},{4,12},{5,13},{6,14},{7,15},{8,16},{9,17... | collective-permute-start | bytes 172040 | tf_op jit(solution)/shard_map/ppermute | solution.py:458
  222.8 4.5 %collective-permute-start.33 = (bf16[32,896]{1,0:T(8,128)(2,1)S(1)}, bf16[32,896]{1,0:T(8,128)(2,1)S(1)}, u32[]{:S(2)}, u32[]{:S(2)}) collective-permute-start(bf16[32,896]{1,0:T(8,128)(2,1)S(1)} %get-tuple-element.76), channel_id=1, source_target_pairs={{0,24},{1,25},{2,26},{3,27},{4,28},{5,29},{6,30},{7,31},{8,0},{9,1... | collective-permute-start | bytes 172040 | tf_op jit(solution)/shard_map/ppermute | solution.py:458
  224.1 5.7 %collective-permute-start.32 = (bf16[32,896]{1,0:T(8,128)(2,1)S(1)}, bf16[32,896]{1,0:T(8,128)(2,1)S(1)}, u32[]{:S(2)}, u32[]{:S(2)}) collective-permute-start(bf16[32,896]{1,0:T(8,128)(2,1)S(1)} %get-tuple-element.77), channel_id=1, source_target_pairs={{0,16},{1,17},{2,18},{3,19},{4,20},{5,21},{6,22},{7,23},{8,24},{9,... | collective-permute-start | bytes 172040 | tf_op jit(solution)/shard_map/ppermute | solution.py:458

commit v5 on v4

--- a/solution.py
+++ b/solution.py
@@ -156,15 +156,15 @@
     n, _ = norm_parts(x)
     normed = (n * vec_ref[0:1] + vec_ref[1:2]).astype(BF)
     for m in range(HALVES):
-        qkv = nn(normed, w_ref[m * D : (m + 1) * D, : 3 * HW]).astype(BF)
         cols = slice(m * HW, (m + 1) * HW)
-        q_ref[:, cols] = qkv[:, :HW]
-        k_ref[:, cols] = qkv[:, HW : 2 * HW]
-        v_ref[:, cols] = qkv[:, 2 * HW :]
+        for i, ref in enumerate((q_ref, k_ref)):
+            ref[:, cols] = nn(normed, w_ref[m * D : (m + 1) * D, i * HW : (i + 1) * HW]).astype(BF)
     for s in range(seqs):
-        for m in range(HALVES):
-            at = seq_slice(s, m, HW)
-            s_ref[at] = nt(k_ref[at], per_head(q_ref[at]))
+        for c in range(D // PAIR):
+            at = seq_slice(s, c, PAIR)
+            s_ref[at] = pair_scores(k_ref[at], q_ref[at])
+    for m in range(HALVES):
+        v_ref[:, m * HW : (m + 1) * HW] = nn(normed, w_ref[m * D : (m + 1) * D, 2 * HW : 3 * HW]).astype(BF)
     key = lax.broadcasted_iota(jnp.int32, (SEQ, PAIR), 0)
     query = lax.broadcasted_iota(jnp.int32, (SEQ, PAIR), 1) % HEAD
     for s in range(seqs):
@@ -235,7 +235,7 @@
     gh = go + norm_back(n, rstd, vec_ref[2:3], gy)
     gh_ref[...] = gh
     for m in range(HALVES):
-        acco_ref[m] += tn(gh.astype(BF), ho_ref[:, m * HW : (m + 1) * HW])
+        acco_ref[m] += tn(gh_ref[...].astype(BF), ho_ref[:, m * HW : (m + 1) * HW])
     gvacc_ref[0] += fold_rows(gy * n)
     gvacc_ref[1] += fold_rows(gy)
 

time: 232 us -> 228 us (0.983)
  Pallas kernels: 148 us -> 145 us
where the time goes in v5:
time: 228 us
  Pallas kernels  145 us (64%)
  starting transfers between devices  36 us (16%)
  waiting for transfers between devices  34 us (15%)
  other arithmetic  7.01 us (3%)
  local copies, waits for them, and re-layouts  4.19 us (2%)
    pallas_call x1, Pallas kernels, feed_forward(): pl.pallas_call(lambda place, live, *refs: feed_forward_kernel(place, live...  77.9 us
    pallas_call x1, Pallas kernels, attn_backward(): pl.pallas_call(attn_backward_kernel, grid_spec=pltpu.PrefetchScalarGridSp...  36.9 us
    ppermute x34, starting transfers between devices, send(): return lax.ppermute(value, both, pairs)  36 us
    ppermute x34, waiting for transfers between devices, send(): return lax.ppermute(value, both, pairs)  34 us
    pallas_call x1, Pallas kernels, attn_forward(): pl.pallas_call(lambda place, frames, *refs: attn_forward_kernel(place, fr...  28.8 us
  transfers between devices with their start and end apart: 34, of which 16 were waited for; matrix products, arithmetic and copies ran while one was open for 2% of the time, Pallas kernels for 29%

profile of v5, /device:TPU:0, one launch (start us, length us, event | category | flops | bytes accessed | tf_op | source)
XLA Modules:
  0.0 228.0 jit_solution(5246004130331196902)
XLA Ops:
  0.6 1.3 pad_maximum_fusion.2.vec_ref
  1.9 1.7 pack.1
  3.6 5.0 %collective-permute-start.2 = (bf16[32,1152]{1,0:T(8,128)(2,1)}, bf16[32,1152]{1,0:T(8,128)(2,1)S(1)}, u32[]{:S(2)}, u32[]{:S(2)}) collective-permute-start(bf16[32,1152]{1,0:T(8,128)(2,1)} %get-tuple-element.36), channel_id=1, source_target_pairs={{0,24},{1,25},{2,26},{3,27},{4,28},{5,29},{6,30},{7,31},{8,0},{9,1... | collective-permute-start | bytes 221192 | tf_op jit(solution)/shard_map/ppermute | solution.py:458
  8.6 1.0 collective-permute-start
  9.6 0.6 stack.38.place
  10.2 1.4 collective-permute-done.2
  11.7 4.2 %collective-permute-done.1 = bf16[32,1152]{1,0:T(8,128)(2,1)S(1)} collective-permute-done((bf16[32,1152]{1,0:T(8,128)(2,1)}, bf16[32,1152]{1,0:T(8,128)(2,1)S(1)}, u32[]{:S(2)}, u32[]{:S(2)}) %collective-permute-start.1) | collective-permute-done | bytes 73760 | tf_op jit(solution)/shard_map/ppermute | solution.py:458
  15.8 0.9 pad_maximum_fusion.1.refs_1_
  16.8 2.5 %collective-permute-start.5 = (bf16[128,1152]{1,0:T(8,128)(2,1)S(1)}, bf16[128,1152]{1,0:T(8,128)(2,1)S(1)}, u32[]{:S(2)}, u32[]{:S(2)}) collective-permute-start(bf16[128,1152]{1,0:T(8,128)(2,1)S(1)} %pad_maximum_fusion.1.refs_1_), channel_id=1, source_target_pairs={{0,5},{1,4},{2,7},{3,6},{4,1},{5,0},{6,3},{7,2},{8,13},{9,12},{10,... | collective-permute-start | bytes 884744 | tf_op jit(solution)/shard_map/ppermute | solution.py:458
  19.3 0.5 collective-permute-start.4
  19.8 0.5 collective-permute-start.3
  20.3 2.0 collective-permute-start.12
  22.3 4.0 %collective-permute-done.12 = bf16[32,2048]{1,0:T(8,128)(2,1)S(1)} collective-permute-done((bf16[32,2048]{1,0:T(8,128)(2,1)}, bf16[32,2048]{1,0:T(8,128)(2,1)S(1)}, u32[]{:S(2)}, u32[]{:S(2)}) %collective-permute-start.12) | collective-permute-done | bytes 131104 | tf_op jit(solution)/shard_map/ppermute | solution.py:458
  26.3 3.1 %collective-permute-start.10 = (bf16[32,2048]{1,0:T(8,128)(2,1)}, bf16[32,2048]{1,0:T(8,128)(2,1)S(1)}, u32[]{:S(2)}, u32[]{:S(2)}) collective-permute-start(bf16[32,2048]{1,0:T(8,128)(2,1)} %get-tuple-element.42), channel_id=1, source_target_pairs={{0,8},{1,9},{2,10},{3,11},{4,12},{5,13},{6,14},{7,15},{8,16},{9,17... | collective-permute-start | bytes 393224 | tf_op jit(solution)/shard_map/ppermute | solution.py:458
  29.4 2.2 collective-permute-done.11
  31.7 0.5 collective-permute-start.9
  32.2 0.7 collective-permute-done.4.refs_3_
  32.9 0.0 collective-permute-start.8
  32.9 0.1 collective-permute-done.3.refs_2_
  33.0 0.4 collective-permute-start.7
  33.4 0.9 pad_maximum_fusion.refs_4_
  34.4 0.2 collective-permute-start.16
  34.6 2.2 collective-permute-start.15
  36.8 0.8 collective-permute-start.14
  37.6 0.5 collective-permute-start.13
  38.1 28.8 %attn_forward.1 = (bf16[4608,2048]{1,0:T(8,128)(2,1)}, bf16[4608,512]{1,0:T(8,128)(2,1)}, f32[4608,512]{1,0:T(8,128)}, f32[8,512]{1,0:T(8,128)}, bf16[1024,1152]{1,0:T(8,128)(2,1)}) custom-call(s32[6]{0:T(128)} %stack.38.place, s32[192]{0:T(256)} %frames.1, bf16[4608,512]{1,0:T(8,128)(2,1)} %x_ref.1, bf16[128,1152]{1,0:T(8,128)(2,1)} %copy-done.5, ...), custom_call_target="tpu_custom_call" | custom-call | flops 28991029248 | bytes 42467328 | tf_op jit(solution)/shard_map/attn_forward/pallas_call | solution.py:356
  67.0 0.1 collective-permute-start.17
  67.1 0.5 collective-permute-start.18
  67.6 0.1 collective-permute-start.19
  68.3 0.6 collective-permute-done.17.refs_9_
  69.0 0.7 collective-permute-done.18.refs_10_
  69.7 0.7 collective-permute-done.19.refs_11_
  70.5 0.8 copy-done.12
  71.3 77.9 %feed_forward.1 = (bf16[4608,512]{1,0:T(8,128)(2,1)}, f32[4608,512]{1,0:T(8,128)}, bf16[4,4,32,2304]{3,2,1,0:T(8,128)(2,1)}, bf16[4,4,32,2304]{3,2,1,0:T(8,128)(2,1)}, f32[2,512]{1,0:T(2,128)}) custom-call(s32[6]{0:T(128)} %stack.38.place, s32[1]{0:T(128)S(6)} %copy.26.live, f32[4608,512]{1,0:T(8,128)} %get-tuple-element.38.refs_0_, ...), custom_call_target="tpu_custom_call" | custom-call | flops 57982058496 | bytes 28311552 | tf_op jit(solution)/shard_map/feed_forward/pallas_call | solution.py:382
  149.2 0.2 collective-permute-start.20
  149.4 4.6 %collective-permute-done.20 = bf16[4,4,32,2304]{3,2,1,0:T(8,128)(2,1)S(1)} collective-permute-done((bf16[4,4,32,2304]{3,2,1,0:T(8,128)(2,1)}, bf16[4,4,32,2304]{3,2,1,0:T(8,128)(2,1)S(1)}, u32[]{:S(2)}, u32[]{:S(2)}) %collective-permute-start.20) | collective-permute-done | bytes 2359328 | tf_op jit(solution)/shard_map/ppermute | solution.py:458
  154.0 2.0 fusion.4
  156.0 2.3 %collective-permute-start.27 = (bf16[4,32,2304]{2,1,0:T(8,128)(2,1)S(1)}, bf16[4,32,2304]{2,1,0:T(8,128)(2,1)S(1)}, u32[]{:S(2)}, u32[]{:S(2)}) collective-permute-start(bf16[4,32,2304]{2,1,0:T(8,128)(2,1)S(1)} %get-tuple-element.64), channel_id=1, source_target_pairs={{0,5},{1,4},{2,7},{3,6},{4,1},{5,0},{6,3},{7,2},{8,13},{9,12},{10,... | collective-permute-start | bytes 1769480 | tf_op jit(solution)/shard_map/ppermute | solution.py:458
  158.3 0.9 collective-permute-start.26
  159.2 0.4 collective-permute-start.25
  159.6 36.9 %attn_backward.1 = (f32[4608,512]{1,0:T(8,128)}, bf16[4,4,32,896]{3,2,1,0:T(8,128)(2,1)S(1)}, bf16[4,4,32,896]{3,2,1,0:T(8,128)(2,1)S(1)}) custom-call(s32[6]{0:T(128)S(1)} %copy-done, bf16[4608,512]{1,0:T(8,128)(2,1)S(1)} %bitcast.56, f32[4608,512]{1,0:T(8,128)} %get-tuple-element.51.gh_ref, bf16[4608,2048]{1,0:T(8,128)(2,1)} %get-tuple-element.52.qkvp_ref, ...), custom_call_target="tpu_custom_call" | custom-call | flops 43486543872 | bytes 42467328 | tf_op jit(solution)/shard_map/attn_backward/pallas_call | solution.py:417
  196.5 1.5 fusion.1
  198.0 1.0 collective-permute-done.21
  199.0 0.2 fusion.11
  199.2 1.5 collective-permute-start.30
  200.7 1.2 collective-permute-start.29
  201.8 0.8 collective-permute-start.28
  202.6 1.5 collective-permute-start.22
  204.1 1.5 collective-permute-start.24
  205.6 1.3 collective-permute-start.23
  206.9 8.3 %collective-permute-done.29 = bf16[32,2304]{1,0:T(8,128)(2,1)S(1)} collective-permute-done((bf16[32,2304]{1,0:T(8,128)(2,1)S(1)}, bf16[32,2304]{1,0:T(8,128)(2,1)S(1)}, u32[]{:S(2)}, u32[]{:S(2)}) %collective-permute-start.29) | collective-permute-done | bytes 147488 | tf_op jit(solution)/shard_map/ppermute | solution.py:458
  215.2 0.1 fusion.9
  215.2 0.7 slice_bitcast_fusion.3
  216.0 0.9 collective-permute-done.23
  216.9 0.1 fusion.7
  217.0 2.6 %collective-permute-start.31 = (bf16[32,896]{1,0:T(8,128)(2,1)S(1)}, bf16[32,896]{1,0:T(8,128)(2,1)S(1)}, u32[]{:S(2)}, u32[]{:S(2)}) collective-permute-start(bf16[32,896]{1,0:T(8,128)(2,1)S(1)} %get-tuple-element.75), channel_id=1, source_target_pairs={{0,8},{1,9},{2,10},{3,11},{4,12},{5,13},{6,14},{7,15},{8,16},{9,17... | collective-permute-start | bytes 172040 | tf_op jit(solution)/shard_map/ppermute | solution.py:458
  219.6 1.3 collective-permute-start.33
  220.9 0.7 collective-permute-start.32
  221.6 0.6 slice_bitcast_fusion.7
  222.2 0.9 collective-permute-done.31
  223.2 0.9 collective-permute-done.33
  224.1 2.5 %collective-permute-done.32 = bf16[32,896]{1,0:T(8,128)(2,1)S(1)} collective-permute-done((bf16[32,896]{1,0:T(8,128)(2,1)S(1)}, bf16[32,896]{1,0:T(8,128)(2,1)S(1)}, u32[]{:S(2)}, u32[]{:S(2)}) %collective-permute-start.32) | collective-permute-done | bytes 57376 | tf_op jit(solution)/shard_map/ppermute | solution.py:458
  226.6 0.7 slice_reduce_fusion
  227.4 0.6 fusion.16
  (61 shorter events, 0.2 us)
Async XLA Ops:
  3.6 8.1 %collective-permute-start.2 = (bf16[32,1152]{1,0:T(8,128)(2,1)}, bf16[32,1152]{1,0:T(8,128)(2,1)S(1)}, u32[]{:S(2)}, u32[]{:S(2)}) collective-permute-start(bf16[32,1152]{1,0:T(8,128)(2,1)} %get-tuple-element.36), channel_id=1, source_target_pairs={{0,24},{1,25},{2,26},{3,27},{4,28},{5,29},{6,30},{7,31},{8,0},{9,1... | collective-permute-start | bytes 221192 | tf_op jit(solution)/shard_map/ppermute | solution.py:458
  8.6 7.2 %collective-permute-start.1 = (bf16[32,1152]{1,0:T(8,128)(2,1)}, bf16[32,1152]{1,0:T(8,128)(2,1)S(1)}, u32[]{:S(2)}, u32[]{:S(2)}) collective-permute-start(bf16[32,1152]{1,0:T(8,128)(2,1)} %get-tuple-element.36), channel_id=1, source_target_pairs={{0,16},{1,17},{2,18},{3,19},{4,20},{5,21},{6,22},{7,23},{8,24},{9,... | collective-permute-start | bytes 221192 | tf_op jit(solution)/shard_map/ppermute | solution.py:458
  8.6 7.2 %collective-permute-start = (bf16[32,1152]{1,0:T(8,128)(2,1)}, bf16[32,1152]{1,0:T(8,128)(2,1)S(1)}, u32[]{:S(2)}, u32[]{:S(2)}) collective-permute-start(bf16[32,1152]{1,0:T(8,128)(2,1)} %get-tuple-element.36), channel_id=1, source_target_pairs={{0,8},{1,9},{2,10},{3,11},{4,12},{5,13},{6,14},{7,15},{8,16},{9,17... | collective-permute-start | bytes 221192 | tf_op jit(solution)/shard_map/ppermute | solution.py:458
  16.7 21.4 %copy-start.5 = (bf16[128,1152]{1,0:T(8,128)(2,1)}, bf16[128,1152]{1,0:T(8,128)(2,1)S(1)}, u32[]{:S(2)}) copy-start(bf16[128,1152]{1,0:T(8,128)(2,1)S(1)} %pad_maximum_fusion.1.refs_1_) | copy-start | bytes 884740
  16.8 14.9 %collective-permute-start.5 = (bf16[128,1152]{1,0:T(8,128)(2,1)S(1)}, bf16[128,1152]{1,0:T(8,128)(2,1)S(1)}, u32[]{:S(2)}, u32[]{:S(2)}) collective-permute-start(bf16[128,1152]{1,0:T(8,128)(2,1)S(1)} %pad_maximum_fusion.1.refs_1_), channel_id=1, source_target_pairs={{0,5},{1,4},{2,7},{3,6},{4,1},{5,0},{6,3},{7,2},{8,13},{9,12},{10,... | collective-permute-start | bytes 884744 | tf_op jit(solution)/shard_map/ppermute | solution.py:458
  19.3 13.6 %collective-permute-start.4 = (bf16[128,1152]{1,0:T(8,128)(2,1)S(1)}, bf16[128,1152]{1,0:T(8,128)(2,1)S(1)}, u32[]{:S(2)}, u32[]{:S(2)}) collective-permute-start(bf16[128,1152]{1,0:T(8,128)(2,1)S(1)} %pad_maximum_fusion.1.refs_1_), channel_id=1, source_target_pairs={{0,1},{1,0},{2,3},{3,2},{4,5},{5,4},{6,7},{7,6},{8,9},{9,8},{10,11... | collective-permute-start | bytes 884744 | tf_op jit(solution)/shard_map/ppermute | solution.py:458
  19.8 13.2 %collective-permute-start.3 = (bf16[128,1152]{1,0:T(8,128)(2,1)S(1)}, bf16[128,1152]{1,0:T(8,128)(2,1)S(1)}, u32[]{:S(2)}, u32[]{:S(2)}) collective-permute-start(bf16[128,1152]{1,0:T(8,128)(2,1)S(1)} %pad_maximum_fusion.1.refs_1_), channel_id=1, source_target_pairs={{0,4},{1,5},{2,6},{3,7},{4,0},{5,1},{6,2},{7,3},{8,12},{9,13},{10,... | collective-permute-start | bytes 884744 | tf_op jit(solution)/shard_map/ppermute | solution.py:458
  20.3 5.9 %collective-permute-start.12 = (bf16[32,2048]{1,0:T(8,128)(2,1)}, bf16[32,2048]{1,0:T(8,128)(2,1)S(1)}, u32[]{:S(2)}, u32[]{:S(2)}) collective-permute-start(bf16[32,2048]{1,0:T(8,128)(2,1)} %get-tuple-element.42), channel_id=1, source_target_pairs={{0,24},{1,25},{2,26},{3,27},{4,28},{5,29},{6,30},{7,31},{8,0},{9,1... | collective-permute-start | bytes 393224 | tf_op jit(solution)/shard_map/ppermute | solution.py:458
  22.3 9.3 %collective-permute-start.11 = (bf16[32,2048]{1,0:T(8,128)(2,1)}, bf16[32,2048]{1,0:T(8,128)(2,1)S(1)}, u32[]{:S(2)}, u32[]{:S(2)}) collective-permute-start(bf16[32,2048]{1,0:T(8,128)(2,1)} %get-tuple-element.42), channel_id=1, source_target_pairs={{0,16},{1,17},{2,18},{3,19},{4,20},{5,21},{6,22},{7,23},{8,24},{9,... | collective-permute-start | bytes 393224 | tf_op jit(solution)/shard_map/ppermute | solution.py:458
  26.3 7.2 %collective-permute-start.10 = (bf16[32,2048]{1,0:T(8,128)(2,1)}, bf16[32,2048]{1,0:T(8,128)(2,1)S(1)}, u32[]{:S(2)}, u32[]{:S(2)}) collective-permute-start(bf16[32,2048]{1,0:T(8,128)(2,1)} %get-tuple-element.42), channel_id=1, source_target_pairs={{0,8},{1,9},{2,10},{3,11},{4,12},{5,13},{6,14},{7,15},{8,16},{9,17... | collective-permute-start | bytes 393224 | tf_op jit(solution)/shard_map/ppermute | solution.py:458
  31.6 2.9 %collective-permute-start.6 = (bf16[128,1152]{1,0:T(8,128)(2,1)S(1)}, bf16[128,1152]{1,0:T(8,128)(2,1)}, u32[]{:S(2)}, u32[]{:S(2)}) collective-permute-start(bf16[128,1152]{1,0:T(8,128)(2,1)S(1)} %pad_maximum_fusion.1.refs_1_), channel_id=1, source_target_pairs={{0,2},{1,3},{2,0},{3,1},{4,6},{5,7},{6,4},{7,5},{8,10},{9,11},{10,... | collective-permute-start | bytes 884744 | tf_op jit(solution)/shard_map/ppermute | solution.py:458
  31.6 6.5 %copy-start.13 = (bf16[128,1152]{1,0:T(8,128)(2,1)}, bf16[128,1152]{1,0:T(8,128)(2,1)S(1)}, u32[]{:S(2)}) copy-start(bf16[128,1152]{1,0:T(8,128)(2,1)S(1)} %collective-permute-done.5.refs_4_) | copy-start | bytes 884740
  31.7 5.2 %collective-permute-start.9 = (bf16[128,1152]{1,0:T(8,128)(2,1)S(1)}, bf16[128,1152]{1,0:T(8,128)(2,1)}, u32[]{:S(2)}, u32[]{:S(2)}) collective-permute-start(bf16[128,1152]{1,0:T(8,128)(2,1)S(1)} %collective-permute-done.5.refs_4_), channel_id=1, source_target_pairs={{0,2},{1,3},{2,0},{3,1},{4,6},{5,7},{6,4},{7,5},{8,10},{9,11},{10,... | collective-permute-start | bytes 884744 | tf_op jit(solution)/shard_map/ppermute | solution.py:458
  32.9 5.2 %copy-start.14 = (bf16[128,1152]{1,0:T(8,128)(2,1)}, bf16[128,1152]{1,0:T(8,128)(2,1)S(1)}, u32[]{:S(2)}) copy-start(bf16[128,1152]{1,0:T(8,128)(2,1)S(1)} %collective-permute-done.4.refs_3_) | copy-start | bytes 884740
  32.9 4.7 %collective-permute-start.8 = (bf16[128,1152]{1,0:T(8,128)(2,1)S(1)}, bf16[128,1152]{1,0:T(8,128)(2,1)}, u32[]{:S(2)}, u32[]{:S(2)}) collective-permute-start(bf16[128,1152]{1,0:T(8,128)(2,1)S(1)} %collective-permute-done.4.refs_3_), channel_id=1, source_target_pairs={{0,2},{1,3},{2,0},{3,1},{4,6},{5,7},{6,4},{7,5},{8,10},{9,11},{10,... | collective-permute-start | bytes 884744 | tf_op jit(solution)/shard_map/ppermute | solution.py:458
  33.0 5.1 %copy-start.15 = (bf16[128,1152]{1,0:T(8,128)(2,1)}, bf16[128,1152]{1,0:T(8,128)(2,1)S(1)}, u32[]{:S(2)}) copy-start(bf16[128,1152]{1,0:T(8,128)(2,1)S(1)} %collective-permute-done.3.refs_2_) | copy-start | bytes 884740
  33.0 5.1 %collective-permute-start.7 = (bf16[128,1152]{1,0:T(8,128)(2,1)S(1)}, bf16[128,1152]{1,0:T(8,128)(2,1)}, u32[]{:S(2)}, u32[]{:S(2)}) collective-permute-start(bf16[128,1152]{1,0:T(8,128)(2,1)S(1)} %collective-permute-done.3.refs_2_), channel_id=1, source_target_pairs={{0,2},{1,3},{2,0},{3,1},{4,6},{5,7},{6,4},{7,5},{8,10},{9,11},{10,... | collective-permute-start | bytes 884744 | tf_op jit(solution)/shard_map/ppermute | solution.py:458
  34.4 32.5 %copy-start.4 = (bf16[128,2048]{1,0:T(8,128)(2,1)}, bf16[128,2048]{1,0:T(8,128)(2,1)S(1)}, u32[]{:S(2)}) copy-start(bf16[128,2048]{1,0:T(8,128)(2,1)S(1)} %pad_maximum_fusion.refs_4_) | copy-start | bytes 1572868
  34.4 33.9 %collective-permute-start.16 = (bf16[128,2048]{1,0:T(8,128)(2,1)S(1)}, bf16[128,2048]{1,0:T(8,128)(2,1)S(1)}, u32[]{:S(2)}, u32[]{:S(2)}) collective-permute-start(bf16[128,2048]{1,0:T(8,128)(2,1)S(1)} %pad_maximum_fusion.refs_4_), channel_id=1, source_target_pairs={{0,2},{1,3},{2,0},{3,1},{4,6},{5,7},{6,4},{7,5},{8,10},{9,11},{10,... | collective-permute-start | bytes 1572872 | tf_op jit(solution)/shard_map/ppermute | solution.py:458
  34.6 32.4 %collective-permute-start.15 = (bf16[128,2048]{1,0:T(8,128)(2,1)S(1)}, bf16[128,2048]{1,0:T(8,128)(2,1)S(1)}, u32[]{:S(2)}, u32[]{:S(2)}) collective-permute-start(bf16[128,2048]{1,0:T(8,128)(2,1)S(1)} %pad_maximum_fusion.refs_4_), channel_id=1, source_target_pairs={{0,5},{1,4},{2,7},{3,6},{4,1},{5,0},{6,3},{7,2},{8,13},{9,12},{10,... | collective-permute-start | bytes 1572872 | tf_op jit(solution)/shard_map/ppermute | solution.py:458
  36.8 30.1 %collective-permute-start.14 = (bf16[128,2048]{1,0:T(8,128)(2,1)S(1)}, bf16[128,2048]{1,0:T(8,128)(2,1)S(1)}, u32[]{:S(2)}, u32[]{:S(2)}) collective-permute-start(bf16[128,2048]{1,0:T(8,128)(2,1)S(1)} %pad_maximum_fusion.refs_4_), channel_id=1, source_target_pairs={{0,1},{1,0},{2,3},{3,2},{4,5},{5,4},{6,7},{7,6},{8,9},{9,8},{10,11... | collective-permute-start | bytes 1572872 | tf_op jit(solution)/shard_map/ppermute | solution.py:458
  37.6 29.4 %collective-permute-start.13 = (bf16[128,2048]{1,0:T(8,128)(2,1)S(1)}, bf16[128,2048]{1,0:T(8,128)(2,1)S(1)}, u32[]{:S(2)}, u32[]{:S(2)}) collective-permute-start(bf16[128,2048]{1,0:T(8,128)(2,1)S(1)} %pad_maximum_fusion.refs_4_), channel_id=1, source_target_pairs={{0,4},{1,5},{2,6},{3,7},{4,0},{5,1},{6,2},{7,3},{8,12},{9,13},{10,... | collective-permute-start | bytes 1572872 | tf_op jit(solution)/shard_map/ppermute | solution.py:458
  38.1 121.4 %slice-start = ((s8[4718592]{0:T(1024)(128)(4,1)}), s8[524288]{0:T(1024)(128)(4,1)S(1)}, s32[]{:S(2)}) async-start(s8[4718592]{0:T(1024)(128)(4,1)} %bitcast.55), calls=%async_computation | async-start | bytes 1048576
  66.9 3.5 %copy-start.7 = (bf16[128,2048]{1,0:T(8,128)(2,1)}, bf16[128,2048]{1,0:T(8,128)(2,1)S(1)}, u32[]{:S(2)}) copy-start(bf16[128,2048]{1,0:T(8,128)(2,1)S(1)} %collective-permute-done.15.refs_7_) | copy-start | bytes 1572868
  66.9 3.5 %copy-start.8 = (bf16[128,2048]{1,0:T(8,128)(2,1)}, bf16[128,2048]{1,0:T(8,128)(2,1)S(1)}, u32[]{:S(2)}) copy-start(bf16[128,2048]{1,0:T(8,128)(2,1)S(1)} %collective-permute-done.14.refs_6_) | copy-start | bytes 1572868
  67.0 3.5 %copy-start.9 = (bf16[128,2048]{1,0:T(8,128)(2,1)}, bf16[128,2048]{1,0:T(8,128)(2,1)S(1)}, u32[]{:S(2)}) copy-start(bf16[128,2048]{1,0:T(8,128)(2,1)S(1)} %collective-permute-done.13.refs_5_) | copy-start | bytes 1572868
  67.0 2.0 collective-permute-start.17
  67.1 2.6 %collective-permute-start.18 = (bf16[128,2048]{1,0:T(8,128)(2,1)S(1)}, bf16[128,2048]{1,0:T(8,128)(2,1)S(1)}, u32[]{:S(2)}, u32[]{:S(2)}) collective-permute-start(bf16[128,2048]{1,0:T(8,128)(2,1)S(1)} %collective-permute-done.14.refs_6_), channel_id=1, source_target_pairs={{0,2},{1,3},{2,0},{3,1},{4,6},{5,7},{6,4},{7,5},{8,10},{9,11},{10,... | collective-permute-start | bytes 1572872 | tf_op jit(solution)/shard_map/ppermute | solution.py:458
  67.6 2.9 %collective-permute-start.19 = (bf16[128,2048]{1,0:T(8,128)(2,1)S(1)}, bf16[128,2048]{1,0:T(8,128)(2,1)S(1)}, u32[]{:S(2)}, u32[]{:S(2)}) collective-permute-start(bf16[128,2048]{1,0:T(8,128)(2,1)S(1)} %collective-permute-done.15.refs_7_), channel_id=1, source_target_pairs={{0,2},{1,3},{2,0},{3,1},{4,6},{5,7},{6,4},{7,5},{8,10},{9,11},{10,... | collective-permute-start | bytes 1572872 | tf_op jit(solution)/shard_map/ppermute | solution.py:458
  68.3 2.2 copy-start.6
  69.0 1.5 copy-start.10
  69.7 0.8 copy-start.11
  70.5 0.8 copy-start.12
  71.3 88.3 %slice-start.1 = ((s8[4718592]{0:T(1024)(128)(4,1)}), s8[4194304]{0:T(1024)(128)(4,1)S(1)}, s32[]{:S(2)}) async-start(s8[4718592]{0:T(1024)(128)(4,1)} %bitcast.55), calls=%async_computation.1 | async-start | bytes 8388608
  149.2 4.8 %collective-permute-start.20 = (bf16[4,4,32,2304]{3,2,1,0:T(8,128)(2,1)}, bf16[4,4,32,2304]{3,2,1,0:T(8,128)(2,1)S(1)}, u32[]{:S(2)}, u32[]{:S(2)}) collective-permute-start(bf16[4,4,32,2304]{3,2,1,0:T(8,128)(2,1)} %get-tuple-element.50), channel_id=1, source_target_pairs={{0,2},{1,3},{2,0},{3,1},{4,6},{5,7},{6,4},{7,5},{8,10},{9,11},{10,... | collective-permute-start | bytes 7077896 | tf_op jit(solution)/shard_map/ppermute | solution.py:458
  154.0 5.6 %copy-start = (s32[6]{0:T(128)S(1)}, s32[6]{0:T(128)}, u32[]{:S(2)}) copy-start(s32[6]{0:T(128)} %stack.38.place) | copy-start | bytes 76
  154.0 5.6 %copy-start.1 = (bf16[1024,1152]{1,0:T(8,128)(2,1)S(1)}, bf16[1024,1152]{1,0:T(8,128)(2,1)}, u32[]{:S(2)}) copy-start(bf16[1024,1152]{1,0:T(8,128)(2,1)} %get-tuple-element.53.w_ref) | copy-start | bytes 7077892
  154.0 5.6 %copy-start.2 = (f32[8,512]{1,0:T(8,128)S(1)}, f32[8,512]{1,0:T(8,128)}, u32[]{:S(2)}) copy-start(f32[8,512]{1,0:T(8,128)} %get-tuple-element.40.refs_3_.vec_ref) | copy-start | bytes 49156
  154.0 5.6 %copy-start.3 = (f32[2,512]{1,0:T(2,128)S(1)}, f32[2,512]{1,0:T(2,128)}, u32[]{:S(2)}) copy-start(f32[2,512]{1,0:T(2,128)} %get-tuple-element.54.gvtwo_ref) | copy-start | bytes 12292
  156.0 40.5 %collective-permute-start.27 = (bf16[4,32,2304]{2,1,0:T(8,128)(2,1)S(1)}, bf16[4,32,2304]{2,1,0:T(8,128)(2,1)S(1)}, u32[]{:S(2)}, u32[]{:S(2)}) collective-permute-start(bf16[4,32,2304]{2,1,0:T(8,128)(2,1)S(1)} %get-tuple-element.64), channel_id=1, source_target_pairs={{0,5},{1,4},{2,7},{3,6},{4,1},{5,0},{6,3},{7,2},{8,13},{9,12},{10,... | collective-permute-start | bytes 1769480 | tf_op jit(solution)/shard_map/ppermute | solution.py:458
  158.3 38.2 %collective-permute-start.26 = (bf16[4,32,2304]{2,1,0:T(8,128)(2,1)S(1)}, bf16[4,32,2304]{2,1,0:T(8,128)(2,1)S(1)}, u32[]{:S(2)}, u32[]{:S(2)}) collective-permute-start(bf16[4,32,2304]{2,1,0:T(8,128)(2,1)S(1)} %get-tuple-element.65), channel_id=1, source_target_pairs={{0,1},{1,0},{2,3},{3,2},{4,5},{5,4},{6,7},{7,6},{8,9},{9,8},{10,11... | collective-permute-start | bytes 1769480 | tf_op jit(solution)/shard_map/ppermute | solution.py:458
  159.2 37.4 %collective-permute-start.25 = (bf16[4,32,2304]{2,1,0:T(8,128)(2,1)S(1)}, bf16[4,32,2304]{2,1,0:T(8,128)(2,1)S(1)}, u32[]{:S(2)}, u32[]{:S(2)}) collective-permute-start(bf16[4,32,2304]{2,1,0:T(8,128)(2,1)S(1)} %get-tuple-element.66), channel_id=1, source_target_pairs={{0,4},{1,5},{2,6},{3,7},{4,0},{5,1},{6,2},{7,3},{8,12},{9,13},{10,... | collective-permute-start | bytes 1769480 | tf_op jit(solution)/shard_map/ppermute | solution.py:458
  196.5 2.5 %collective-permute-start.21 = (bf16[4,4,32,896]{3,2,1,0:T(8,128)(2,1)S(1)}, bf16[4,4,32,896]{3,2,1,0:T(8,128)(2,1)S(1)}, u32[]{:S(2)}, u32[]{:S(2)}) collective-permute-start(bf16[4,4,32,896]{3,2,1,0:T(8,128)(2,1)S(1)} %get-tuple-element.57), channel_id=1, source_target_pairs={{0,2},{1,3},{2,0},{3,1},{4,6},{5,7},{6,4},{7,5},{8,10},{9,11},{10,... | collective-permute-start | bytes 2752520 | tf_op jit(solution)/shard_map/ppermute | solution.py:458
  199.2 6.4 %collective-permute-start.30 = (bf16[32,2304]{1,0:T(8,128)(2,1)S(1)}, bf16[32,2304]{1,0:T(8,128)(2,1)S(1)}, u32[]{:S(2)}, u32[]{:S(2)}) collective-permute-start(bf16[32,2304]{1,0:T(8,128)(2,1)S(1)} %get-tuple-element.70), channel_id=1, source_target_pairs={{0,24},{1,25},{2,26},{3,27},{4,28},{5,29},{6,30},{7,31},{8,0},{9,1... | collective-permute-start | bytes 442376 | tf_op jit(solution)/shard_map/ppermute | solution.py:458
  200.7 14.5 %collective-permute-start.29 = (bf16[32,2304]{1,0:T(8,128)(2,1)S(1)}, bf16[32,2304]{1,0:T(8,128)(2,1)S(1)}, u32[]{:S(2)}, u32[]{:S(2)}) collective-permute-start(bf16[32,2304]{1,0:T(8,128)(2,1)S(1)} %get-tuple-element.71), channel_id=1, source_target_pairs={{0,16},{1,17},{2,18},{3,19},{4,20},{5,21},{6,22},{7,23},{8,24},{9,... | collective-permute-start | bytes 442376 | tf_op jit(solution)/shard_map/ppermute | solution.py:458
  201.8 13.3 %collective-permute-start.28 = (bf16[32,2304]{1,0:T(8,128)(2,1)S(1)}, bf16[32,2304]{1,0:T(8,128)(2,1)S(1)}, u32[]{:S(2)}, u32[]{:S(2)}) collective-permute-start(bf16[32,2304]{1,0:T(8,128)(2,1)S(1)} %get-tuple-element.72), channel_id=1, source_target_pairs={{0,8},{1,9},{2,10},{3,11},{4,12},{5,13},{6,14},{7,15},{8,16},{9,17... | collective-permute-start | bytes 442376 | tf_op jit(solution)/shard_map/ppermute | solution.py:458
  202.6 13.4 %collective-permute-start.22 = (bf16[4,32,896]{2,1,0:T(8,128)(2,1)S(1)}, bf16[4,32,896]{2,1,0:T(8,128)(2,1)S(1)}, u32[]{:S(2)}, u32[]{:S(2)}) collective-permute-start(bf16[4,32,896]{2,1,0:T(8,128)(2,1)S(1)} %get-tuple-element.67), channel_id=1, source_target_pairs={{0,4},{1,5},{2,6},{3,7},{4,0},{5,1},{6,2},{7,3},{8,12},{9,13},{10,... | collective-permute-start | bytes 688136 | tf_op jit(solution)/shard_map/ppermute | solution.py:458
  204.1 11.9 %collective-permute-start.24 = (bf16[4,32,896]{2,1,0:T(8,128)(2,1)S(1)}, bf16[4,32,896]{2,1,0:T(8,128)(2,1)S(1)}, u32[]{:S(2)}, u32[]{:S(2)}) collective-permute-start(bf16[4,32,896]{2,1,0:T(8,128)(2,1)S(1)} %get-tuple-element.68), channel_id=1, source_target_pairs={{0,5},{1,4},{2,7},{3,6},{4,1},{5,0},{6,3},{7,2},{8,13},{9,12},{10,... | collective-permute-start | bytes 688136 | tf_op jit(solution)/shard_map/ppermute | solution.py:458
  205.6 11.2 %collective-permute-start.23 = (bf16[4,32,896]{2,1,0:T(8,128)(2,1)S(1)}, bf16[4,32,896]{2,1,0:T(8,128)(2,1)S(1)}, u32[]{:S(2)}, u32[]{:S(2)}) collective-permute-start(bf16[4,32,896]{2,1,0:T(8,128)(2,1)S(1)} %get-tuple-element.69), channel_id=1, source_target_pairs={{0,1},{1,0},{2,3},{3,2},{4,5},{5,4},{6,7},{7,6},{8,9},{9,8},{10,11... | collective-permute-start | bytes 688136 | tf_op jit(solution)/shard_map/ppermute | solution.py:458
  217.0 6.1 %collective-permute-start.31 = (bf16[32,896]{1,0:T(8,128)(2,1)S(1)}, bf16[32,896]{1,0:T(8,128)(2,1)S(1)}, u32[]{:S(2)}, u32[]{:S(2)}) collective-permute-start(bf16[32,896]{1,0:T(8,128)(2,1)S(1)} %get-tuple-element.75), channel_id=1, source_target_pairs={{0,8},{1,9},{2,10},{3,11},{4,12},{5,13},{6,14},{7,15},{8,16},{9,17... | collective-permute-start | bytes 172040 | tf_op jit(solution)/shard_map/ppermute | solution.py:458
  219.6 4.5 %collective-permute-start.33 = (bf16[32,896]{1,0:T(8,128)(2,1)S(1)}, bf16[32,896]{1,0:T(8,128)(2,1)S(1)}, u32[]{:S(2)}, u32[]{:S(2)}) collective-permute-start(bf16[32,896]{1,0:T(8,128)(2,1)S(1)} %get-tuple-element.76), channel_id=1, source_target_pairs={{0,24},{1,25},{2,26},{3,27},{4,28},{5,29},{6,30},{7,31},{8,0},{9,1... | collective-permute-start | bytes 172040 | tf_op jit(solution)/shard_map/ppermute | solution.py:458
  220.9 5.7 %collective-permute-start.32 = (bf16[32,896]{1,0:T(8,128)(2,1)S(1)}, bf16[32,896]{1,0:T(8,128)(2,1)S(1)}, u32[]{:S(2)}, u32[]{:S(2)}) collective-permute-start(bf16[32,896]{1,0:T(8,128)(2,1)S(1)} %get-tuple-element.77), channel_id=1, source_target_pairs={{0,16},{1,17},{2,18},{3,19},{4,20},{5,21},{6,22},{7,23},{8,24},{9,... | collective-permute-start | bytes 172040 | tf_op jit(solution)/shard_map/ppermute | solution.py:458

commit v6 on v5

--- a/solution.py
+++ b/solution.py
@@ -232,10 +232,9 @@
         accu_ref[m] += tn(normed, gup_ref[:, cols])
         accd_ref[m] += tn(go_ref[...], act_ref[:, cols])
     mixed_ref[...] = (hidden + down).astype(BF)
-    gh = go + norm_back(n, rstd, vec_ref[2:3], gy)
-    gh_ref[...] = gh
+    gh_ref[...] = (go + norm_back(n, rstd, vec_ref[2:3], gy)).astype(BF)
     for m in range(HALVES):
-        acco_ref[m] += tn(gh_ref[...].astype(BF), ho_ref[:, m * HW : (m + 1) * HW])
+        acco_ref[m] += tn(gh_ref[...], ho_ref[:, m * HW : (m + 1) * HW])
     gvacc_ref[0] += fold_rows(gy * n)
     gvacc_ref[1] += fold_rows(gy)
 
@@ -262,10 +261,8 @@
         acc_ref[...] = jnp.zeros_like(acc_ref)
         gvacc_ref[...] = jnp.zeros_like(gvacc_ref)
 
-    gh = gh_ref[...]
-    gat = gh.astype(BF)
     for m in range(HALVES):
-        dh_ref[:, m * HW : (m + 1) * HW] = nn(gat, w_ref[m * D : (m + 1) * D, 3 * HW : 4 * HW]).astype(BF)
+        dh_ref[:, m * HW : (m + 1) * HW] = nn(gh_ref[...], w_ref[m * D : (m + 1) * D, 3 * HW : 4 * HW]).astype(BF)
     for s in range(seqs):
         for c in range(D // PAIR):
             at = seq_slice(s, c, PAIR)
@@ -292,7 +289,7 @@
         cols = slice(3 * HW * m, 3 * HW * (m + 1))
         gy += nt(dqkv_ref[:, cols], w_ref[m * D : (m + 1) * D, : 3 * HW])
         acc_ref[m] += tn(normed, dqkv_ref[:, cols])
-    gi_ref[...] = gh + norm_back(n, rstd, vec_ref[0:1], gy)
+    gi_ref[...] = gh_ref[...].astype(F32) + norm_back(n, rstd, vec_ref[0:1], gy)
     gvacc_ref[0] += fold_rows(gy * n)
     gvacc_ref[1] += fold_rows(gy)
 
@@ -400,7 +397,7 @@
         ),
         out_shape=[
             shape((rows, D), BF),
-            shape((rows, D), F32),
+            shape((rows, D), BF),
             shape(grads, BF),
             shape(grads, BF),
             shape((2, D), F32),

time: 228 us -> 228 us (level)
  no operation moved by 1% of the time
where the time goes in v6:
time: 228 us; the launch traced here: 227 us
  Pallas kernels  144 us (63%)
  starting transfers between devices  35.9 us (16%)
  waiting for transfers between devices  34.3 us (15%)
  other arithmetic  6.98 us (3%)
  local copies, waits for them, and re-layouts  4.36 us (2%)
    pallas_call x1, Pallas kernels, feed_forward(): pl.pallas_call(lambda place, live, *refs: feed_forward_kernel(place, live...  77.7 us
    pallas_call x1, Pallas kernels, attn_backward(): pl.pallas_call(attn_backward_kernel, grid_spec=pltpu.PrefetchScalarGridSp...  36.1 us
    ppermute x34, starting transfers between devices, send(): return lax.ppermute(value, both, pairs)  35.9 us
    ppermute x34, waiting for transfers between devices, send(): return lax.ppermute(value, both, pairs)  34.3 us
    pallas_call x1, Pallas kernels, attn_forward(): pl.pallas_call(lambda place, frames, *refs: attn_forward_kernel(place, fr...  28.7 us
  transfers between devices with their start and end apart: 34, of which 16 were waited for; matrix products, arithmetic and copies ran while one was open for 2% of the time, Pallas kernels for 29%

profile of v6, /device:TPU:0, one launch (start us, length us, event | category | flops | bytes accessed | tf_op | source)
XLA Modules:
  0.0 227.3 jit_solution(9726098115001754280)
XLA Ops:
  0.6 1.3 pad_maximum_fusion.2.vec_ref
  1.9 1.7 pack.1
  3.6 5.0 %collective-permute-start.2 = (bf16[32,1152]{1,0:T(8,128)(2,1)}, bf16[32,1152]{1,0:T(8,128)(2,1)S(1)}, u32[]{:S(2)}, u32[]{:S(2)}) collective-permute-start(bf16[32,1152]{1,0:T(8,128)(2,1)} %get-tuple-element.36), channel_id=1, source_target_pairs={{0,24},{1,25},{2,26},{3,27},{4,28},{5,29},{6,30},{7,31},{8,0},{9,1... | collective-permute-start | bytes 221192 | tf_op jit(solution)/shard_map/ppermute | solution.py:455
  8.6 1.0 collective-permute-start
  9.6 0.6 stack.38.place
  10.2 1.4 collective-permute-done.2
  11.7 4.2 %collective-permute-done.1 = bf16[32,1152]{1,0:T(8,128)(2,1)S(1)} collective-permute-done((bf16[32,1152]{1,0:T(8,128)(2,1)}, bf16[32,1152]{1,0:T(8,128)(2,1)S(1)}, u32[]{:S(2)}, u32[]{:S(2)}) %collective-permute-start.1) | collective-permute-done | bytes 73760 | tf_op jit(solution)/shard_map/ppermute | solution.py:455
  15.8 0.9 pad_maximum_fusion.1.refs_1_
  16.8 2.5 %collective-permute-start.5 = (bf16[128,1152]{1,0:T(8,128)(2,1)S(1)}, bf16[128,1152]{1,0:T(8,128)(2,1)S(1)}, u32[]{:S(2)}, u32[]{:S(2)}) collective-permute-start(bf16[128,1152]{1,0:T(8,128)(2,1)S(1)} %pad_maximum_fusion.1.refs_1_), channel_id=1, source_target_pairs={{0,5},{1,4},{2,7},{3,6},{4,1},{5,0},{6,3},{7,2},{8,13},{9,12},{10,... | collective-permute-start | bytes 884744 | tf_op jit(solution)/shard_map/ppermute | solution.py:455
  19.3 0.5 collective-permute-start.4
  19.8 0.5 collective-permute-start.3
  20.3 2.0 collective-permute-start.12
  22.3 4.0 %collective-permute-done.12 = bf16[32,2048]{1,0:T(8,128)(2,1)S(1)} collective-permute-done((bf16[32,2048]{1,0:T(8,128)(2,1)}, bf16[32,2048]{1,0:T(8,128)(2,1)S(1)}, u32[]{:S(2)}, u32[]{:S(2)}) %collective-permute-start.12) | collective-permute-done | bytes 131104 | tf_op jit(solution)/shard_map/ppermute | solution.py:455
  26.3 3.1 %collective-permute-start.10 = (bf16[32,2048]{1,0:T(8,128)(2,1)}, bf16[32,2048]{1,0:T(8,128)(2,1)S(1)}, u32[]{:S(2)}, u32[]{:S(2)}) collective-permute-start(bf16[32,2048]{1,0:T(8,128)(2,1)} %get-tuple-element.42), channel_id=1, source_target_pairs={{0,8},{1,9},{2,10},{3,11},{4,12},{5,13},{6,14},{7,15},{8,16},{9,17... | collective-permute-start | bytes 393224 | tf_op jit(solution)/shard_map/ppermute | solution.py:455
  29.4 2.2 collective-permute-done.11
  31.7 0.5 collective-permute-start.9
  32.2 0.7 collective-permute-done.4.refs_3_
  32.9 0.1 collective-permute-done.3.refs_2_
  33.0 0.4 collective-permute-start.7
  33.4 0.9 pad_maximum_fusion.refs_4_
  34.4 0.2 collective-permute-start.16
  34.6 2.2 collective-permute-start.15
  36.8 0.8 collective-permute-start.14
  37.6 0.6 collective-permute-start.13
  38.2 0.1 copy-done.19
  38.4 28.7 %attn_forward.1 = (bf16[4608,2048]{1,0:T(8,128)(2,1)}, bf16[4608,512]{1,0:T(8,128)(2,1)}, f32[4608,512]{1,0:T(8,128)}, f32[8,512]{1,0:T(8,128)}, bf16[1024,1152]{1,0:T(8,128)(2,1)}) custom-call(s32[6]{0:T(128)} %stack.38.place, s32[192]{0:T(256)} %frames.1, bf16[4608,512]{1,0:T(8,128)(2,1)} %x_ref.1, bf16[128,1152]{1,0:T(8,128)(2,1)} %copy-done.6, ...), custom_call_target="tpu_custom_call" | custom-call | flops 28991029248 | bytes 42467328 | tf_op jit(solution)/shard_map/attn_forward/pallas_call | solution.py:353
  67.2 0.1 collective-permute-start.17
  67.3 0.5 collective-permute-start.18
  67.8 0.1 collective-permute-start.19
  68.5 0.6 collective-permute-done.17.refs_9_
  69.2 0.7 collective-permute-done.18.refs_10_
  69.9 0.7 collective-permute-done.19.refs_11_
  70.7 0.8 copy-done.13
  71.5 77.7 %feed_forward.1 = (bf16[4608,512]{1,0:T(8,128)(2,1)}, bf16[4608,512]{1,0:T(8,128)(2,1)}, bf16[4,4,32,2304]{3,2,1,0:T(8,128)(2,1)}, bf16[4,4,32,2304]{3,2,1,0:T(8,128)(2,1)}, f32[2,512]{1,0:T(2,128)}) custom-call(s32[6]{0:T(128)} %stack.38.place, s32[1]{0:T(128)S(6)} %copy.26.live, f32[4608,512]{1,0:T(8,128)} %get-tuple-element.38.refs_0_, ...), custom_call_target="tpu_custom_call" | custom-call | flops 57982058496 | bytes 28311552 | tf_op jit(solution)/shard_map/feed_forward/pallas_call | solution.py:379
  149.3 0.2 collective-permute-start.20
  149.5 4.6 %collective-permute-done.20 = bf16[4,4,32,2304]{3,2,1,0:T(8,128)(2,1)S(1)} collective-permute-done((bf16[4,4,32,2304]{3,2,1,0:T(8,128)(2,1)}, bf16[4,4,32,2304]{3,2,1,0:T(8,128)(2,1)S(1)}, u32[]{:S(2)}, u32[]{:S(2)}) %collective-permute-start.20) | collective-permute-done | bytes 2359328 | tf_op jit(solution)/shard_map/ppermute | solution.py:455
  154.1 2.0 fusion.4
  156.1 2.3 %collective-permute-start.27 = (bf16[4,32,2304]{2,1,0:T(8,128)(2,1)S(1)}, bf16[4,32,2304]{2,1,0:T(8,128)(2,1)S(1)}, u32[]{:S(2)}, u32[]{:S(2)}) collective-permute-start(bf16[4,32,2304]{2,1,0:T(8,128)(2,1)S(1)} %get-tuple-element.64), channel_id=1, source_target_pairs={{0,5},{1,4},{2,7},{3,6},{4,1},{5,0},{6,3},{7,2},{8,13},{9,12},{10,... | collective-permute-start | bytes 1769480 | tf_op jit(solution)/shard_map/ppermute | solution.py:455
  158.4 0.6 collective-permute-start.26
  159.1 0.6 collective-permute-start.25
  159.7 36.1 %attn_backward.1 = (f32[4608,512]{1,0:T(8,128)}, bf16[4,4,32,896]{3,2,1,0:T(8,128)(2,1)S(1)}, bf16[4,4,32,896]{3,2,1,0:T(8,128)(2,1)S(1)}) custom-call(s32[6]{0:T(128)S(1)} %copy-done, bf16[4608,512]{1,0:T(8,128)(2,1)S(1)} %bitcast.56, bf16[4608,512]{1,0:T(8,128)(2,1)S(1)} %copy-done.1, bf16[4608,2048]{1,0:T(8,128)(2,1)} %get-tuple-element.52.qkvp_ref, ...), custom_call_target="tpu_custom_call" | custom-call | flops 43486543872 | bytes 42467328 | tf_op jit(solution)/shard_map/attn_backward/pallas_call | solution.py:414
  195.8 1.4 fusion.1
  197.3 1.0 collective-permute-done.21
  198.3 0.2 fusion.11
  198.5 1.4 collective-permute-start.30
  199.9 1.2 collective-permute-start.29
  201.1 0.8 collective-permute-start.28
  201.9 1.4 collective-permute-start.22
  203.3 1.5 collective-permute-start.24
  204.8 1.2 collective-permute-start.23
  206.0 8.5 %collective-permute-done.29 = bf16[32,2304]{1,0:T(8,128)(2,1)S(1)} collective-permute-done((bf16[32,2304]{1,0:T(8,128)(2,1)S(1)}, bf16[32,2304]{1,0:T(8,128)(2,1)S(1)}, u32[]{:S(2)}, u32[]{:S(2)}) %collective-permute-start.29) | collective-permute-done | bytes 147488 | tf_op jit(solution)/shard_map/ppermute | solution.py:455
  214.5 0.1 fusion.9
  214.6 0.7 slice_bitcast_fusion.3
  215.3 0.9 collective-permute-done.23
  216.2 0.2 fusion.7
  216.4 2.6 %collective-permute-start.31 = (bf16[32,896]{1,0:T(8,128)(2,1)S(1)}, bf16[32,896]{1,0:T(8,128)(2,1)S(1)}, u32[]{:S(2)}, u32[]{:S(2)}) collective-permute-start(bf16[32,896]{1,0:T(8,128)(2,1)S(1)} %get-tuple-element.75), channel_id=1, source_target_pairs={{0,8},{1,9},{2,10},{3,11},{4,12},{5,13},{6,14},{7,15},{8,16},{9,17... | collective-permute-start | bytes 172040 | tf_op jit(solution)/shard_map/ppermute | solution.py:455
  218.9 1.3 collective-permute-start.33
  220.2 0.6 collective-permute-start.32
  220.8 0.6 slice_bitcast_fusion.7
  221.5 1.0 collective-permute-done.31
  222.5 1.0 collective-permute-done.33
  223.5 2.5 %collective-permute-done.32 = bf16[32,896]{1,0:T(8,128)(2,1)S(1)} collective-permute-done((bf16[32,896]{1,0:T(8,128)(2,1)S(1)}, bf16[32,896]{1,0:T(8,128)(2,1)S(1)}, u32[]{:S(2)}, u32[]{:S(2)}) %collective-permute-start.32) | collective-permute-done | bytes 57376 | tf_op jit(solution)/shard_map/ppermute | solution.py:455
  226.0 0.7 slice_reduce_fusion
  226.7 0.6 fusion.16
  (69 shorter events, 0.2 us)
Async XLA Ops:
  3.6 8.1 %collective-permute-start.2 = (bf16[32,1152]{1,0:T(8,128)(2,1)}, bf16[32,1152]{1,0:T(8,128)(2,1)S(1)}, u32[]{:S(2)}, u32[]{:S(2)}) collective-permute-start(bf16[32,1152]{1,0:T(8,128)(2,1)} %get-tuple-element.36), channel_id=1, source_target_pairs={{0,24},{1,25},{2,26},{3,27},{4,28},{5,29},{6,30},{7,31},{8,0},{9,1... | collective-permute-start | bytes 221192 | tf_op jit(solution)/shard_map/ppermute | solution.py:455
  8.6 7.2 %collective-permute-start.1 = (bf16[32,1152]{1,0:T(8,128)(2,1)}, bf16[32,1152]{1,0:T(8,128)(2,1)S(1)}, u32[]{:S(2)}, u32[]{:S(2)}) collective-permute-start(bf16[32,1152]{1,0:T(8,128)(2,1)} %get-tuple-element.36), channel_id=1, source_target_pairs={{0,16},{1,17},{2,18},{3,19},{4,20},{5,21},{6,22},{7,23},{8,24},{9,... | collective-permute-start | bytes 221192 | tf_op jit(solution)/shard_map/ppermute | solution.py:455
  8.6 7.2 %collective-permute-start = (bf16[32,1152]{1,0:T(8,128)(2,1)}, bf16[32,1152]{1,0:T(8,128)(2,1)S(1)}, u32[]{:S(2)}, u32[]{:S(2)}) collective-permute-start(bf16[32,1152]{1,0:T(8,128)(2,1)} %get-tuple-element.36), channel_id=1, source_target_pairs={{0,8},{1,9},{2,10},{3,11},{4,12},{5,13},{6,14},{7,15},{8,16},{9,17... | collective-permute-start | bytes 221192 | tf_op jit(solution)/shard_map/ppermute | solution.py:455
  16.7 21.6 %copy-start.6 = (bf16[128,1152]{1,0:T(8,128)(2,1)}, bf16[128,1152]{1,0:T(8,128)(2,1)S(1)}, u32[]{:S(2)}) copy-start(bf16[128,1152]{1,0:T(8,128)(2,1)S(1)} %pad_maximum_fusion.1.refs_1_) | copy-start | bytes 884740
  16.8 14.9 %collective-permute-start.5 = (bf16[128,1152]{1,0:T(8,128)(2,1)S(1)}, bf16[128,1152]{1,0:T(8,128)(2,1)S(1)}, u32[]{:S(2)}, u32[]{:S(2)}) collective-permute-start(bf16[128,1152]{1,0:T(8,128)(2,1)S(1)} %pad_maximum_fusion.1.refs_1_), channel_id=1, source_target_pairs={{0,5},{1,4},{2,7},{3,6},{4,1},{5,0},{6,3},{7,2},{8,13},{9,12},{10,... | collective-permute-start | bytes 884744 | tf_op jit(solution)/shard_map/ppermute | solution.py:455
  19.3 13.6 %collective-permute-start.4 = (bf16[128,1152]{1,0:T(8,128)(2,1)S(1)}, bf16[128,1152]{1,0:T(8,128)(2,1)S(1)}, u32[]{:S(2)}, u32[]{:S(2)}) collective-permute-start(bf16[128,1152]{1,0:T(8,128)(2,1)S(1)} %pad_maximum_fusion.1.refs_1_), channel_id=1, source_target_pairs={{0,1},{1,0},{2,3},{3,2},{4,5},{5,4},{6,7},{7,6},{8,9},{9,8},{10,11... | collective-permute-start | bytes 884744 | tf_op jit(solution)/shard_map/ppermute | solution.py:455
  19.8 13.2 %collective-permute-start.3 = (bf16[128,1152]{1,0:T(8,128)(2,1)S(1)}, bf16[128,1152]{1,0:T(8,128)(2,1)S(1)}, u32[]{:S(2)}, u32[]{:S(2)}) collective-permute-start(bf16[128,1152]{1,0:T(8,128)(2,1)S(1)} %pad_maximum_fusion.1.refs_1_), channel_id=1, source_target_pairs={{0,4},{1,5},{2,6},{3,7},{4,0},{5,1},{6,2},{7,3},{8,12},{9,13},{10,... | collective-permute-start | bytes 884744 | tf_op jit(solution)/shard_map/ppermute | solution.py:455
  20.3 5.9 %collective-permute-start.12 = (bf16[32,2048]{1,0:T(8,128)(2,1)}, bf16[32,2048]{1,0:T(8,128)(2,1)S(1)}, u32[]{:S(2)}, u32[]{:S(2)}) collective-permute-start(bf16[32,2048]{1,0:T(8,128)(2,1)} %get-tuple-element.42), channel_id=1, source_target_pairs={{0,24},{1,25},{2,26},{3,27},{4,28},{5,29},{6,30},{7,31},{8,0},{9,1... | collective-permute-start | bytes 393224 | tf_op jit(solution)/shard_map/ppermute | solution.py:455
  22.3 9.3 %collective-permute-start.11 = (bf16[32,2048]{1,0:T(8,128)(2,1)}, bf16[32,2048]{1,0:T(8,128)(2,1)S(1)}, u32[]{:S(2)}, u32[]{:S(2)}) collective-permute-start(bf16[32,2048]{1,0:T(8,128)(2,1)} %get-tuple-element.42), channel_id=1, source_target_pairs={{0,16},{1,17},{2,18},{3,19},{4,20},{5,21},{6,22},{7,23},{8,24},{9,... | collective-permute-start | bytes 393224 | tf_op jit(solution)/shard_map/ppermute | solution.py:455
  26.3 7.2 %collective-permute-start.10 = (bf16[32,2048]{1,0:T(8,128)(2,1)}, bf16[32,2048]{1,0:T(8,128)(2,1)S(1)}, u32[]{:S(2)}, u32[]{:S(2)}) collective-permute-start(bf16[32,2048]{1,0:T(8,128)(2,1)} %get-tuple-element.42), channel_id=1, source_target_pairs={{0,8},{1,9},{2,10},{3,11},{4,12},{5,13},{6,14},{7,15},{8,16},{9,17... | collective-permute-start | bytes 393224 | tf_op jit(solution)/shard_map/ppermute | solution.py:455
  31.6 2.9 %collective-permute-start.6 = (bf16[128,1152]{1,0:T(8,128)(2,1)S(1)}, bf16[128,1152]{1,0:T(8,128)(2,1)S(1)}, u32[]{:S(2)}, u32[]{:S(2)}) collective-permute-start(bf16[128,1152]{1,0:T(8,128)(2,1)S(1)} %pad_maximum_fusion.1.refs_1_), channel_id=1, source_target_pairs={{0,2},{1,3},{2,0},{3,1},{4,6},{5,7},{6,4},{7,5},{8,10},{9,11},{10,... | collective-permute-start | bytes 884744 | tf_op jit(solution)/shard_map/ppermute | solution.py:455
  31.6 5.2 %copy-start.14 = (bf16[128,1152]{1,0:T(8,128)(2,1)}, bf16[128,1152]{1,0:T(8,128)(2,1)S(1)}, u32[]{:S(2)}) copy-start(bf16[128,1152]{1,0:T(8,128)(2,1)S(1)} %collective-permute-done.5.refs_4_) | copy-start | bytes 884740
  31.7 5.2 %collective-permute-start.9 = (bf16[128,1152]{1,0:T(8,128)(2,1)S(1)}, bf16[128,1152]{1,0:T(8,128)(2,1)S(1)}, u32[]{:S(2)}, u32[]{:S(2)}) collective-permute-start(bf16[128,1152]{1,0:T(8,128)(2,1)S(1)} %collective-permute-done.5.refs_4_), channel_id=1, source_target_pairs={{0,2},{1,3},{2,0},{3,1},{4,6},{5,7},{6,4},{7,5},{8,10},{9,11},{10,... | collective-permute-start | bytes 884744 | tf_op jit(solution)/shard_map/ppermute | solution.py:455
  32.9 4.7 %copy-start.15 = (bf16[128,1152]{1,0:T(8,128)(2,1)}, bf16[128,1152]{1,0:T(8,128)(2,1)S(1)}, u32[]{:S(2)}) copy-start(bf16[128,1152]{1,0:T(8,128)(2,1)S(1)} %collective-permute-done.4.refs_3_) | copy-start | bytes 884740
  32.9 4.7 %collective-permute-start.8 = (bf16[128,1152]{1,0:T(8,128)(2,1)S(1)}, bf16[128,1152]{1,0:T(8,128)(2,1)S(1)}, u32[]{:S(2)}, u32[]{:S(2)}) collective-permute-start(bf16[128,1152]{1,0:T(8,128)(2,1)S(1)} %collective-permute-done.4.refs_3_), channel_id=1, source_target_pairs={{0,2},{1,3},{2,0},{3,1},{4,6},{5,7},{6,4},{7,5},{8,10},{9,11},{10,... | collective-permute-start | bytes 884744 | tf_op jit(solution)/shard_map/ppermute | solution.py:455
  33.0 5.2 %copy-start.16 = (bf16[128,1152]{1,0:T(8,128)(2,1)}, bf16[128,1152]{1,0:T(8,128)(2,1)S(1)}, u32[]{:S(2)}) copy-start(bf16[128,1152]{1,0:T(8,128)(2,1)S(1)} %collective-permute-done.3.refs_2_) | copy-start | bytes 884740
  33.0 5.4 %collective-permute-start.7 = (bf16[128,1152]{1,0:T(8,128)(2,1)S(1)}, bf16[128,1152]{1,0:T(8,128)(2,1)}, u32[]{:S(2)}, u32[]{:S(2)}) collective-permute-start(bf16[128,1152]{1,0:T(8,128)(2,1)S(1)} %collective-permute-done.3.refs_2_), channel_id=1, source_target_pairs={{0,2},{1,3},{2,0},{3,1},{4,6},{5,7},{6,4},{7,5},{8,10},{9,11},{10,... | collective-permute-start | bytes 884744 | tf_op jit(solution)/shard_map/ppermute | solution.py:455
  34.4 32.8 %copy-start.5 = (bf16[128,2048]{1,0:T(8,128)(2,1)}, bf16[128,2048]{1,0:T(8,128)(2,1)S(1)}, u32[]{:S(2)}) copy-start(bf16[128,2048]{1,0:T(8,128)(2,1)S(1)} %pad_maximum_fusion.refs_4_) | copy-start | bytes 1572868
  34.4 34.1 %collective-permute-start.16 = (bf16[128,2048]{1,0:T(8,128)(2,1)S(1)}, bf16[128,2048]{1,0:T(8,128)(2,1)S(1)}, u32[]{:S(2)}, u32[]{:S(2)}) collective-permute-start(bf16[128,2048]{1,0:T(8,128)(2,1)S(1)} %pad_maximum_fusion.refs_4_), channel_id=1, source_target_pairs={{0,2},{1,3},{2,0},{3,1},{4,6},{5,7},{6,4},{7,5},{8,10},{9,11},{10,... | collective-permute-start | bytes 1572872 | tf_op jit(solution)/shard_map/ppermute | solution.py:455
  34.6 3.1 %copy-start.17 = (bf16[128,1152]{1,0:T(8,128)(2,1)}, bf16[128,1152]{1,0:T(8,128)(2,1)S(1)}, u32[]{:S(2)}) copy-start(bf16[128,1152]{1,0:T(8,128)(2,1)S(1)} %collective-permute-done.6.refs_5_) | copy-start | bytes 884740
  34.6 32.6 %collective-permute-start.15 = (bf16[128,2048]{1,0:T(8,128)(2,1)S(1)}, bf16[128,2048]{1,0:T(8,128)(2,1)S(1)}, u32[]{:S(2)}, u32[]{:S(2)}) collective-permute-start(bf16[128,2048]{1,0:T(8,128)(2,1)S(1)} %pad_maximum_fusion.refs_4_), channel_id=1, source_target_pairs={{0,5},{1,4},{2,7},{3,6},{4,1},{5,0},{6,3},{7,2},{8,13},{9,12},{10,... | collective-permute-start | bytes 1572872 | tf_op jit(solution)/shard_map/ppermute | solution.py:455
  36.8 1.4 copy-start.18
  36.8 30.4 %collective-permute-start.14 = (bf16[128,2048]{1,0:T(8,128)(2,1)S(1)}, bf16[128,2048]{1,0:T(8,128)(2,1)S(1)}, u32[]{:S(2)}, u32[]{:S(2)}) collective-permute-start(bf16[128,2048]{1,0:T(8,128)(2,1)S(1)} %pad_maximum_fusion.refs_4_), channel_id=1, source_target_pairs={{0,1},{1,0},{2,3},{3,2},{4,5},{5,4},{6,7},{7,6},{8,9},{9,8},{10,11... | collective-permute-start | bytes 1572872 | tf_op jit(solution)/shard_map/ppermute | solution.py:455
  37.6 0.7 copy-start.19
  37.6 29.5 %collective-permute-start.13 = (bf16[128,2048]{1,0:T(8,128)(2,1)S(1)}, bf16[128,2048]{1,0:T(8,128)(2,1)S(1)}, u32[]{:S(2)}, u32[]{:S(2)}) collective-permute-start(bf16[128,2048]{1,0:T(8,128)(2,1)S(1)} %pad_maximum_fusion.refs_4_), channel_id=1, source_target_pairs={{0,4},{1,5},{2,6},{3,7},{4,0},{5,1},{6,2},{7,3},{8,12},{9,13},{10,... | collective-permute-start | bytes 1572872 | tf_op jit(solution)/shard_map/ppermute | solution.py:455
  38.4 121.3 %slice-start = ((s8[4718592]{0:T(1024)(128)(4,1)}), s8[524288]{0:T(1024)(128)(4,1)S(1)}, s32[]{:S(2)}) async-start(s8[4718592]{0:T(1024)(128)(4,1)} %bitcast.55), calls=%async_computation | async-start | bytes 1048576
  67.2 3.5 %copy-start.8 = (bf16[128,2048]{1,0:T(8,128)(2,1)}, bf16[128,2048]{1,0:T(8,128)(2,1)S(1)}, u32[]{:S(2)}) copy-start(bf16[128,2048]{1,0:T(8,128)(2,1)S(1)} %collective-permute-done.15.refs_7_) | copy-start | bytes 1572868
  67.2 3.5 %copy-start.9 = (bf16[128,2048]{1,0:T(8,128)(2,1)}, bf16[128,2048]{1,0:T(8,128)(2,1)S(1)}, u32[]{:S(2)}) copy-start(bf16[128,2048]{1,0:T(8,128)(2,1)S(1)} %collective-permute-done.14.refs_6_) | copy-start | bytes 1572868
  67.2 3.5 %copy-start.10 = (bf16[128,2048]{1,0:T(8,128)(2,1)}, bf16[128,2048]{1,0:T(8,128)(2,1)S(1)}, u32[]{:S(2)}) copy-start(bf16[128,2048]{1,0:T(8,128)(2,1)S(1)} %collective-permute-done.13.refs_5_) | copy-start | bytes 1572868
  67.2 2.0 collective-permute-start.17
  67.3 2.6 %collective-permute-start.18 = (bf16[128,2048]{1,0:T(8,128)(2,1)S(1)}, bf16[128,2048]{1,0:T(8,128)(2,1)S(1)}, u32[]{:S(2)}, u32[]{:S(2)}) collective-permute-start(bf16[128,2048]{1,0:T(8,128)(2,1)S(1)} %collective-permute-done.14.refs_6_), channel_id=1, source_target_pairs={{0,2},{1,3},{2,0},{3,1},{4,6},{5,7},{6,4},{7,5},{8,10},{9,11},{10,... | collective-permute-start | bytes 1572872 | tf_op jit(solution)/shard_map/ppermute | solution.py:455
  67.8 2.9 %collective-permute-start.19 = (bf16[128,2048]{1,0:T(8,128)(2,1)S(1)}, bf16[128,2048]{1,0:T(8,128)(2,1)S(1)}, u32[]{:S(2)}, u32[]{:S(2)}) collective-permute-start(bf16[128,2048]{1,0:T(8,128)(2,1)S(1)} %collective-permute-done.15.refs_7_), channel_id=1, source_target_pairs={{0,2},{1,3},{2,0},{3,1},{4,6},{5,7},{6,4},{7,5},{8,10},{9,11},{10,... | collective-permute-start | bytes 1572872 | tf_op jit(solution)/shard_map/ppermute | solution.py:455
  68.5 2.2 copy-start.7
  69.2 1.5 copy-start.11
  69.9 0.8 copy-start.12
  70.7 0.8 copy-start.13
  71.5 88.1 %slice-start.1 = ((s8[4718592]{0:T(1024)(128)(4,1)}), s8[4194304]{0:T(1024)(128)(4,1)S(1)}, s32[]{:S(2)}) async-start(s8[4718592]{0:T(1024)(128)(4,1)} %bitcast.55), calls=%async_computation.1 | async-start | bytes 8388608
  71.5 88.1 %copy-start.2 = (bf16[1024,1152]{1,0:T(8,128)(2,1)S(1)}, bf16[1024,1152]{1,0:T(8,128)(2,1)}, u32[]{:S(2)}) copy-start(bf16[1024,1152]{1,0:T(8,128)(2,1)} %get-tuple-element.53.w_ref) | copy-start | bytes 7077892
  149.3 4.8 %collective-permute-start.20 = (bf16[4,4,32,2304]{3,2,1,0:T(8,128)(2,1)}, bf16[4,4,32,2304]{3,2,1,0:T(8,128)(2,1)S(1)}, u32[]{:S(2)}, u32[]{:S(2)}) collective-permute-start(bf16[4,4,32,2304]{3,2,1,0:T(8,128)(2,1)} %get-tuple-element.50), channel_id=1, source_target_pairs={{0,2},{1,3},{2,0},{3,1},{4,6},{5,7},{6,4},{7,5},{8,10},{9,11},{10,... | collective-permute-start | bytes 7077896 | tf_op jit(solution)/shard_map/ppermute | solution.py:455
  154.1 5.6 %copy-start = (s32[6]{0:T(128)S(1)}, s32[6]{0:T(128)}, u32[]{:S(2)}) copy-start(s32[6]{0:T(128)} %stack.38.place) | copy-start | bytes 76
  154.1 5.6 %copy-start.1 = (bf16[4608,512]{1,0:T(8,128)(2,1)S(1)}, bf16[4608,512]{1,0:T(8,128)(2,1)}, u32[]{:S(2)}) copy-start(bf16[4608,512]{1,0:T(8,128)(2,1)} %get-tuple-element.51.gh_ref) | copy-start | bytes 14155780
  154.1 5.6 %copy-start.3 = (f32[8,512]{1,0:T(8,128)S(1)}, f32[8,512]{1,0:T(8,128)}, u32[]{:S(2)}) copy-start(f32[8,512]{1,0:T(8,128)} %get-tuple-element.40.refs_3_.vec_ref) | copy-start | bytes 49156
  154.1 5.6 %copy-start.4 = (f32[2,512]{1,0:T(2,128)S(1)}, f32[2,512]{1,0:T(2,128)}, u32[]{:S(2)}) copy-start(f32[2,512]{1,0:T(2,128)} %get-tuple-element.54.gvtwo_ref) | copy-start | bytes 12292
  156.1 39.7 %collective-permute-start.27 = (bf16[4,32,2304]{2,1,0:T(8,128)(2,1)S(1)}, bf16[4,32,2304]{2,1,0:T(8,128)(2,1)S(1)}, u32[]{:S(2)}, u32[]{:S(2)}) collective-permute-start(bf16[4,32,2304]{2,1,0:T(8,128)(2,1)S(1)} %get-tuple-element.64), channel_id=1, source_target_pairs={{0,5},{1,4},{2,7},{3,6},{4,1},{5,0},{6,3},{7,2},{8,13},{9,12},{10,... | collective-permute-start | bytes 1769480 | tf_op jit(solution)/shard_map/ppermute | solution.py:455
  158.4 37.4 %collective-permute-start.26 = (bf16[4,32,2304]{2,1,0:T(8,128)(2,1)S(1)}, bf16[4,32,2304]{2,1,0:T(8,128)(2,1)S(1)}, u32[]{:S(2)}, u32[]{:S(2)}) collective-permute-start(bf16[4,32,2304]{2,1,0:T(8,128)(2,1)S(1)} %get-tuple-element.65), channel_id=1, source_target_pairs={{0,1},{1,0},{2,3},{3,2},{4,5},{5,4},{6,7},{7,6},{8,9},{9,8},{10,11... | collective-permute-start | bytes 1769480 | tf_op jit(solution)/shard_map/ppermute | solution.py:455
  159.1 36.8 %collective-permute-start.25 = (bf16[4,32,2304]{2,1,0:T(8,128)(2,1)S(1)}, bf16[4,32,2304]{2,1,0:T(8,128)(2,1)S(1)}, u32[]{:S(2)}, u32[]{:S(2)}) collective-permute-start(bf16[4,32,2304]{2,1,0:T(8,128)(2,1)S(1)} %get-tuple-element.66), channel_id=1, source_target_pairs={{0,4},{1,5},{2,6},{3,7},{4,0},{5,1},{6,2},{7,3},{8,12},{9,13},{10,... | collective-permute-start | bytes 1769480 | tf_op jit(solution)/shard_map/ppermute | solution.py:455
  195.8 2.5 %collective-permute-start.21 = (bf16[4,4,32,896]{3,2,1,0:T(8,128)(2,1)S(1)}, bf16[4,4,32,896]{3,2,1,0:T(8,128)(2,1)S(1)}, u32[]{:S(2)}, u32[]{:S(2)}) collective-permute-start(bf16[4,4,32,896]{3,2,1,0:T(8,128)(2,1)S(1)} %get-tuple-element.57), channel_id=1, source_target_pairs={{0,2},{1,3},{2,0},{3,1},{4,6},{5,7},{6,4},{7,5},{8,10},{9,11},{10,... | collective-permute-start | bytes 2752520 | tf_op jit(solution)/shard_map/ppermute | solution.py:455
  198.5 6.3 %collective-permute-start.30 = (bf16[32,2304]{1,0:T(8,128)(2,1)S(1)}, bf16[32,2304]{1,0:T(8,128)(2,1)S(1)}, u32[]{:S(2)}, u32[]{:S(2)}) collective-permute-start(bf16[32,2304]{1,0:T(8,128)(2,1)S(1)} %get-tuple-element.70), channel_id=1, source_target_pairs={{0,24},{1,25},{2,26},{3,27},{4,28},{5,29},{6,30},{7,31},{8,0},{9,1... | collective-permute-start | bytes 442376 | tf_op jit(solution)/shard_map/ppermute | solution.py:455
  199.9 14.5 %collective-permute-start.29 = (bf16[32,2304]{1,0:T(8,128)(2,1)S(1)}, bf16[32,2304]{1,0:T(8,128)(2,1)S(1)}, u32[]{:S(2)}, u32[]{:S(2)}) collective-permute-start(bf16[32,2304]{1,0:T(8,128)(2,1)S(1)} %get-tuple-element.71), channel_id=1, source_target_pairs={{0,16},{1,17},{2,18},{3,19},{4,20},{5,21},{6,22},{7,23},{8,24},{9,... | collective-permute-start | bytes 442376 | tf_op jit(solution)/shard_map/ppermute | solution.py:455
  201.1 13.3 %collective-permute-start.28 = (bf16[32,2304]{1,0:T(8,128)(2,1)S(1)}, bf16[32,2304]{1,0:T(8,128)(2,1)S(1)}, u32[]{:S(2)}, u32[]{:S(2)}) collective-permute-start(bf16[32,2304]{1,0:T(8,128)(2,1)S(1)} %get-tuple-element.72), channel_id=1, source_target_pairs={{0,8},{1,9},{2,10},{3,11},{4,12},{5,13},{6,14},{7,15},{8,16},{9,17... | collective-permute-start | bytes 442376 | tf_op jit(solution)/shard_map/ppermute | solution.py:455
  201.9 13.4 %collective-permute-start.22 = (bf16[4,32,896]{2,1,0:T(8,128)(2,1)S(1)}, bf16[4,32,896]{2,1,0:T(8,128)(2,1)S(1)}, u32[]{:S(2)}, u32[]{:S(2)}) collective-permute-start(bf16[4,32,896]{2,1,0:T(8,128)(2,1)S(1)} %get-tuple-element.67), channel_id=1, source_target_pairs={{0,4},{1,5},{2,6},{3,7},{4,0},{5,1},{6,2},{7,3},{8,12},{9,13},{10,... | collective-permute-start | bytes 688136 | tf_op jit(solution)/shard_map/ppermute | solution.py:455
  203.3 12.0 %collective-permute-start.24 = (bf16[4,32,896]{2,1,0:T(8,128)(2,1)S(1)}, bf16[4,32,896]{2,1,0:T(8,128)(2,1)S(1)}, u32[]{:S(2)}, u32[]{:S(2)}) collective-permute-start(bf16[4,32,896]{2,1,0:T(8,128)(2,1)S(1)} %get-tuple-element.68), channel_id=1, source_target_pairs={{0,5},{1,4},{2,7},{3,6},{4,1},{5,0},{6,3},{7,2},{8,13},{9,12},{10,... | collective-permute-start | bytes 688136 | tf_op jit(solution)/shard_map/ppermute | solution.py:455
  204.8 11.4 %collective-permute-start.23 = (bf16[4,32,896]{2,1,0:T(8,128)(2,1)S(1)}, bf16[4,32,896]{2,1,0:T(8,128)(2,1)S(1)}, u32[]{:S(2)}, u32[]{:S(2)}) collective-permute-start(bf16[4,32,896]{2,1,0:T(8,128)(2,1)S(1)} %get-tuple-element.69), channel_id=1, source_target_pairs={{0,1},{1,0},{2,3},{3,2},{4,5},{5,4},{6,7},{7,6},{8,9},{9,8},{10,11... | collective-permute-start | bytes 688136 | tf_op jit(solution)/shard_map/ppermute | solution.py:455
  216.4 6.1 %collective-permute-start.31 = (bf16[32,896]{1,0:T(8,128)(2,1)S(1)}, bf16[32,896]{1,0:T(8,128)(2,1)S(1)}, u32[]{:S(2)}, u32[]{:S(2)}) collective-permute-start(bf16[32,896]{1,0:T(8,128)(2,1)S(1)} %get-tuple-element.75), channel_id=1, source_target_pairs={{0,8},{1,9},{2,10},{3,11},{4,12},{5,13},{6,14},{7,15},{8,16},{9,17... | collective-permute-start | bytes 172040 | tf_op jit(solution)/shard_map/ppermute | solution.py:455
  218.9 4.5 %collective-permute-start.33 = (bf16[32,896]{1,0:T(8,128)(2,1)S(1)}, bf16[32,896]{1,0:T(8,128)(2,1)S(1)}, u32[]{:S(2)}, u32[]{:S(2)}) collective-permute-start(bf16[32,896]{1,0:T(8,128)(2,1)S(1)} %get-tuple-element.76), channel_id=1, source_target_pairs={{0,24},{1,25},{2,26},{3,27},{4,28},{5,29},{6,30},{7,31},{8,0},{9,1... | collective-permute-start | bytes 172040 | tf_op jit(solution)/shard_map/ppermute | solution.py:455
  220.2 5.7 %collective-permute-start.32 = (bf16[32,896]{1,0:T(8,128)(2,1)S(1)}, bf16[32,896]{1,0:T(8,128)(2,1)S(1)}, u32[]{:S(2)}, u32[]{:S(2)}) collective-permute-start(bf16[32,896]{1,0:T(8,128)(2,1)S(1)} %get-tuple-element.77), channel_id=1, source_target_pairs={{0,16},{1,17},{2,18},{3,19},{4,20},{5,21},{6,22},{7,23},{8,24},{9,... | collective-permute-start | bytes 172040 | tf_op jit(solution)/shard_map/ppermute | solution.py:455

commit v7 on v6

--- a/solution.py
+++ b/solution.py
@@ -220,8 +220,9 @@
             sq = up * up
             th = jnp.tanh(up * (GELU_A + (GELU_A * GELU_B) * sq))
             half = 0.5 + 0.5 * th
-            act_ref[:, cols] = (up * half).astype(BF)
-            slope = half + (0.5 * up) * (1.0 - th * th) * (GELU_A + (3.0 * GELU_A * GELU_B) * sq)
+            act = up * half
+            act_ref[:, cols] = act.astype(BF)
+            slope = half + (act - act * half) * (2.0 * GELU_A + (6.0 * GELU_A * GELU_B) * sq)
             gup_ref[:, cols] = (ga * slope).astype(BF)
     down = jnp.zeros((rows, D), F32)
     gy = jnp.zeros((rows, D), F32)

time: 228 us -> 228 us (level)
  no operation moved by 1% of the time
where the time goes in v7:
time: 228 us; the launch traced here: 227 us
  Pallas kernels  144 us (63%)
  starting transfers between devices  35.9 us (16%)
  waiting for transfers between devices  34.3 us (15%)
  other arithmetic  6.98 us (3%)
  local copies, waits for them, and re-layouts  4.36 us (2%)
    pallas_call x1, Pallas kernels, feed_forward(): pl.pallas_call(lambda place, live, *refs: feed_forward_kernel(place, live...  77.7 us
    pallas_call x1, Pallas kernels, attn_backward(): pl.pallas_call(attn_backward_kernel, grid_spec=pltpu.PrefetchScalarGridSp...  36.1 us
    ppermute x34, starting transfers between devices, send(): return lax.ppermute(value, both, pairs)  35.9 us
    ppermute x34, waiting for transfers between devices, send(): return lax.ppermute(value, both, pairs)  34.3 us
    pallas_call x1, Pallas kernels, attn_forward(): pl.pallas_call(lambda place, frames, *refs: attn_forward_kernel(place, fr...  28.7 us
  transfers between devices with their start and end apart: 34, of which 16 were waited for; matrix products, arithmetic and copies ran while one was open for 2% of the time, Pallas kernels for 29%

profile of v7, /device:TPU:0, one launch (start us, length us, event | category | flops | bytes accessed | tf_op | source)
XLA Modules:
  0.0 227.3 jit_solution(15452479764077341858)
XLA Ops:
  0.6 1.3 pad_maximum_fusion.2.vec_ref
  1.9 1.7 pack.1
  3.6 5.0 %collective-permute-start.2 = (bf16[32,1152]{1,0:T(8,128)(2,1)}, bf16[32,1152]{1,0:T(8,128)(2,1)S(1)}, u32[]{:S(2)}, u32[]{:S(2)}) collective-permute-start(bf16[32,1152]{1,0:T(8,128)(2,1)} %get-tuple-element.36), channel_id=1, source_target_pairs={{0,24},{1,25},{2,26},{3,27},{4,28},{5,29},{6,30},{7,31},{8,0},{9,1... | collective-permute-start | bytes 221192 | tf_op jit(solution)/shard_map/ppermute | solution.py:456
  8.6 1.0 collective-permute-start
  9.6 0.6 stack.38.place
  10.2 1.4 collective-permute-done.2
  11.7 4.2 %collective-permute-done.1 = bf16[32,1152]{1,0:T(8,128)(2,1)S(1)} collective-permute-done((bf16[32,1152]{1,0:T(8,128)(2,1)}, bf16[32,1152]{1,0:T(8,128)(2,1)S(1)}, u32[]{:S(2)}, u32[]{:S(2)}) %collective-permute-start.1) | collective-permute-done | bytes 73760 | tf_op jit(solution)/shard_map/ppermute | solution.py:456
  15.8 0.9 pad_maximum_fusion.1.refs_1_
  16.8 2.5 %collective-permute-start.5 = (bf16[128,1152]{1,0:T(8,128)(2,1)S(1)}, bf16[128,1152]{1,0:T(8,128)(2,1)S(1)}, u32[]{:S(2)}, u32[]{:S(2)}) collective-permute-start(bf16[128,1152]{1,0:T(8,128)(2,1)S(1)} %pad_maximum_fusion.1.refs_1_), channel_id=1, source_target_pairs={{0,5},{1,4},{2,7},{3,6},{4,1},{5,0},{6,3},{7,2},{8,13},{9,12},{10,... | collective-permute-start | bytes 884744 | tf_op jit(solution)/shard_map/ppermute | solution.py:456
  19.3 0.5 collective-permute-start.4
  19.8 0.5 collective-permute-start.3
  20.3 2.0 collective-permute-start.12
  22.3 4.0 %collective-permute-done.12 = bf16[32,2048]{1,0:T(8,128)(2,1)S(1)} collective-permute-done((bf16[32,2048]{1,0:T(8,128)(2,1)}, bf16[32,2048]{1,0:T(8,128)(2,1)S(1)}, u32[]{:S(2)}, u32[]{:S(2)}) %collective-permute-start.12) | collective-permute-done | bytes 131104 | tf_op jit(solution)/shard_map/ppermute | solution.py:456
  26.3 3.1 %collective-permute-start.10 = (bf16[32,2048]{1,0:T(8,128)(2,1)}, bf16[32,2048]{1,0:T(8,128)(2,1)S(1)}, u32[]{:S(2)}, u32[]{:S(2)}) collective-permute-start(bf16[32,2048]{1,0:T(8,128)(2,1)} %get-tuple-element.42), channel_id=1, source_target_pairs={{0,8},{1,9},{2,10},{3,11},{4,12},{5,13},{6,14},{7,15},{8,16},{9,17... | collective-permute-start | bytes 393224 | tf_op jit(solution)/shard_map/ppermute | solution.py:456
  29.4 2.2 collective-permute-done.11
  31.7 0.5 collective-permute-start.9
  32.2 0.7 collective-permute-done.4.refs_3_
  32.9 0.1 collective-permute-done.3.refs_2_
  33.0 0.4 collective-permute-start.7
  33.4 0.9 pad_maximum_fusion.refs_4_
  34.4 0.2 collective-permute-start.16
  34.6 2.2 collective-permute-start.15
  36.8 0.8 collective-permute-start.14
  37.6 0.6 collective-permute-start.13
  38.2 0.1 copy-done.19
  38.4 28.7 %attn_forward.1 = (bf16[4608,2048]{1,0:T(8,128)(2,1)}, bf16[4608,512]{1,0:T(8,128)(2,1)}, f32[4608,512]{1,0:T(8,128)}, f32[8,512]{1,0:T(8,128)}, bf16[1024,1152]{1,0:T(8,128)(2,1)}) custom-call(s32[6]{0:T(128)} %stack.38.place, s32[192]{0:T(256)} %frames.1, bf16[4608,512]{1,0:T(8,128)(2,1)} %x_ref.1, bf16[128,1152]{1,0:T(8,128)(2,1)} %copy-done.6, ...), custom_call_target="tpu_custom_call" | custom-call | flops 28991029248 | bytes 42467328 | tf_op jit(solution)/shard_map/attn_forward/pallas_call | solution.py:354
  67.2 0.1 collective-permute-start.17
  67.3 0.5 collective-permute-start.18
  67.8 0.1 collective-permute-start.19
  68.5 0.6 collective-permute-done.17.refs_9_
  69.2 0.7 collective-permute-done.18.refs_10_
  69.9 0.7 collective-permute-done.19.refs_11_
  70.7 0.8 copy-done.13
  71.5 77.7 %feed_forward.1 = (bf16[4608,512]{1,0:T(8,128)(2,1)}, bf16[4608,512]{1,0:T(8,128)(2,1)}, bf16[4,4,32,2304]{3,2,1,0:T(8,128)(2,1)}, bf16[4,4,32,2304]{3,2,1,0:T(8,128)(2,1)}, f32[2,512]{1,0:T(2,128)}) custom-call(s32[6]{0:T(128)} %stack.38.place, s32[1]{0:T(128)S(6)} %copy.26.live, f32[4608,512]{1,0:T(8,128)} %get-tuple-element.38.refs_0_, ...), custom_call_target="tpu_custom_call" | custom-call | flops 57982058496 | bytes 28311552 | tf_op jit(solution)/shard_map/feed_forward/pallas_call | solution.py:380
  149.2 0.2 collective-permute-start.20
  149.4 4.6 %collective-permute-done.20 = bf16[4,4,32,2304]{3,2,1,0:T(8,128)(2,1)S(1)} collective-permute-done((bf16[4,4,32,2304]{3,2,1,0:T(8,128)(2,1)}, bf16[4,4,32,2304]{3,2,1,0:T(8,128)(2,1)S(1)}, u32[]{:S(2)}, u32[]{:S(2)}) %collective-permute-start.20) | collective-permute-done | bytes 2359328 | tf_op jit(solution)/shard_map/ppermute | solution.py:456
  154.0 2.0 fusion.4
  156.0 2.3 %collective-permute-start.27 = (bf16[4,32,2304]{2,1,0:T(8,128)(2,1)S(1)}, bf16[4,32,2304]{2,1,0:T(8,128)(2,1)S(1)}, u32[]{:S(2)}, u32[]{:S(2)}) collective-permute-start(bf16[4,32,2304]{2,1,0:T(8,128)(2,1)S(1)} %get-tuple-element.64), channel_id=1, source_target_pairs={{0,5},{1,4},{2,7},{3,6},{4,1},{5,0},{6,3},{7,2},{8,13},{9,12},{10,... | collective-permute-start | bytes 1769480 | tf_op jit(solution)/shard_map/ppermute | solution.py:456
  158.4 0.6 collective-permute-start.26
  159.0 0.6 collective-permute-start.25
  159.6 36.1 %attn_backward.1 = (f32[4608,512]{1,0:T(8,128)}, bf16[4,4,32,896]{3,2,1,0:T(8,128)(2,1)S(1)}, bf16[4,4,32,896]{3,2,1,0:T(8,128)(2,1)S(1)}) custom-call(s32[6]{0:T(128)S(1)} %copy-done, bf16[4608,512]{1,0:T(8,128)(2,1)S(1)} %bitcast.56, bf16[4608,512]{1,0:T(8,128)(2,1)S(1)} %copy-done.1, bf16[4608,2048]{1,0:T(8,128)(2,1)} %get-tuple-element.52.qkvp_ref, ...), custom_call_target="tpu_custom_call" | custom-call | flops 43486543872 | bytes 42467328 | tf_op jit(solution)/shard_map/attn_backward/pallas_call | solution.py:415
  195.8 1.4 fusion.1
  197.2 1.0 collective-permute-done.21
  198.2 0.2 fusion.11
  198.4 1.4 collective-permute-start.30
  199.9 1.2 collective-permute-start.29
  201.1 0.8 collective-permute-start.28
  201.9 1.4 collective-permute-start.22
  203.3 1.5 collective-permute-start.24
  204.7 1.2 collective-permute-start.23
  205.9 8.5 %collective-permute-done.29 = bf16[32,2304]{1,0:T(8,128)(2,1)S(1)} collective-permute-done((bf16[32,2304]{1,0:T(8,128)(2,1)S(1)}, bf16[32,2304]{1,0:T(8,128)(2,1)S(1)}, u32[]{:S(2)}, u32[]{:S(2)}) %collective-permute-start.29) | collective-permute-done | bytes 147488 | tf_op jit(solution)/shard_map/ppermute | solution.py:456
  214.4 0.1 fusion.9
  214.5 0.7 slice_bitcast_fusion.3
  215.2 0.9 collective-permute-done.23
  216.1 0.2 fusion.7
  216.3 2.6 %collective-permute-start.31 = (bf16[32,896]{1,0:T(8,128)(2,1)S(1)}, bf16[32,896]{1,0:T(8,128)(2,1)S(1)}, u32[]{:S(2)}, u32[]{:S(2)}) collective-permute-start(bf16[32,896]{1,0:T(8,128)(2,1)S(1)} %get-tuple-element.75), channel_id=1, source_target_pairs={{0,8},{1,9},{2,10},{3,11},{4,12},{5,13},{6,14},{7,15},{8,16},{9,17... | collective-permute-start | bytes 172040 | tf_op jit(solution)/shard_map/ppermute | solution.py:456
  218.9 1.3 collective-permute-start.33
  220.2 0.6 collective-permute-start.32
  220.8 0.6 slice_bitcast_fusion.7
  221.4 1.0 collective-permute-done.31
  222.4 1.0 collective-permute-done.33
  223.4 2.5 %collective-permute-done.32 = bf16[32,896]{1,0:T(8,128)(2,1)S(1)} collective-permute-done((bf16[32,896]{1,0:T(8,128)(2,1)S(1)}, bf16[32,896]{1,0:T(8,128)(2,1)S(1)}, u32[]{:S(2)}, u32[]{:S(2)}) %collective-permute-start.32) | collective-permute-done | bytes 57376 | tf_op jit(solution)/shard_map/ppermute | solution.py:456
  225.9 0.7 slice_reduce_fusion
  226.6 0.6 fusion.16
  (69 shorter events, 0.2 us)
Async XLA Ops:
  3.6 8.1 %collective-permute-start.2 = (bf16[32,1152]{1,0:T(8,128)(2,1)}, bf16[32,1152]{1,0:T(8,128)(2,1)S(1)}, u32[]{:S(2)}, u32[]{:S(2)}) collective-permute-start(bf16[32,1152]{1,0:T(8,128)(2,1)} %get-tuple-element.36), channel_id=1, source_target_pairs={{0,24},{1,25},{2,26},{3,27},{4,28},{5,29},{6,30},{7,31},{8,0},{9,1... | collective-permute-start | bytes 221192 | tf_op jit(solution)/shard_map/ppermute | solution.py:456
  8.6 7.2 %collective-permute-start.1 = (bf16[32,1152]{1,0:T(8,128)(2,1)}, bf16[32,1152]{1,0:T(8,128)(2,1)S(1)}, u32[]{:S(2)}, u32[]{:S(2)}) collective-permute-start(bf16[32,1152]{1,0:T(8,128)(2,1)} %get-tuple-element.36), channel_id=1, source_target_pairs={{0,16},{1,17},{2,18},{3,19},{4,20},{5,21},{6,22},{7,23},{8,24},{9,... | collective-permute-start | bytes 221192 | tf_op jit(solution)/shard_map/ppermute | solution.py:456
  8.6 7.2 %collective-permute-start = (bf16[32,1152]{1,0:T(8,128)(2,1)}, bf16[32,1152]{1,0:T(8,128)(2,1)S(1)}, u32[]{:S(2)}, u32[]{:S(2)}) collective-permute-start(bf16[32,1152]{1,0:T(8,128)(2,1)} %get-tuple-element.36), channel_id=1, source_target_pairs={{0,8},{1,9},{2,10},{3,11},{4,12},{5,13},{6,14},{7,15},{8,16},{9,17... | collective-permute-start | bytes 221192 | tf_op jit(solution)/shard_map/ppermute | solution.py:456
  16.7 21.6 %copy-start.6 = (bf16[128,1152]{1,0:T(8,128)(2,1)}, bf16[128,1152]{1,0:T(8,128)(2,1)S(1)}, u32[]{:S(2)}) copy-start(bf16[128,1152]{1,0:T(8,128)(2,1)S(1)} %pad_maximum_fusion.1.refs_1_) | copy-start | bytes 884740
  16.8 14.9 %collective-permute-start.5 = (bf16[128,1152]{1,0:T(8,128)(2,1)S(1)}, bf16[128,1152]{1,0:T(8,128)(2,1)S(1)}, u32[]{:S(2)}, u32[]{:S(2)}) collective-permute-start(bf16[128,1152]{1,0:T(8,128)(2,1)S(1)} %pad_maximum_fusion.1.refs_1_), channel_id=1, source_target_pairs={{0,5},{1,4},{2,7},{3,6},{4,1},{5,0},{6,3},{7,2},{8,13},{9,12},{10,... | collective-permute-start | bytes 884744 | tf_op jit(solution)/shard_map/ppermute | solution.py:456
  19.3 13.6 %collective-permute-start.4 = (bf16[128,1152]{1,0:T(8,128)(2,1)S(1)}, bf16[128,1152]{1,0:T(8,128)(2,1)S(1)}, u32[]{:S(2)}, u32[]{:S(2)}) collective-permute-start(bf16[128,1152]{1,0:T(8,128)(2,1)S(1)} %pad_maximum_fusion.1.refs_1_), channel_id=1, source_target_pairs={{0,1},{1,0},{2,3},{3,2},{4,5},{5,4},{6,7},{7,6},{8,9},{9,8},{10,11... | collective-permute-start | bytes 884744 | tf_op jit(solution)/shard_map/ppermute | solution.py:456
  19.8 13.2 %collective-permute-start.3 = (bf16[128,1152]{1,0:T(8,128)(2,1)S(1)}, bf16[128,1152]{1,0:T(8,128)(2,1)S(1)}, u32[]{:S(2)}, u32[]{:S(2)}) collective-permute-start(bf16[128,1152]{1,0:T(8,128)(2,1)S(1)} %pad_maximum_fusion.1.refs_1_), channel_id=1, source_target_pairs={{0,4},{1,5},{2,6},{3,7},{4,0},{5,1},{6,2},{7,3},{8,12},{9,13},{10,... | collective-permute-start | bytes 884744 | tf_op jit(solution)/shard_map/ppermute | solution.py:456
  20.3 5.9 %collective-permute-start.12 = (bf16[32,2048]{1,0:T(8,128)(2,1)}, bf16[32,2048]{1,0:T(8,128)(2,1)S(1)}, u32[]{:S(2)}, u32[]{:S(2)}) collective-permute-start(bf16[32,2048]{1,0:T(8,128)(2,1)} %get-tuple-element.42), channel_id=1, source_target_pairs={{0,24},{1,25},{2,26},{3,27},{4,28},{5,29},{6,30},{7,31},{8,0},{9,1... | collective-permute-start | bytes 393224 | tf_op jit(solution)/shard_map/ppermute | solution.py:456
  22.3 9.3 %collective-permute-start.11 = (bf16[32,2048]{1,0:T(8,128)(2,1)}, bf16[32,2048]{1,0:T(8,128)(2,1)S(1)}, u32[]{:S(2)}, u32[]{:S(2)}) collective-permute-start(bf16[32,2048]{1,0:T(8,128)(2,1)} %get-tuple-element.42), channel_id=1, source_target_pairs={{0,16},{1,17},{2,18},{3,19},{4,20},{5,21},{6,22},{7,23},{8,24},{9,... | collective-permute-start | bytes 393224 | tf_op jit(solution)/shard_map/ppermute | solution.py:456
  26.3 7.2 %collective-permute-start.10 = (bf16[32,2048]{1,0:T(8,128)(2,1)}, bf16[32,2048]{1,0:T(8,128)(2,1)S(1)}, u32[]{:S(2)}, u32[]{:S(2)}) collective-permute-start(bf16[32,2048]{1,0:T(8,128)(2,1)} %get-tuple-element.42), channel_id=1, source_target_pairs={{0,8},{1,9},{2,10},{3,11},{4,12},{5,13},{6,14},{7,15},{8,16},{9,17... | collective-permute-start | bytes 393224 | tf_op jit(solution)/shard_map/ppermute | solution.py:456
  31.6 2.9 %collective-permute-start.6 = (bf16[128,1152]{1,0:T(8,128)(2,1)S(1)}, bf16[128,1152]{1,0:T(8,128)(2,1)S(1)}, u32[]{:S(2)}, u32[]{:S(2)}) collective-permute-start(bf16[128,1152]{1,0:T(8,128)(2,1)S(1)} %pad_maximum_fusion.1.refs_1_), channel_id=1, source_target_pairs={{0,2},{1,3},{2,0},{3,1},{4,6},{5,7},{6,4},{7,5},{8,10},{9,11},{10,... | collective-permute-start | bytes 884744 | tf_op jit(solution)/shard_map/ppermute | solution.py:456
  31.6 5.2 %copy-start.14 = (bf16[128,1152]{1,0:T(8,128)(2,1)}, bf16[128,1152]{1,0:T(8,128)(2,1)S(1)}, u32[]{:S(2)}) copy-start(bf16[128,1152]{1,0:T(8,128)(2,1)S(1)} %collective-permute-done.5.refs_4_) | copy-start | bytes 884740
  31.7 5.2 %collective-permute-start.9 = (bf16[128,1152]{1,0:T(8,128)(2,1)S(1)}, bf16[128,1152]{1,0:T(8,128)(2,1)S(1)}, u32[]{:S(2)}, u32[]{:S(2)}) collective-permute-start(bf16[128,1152]{1,0:T(8,128)(2,1)S(1)} %collective-permute-done.5.refs_4_), channel_id=1, source_target_pairs={{0,2},{1,3},{2,0},{3,1},{4,6},{5,7},{6,4},{7,5},{8,10},{9,11},{10,... | collective-permute-start | bytes 884744 | tf_op jit(solution)/shard_map/ppermute | solution.py:456
  32.9 4.7 %copy-start.15 = (bf16[128,1152]{1,0:T(8,128)(2,1)}, bf16[128,1152]{1,0:T(8,128)(2,1)S(1)}, u32[]{:S(2)}) copy-start(bf16[128,1152]{1,0:T(8,128)(2,1)S(1)} %collective-permute-done.4.refs_3_) | copy-start | bytes 884740
  32.9 4.7 %collective-permute-start.8 = (bf16[128,1152]{1,0:T(8,128)(2,1)S(1)}, bf16[128,1152]{1,0:T(8,128)(2,1)S(1)}, u32[]{:S(2)}, u32[]{:S(2)}) collective-permute-start(bf16[128,1152]{1,0:T(8,128)(2,1)S(1)} %collective-permute-done.4.refs_3_), channel_id=1, source_target_pairs={{0,2},{1,3},{2,0},{3,1},{4,6},{5,7},{6,4},{7,5},{8,10},{9,11},{10,... | collective-permute-start | bytes 884744 | tf_op jit(solution)/shard_map/ppermute | solution.py:456
  33.0 5.2 %copy-start.16 = (bf16[128,1152]{1,0:T(8,128)(2,1)}, bf16[128,1152]{1,0:T(8,128)(2,1)S(1)}, u32[]{:S(2)}) copy-start(bf16[128,1152]{1,0:T(8,128)(2,1)S(1)} %collective-permute-done.3.refs_2_) | copy-start | bytes 884740
  33.0 5.4 %collective-permute-start.7 = (bf16[128,1152]{1,0:T(8,128)(2,1)S(1)}, bf16[128,1152]{1,0:T(8,128)(2,1)}, u32[]{:S(2)}, u32[]{:S(2)}) collective-permute-start(bf16[128,1152]{1,0:T(8,128)(2,1)S(1)} %collective-permute-done.3.refs_2_), channel_id=1, source_target_pairs={{0,2},{1,3},{2,0},{3,1},{4,6},{5,7},{6,4},{7,5},{8,10},{9,11},{10,... | collective-permute-start | bytes 884744 | tf_op jit(solution)/shard_map/ppermute | solution.py:456
  34.4 32.8 %copy-start.5 = (bf16[128,2048]{1,0:T(8,128)(2,1)}, bf16[128,2048]{1,0:T(8,128)(2,1)S(1)}, u32[]{:S(2)}) copy-start(bf16[128,2048]{1,0:T(8,128)(2,1)S(1)} %pad_maximum_fusion.refs_4_) | copy-start | bytes 1572868
  34.4 34.1 %collective-permute-start.16 = (bf16[128,2048]{1,0:T(8,128)(2,1)S(1)}, bf16[128,2048]{1,0:T(8,128)(2,1)S(1)}, u32[]{:S(2)}, u32[]{:S(2)}) collective-permute-start(bf16[128,2048]{1,0:T(8,128)(2,1)S(1)} %pad_maximum_fusion.refs_4_), channel_id=1, source_target_pairs={{0,2},{1,3},{2,0},{3,1},{4,6},{5,7},{6,4},{7,5},{8,10},{9,11},{10,... | collective-permute-start | bytes 1572872 | tf_op jit(solution)/shard_map/ppermute | solution.py:456
  34.6 3.1 %copy-start.17 = (bf16[128,1152]{1,0:T(8,128)(2,1)}, bf16[128,1152]{1,0:T(8,128)(2,1)S(1)}, u32[]{:S(2)}) copy-start(bf16[128,1152]{1,0:T(8,128)(2,1)S(1)} %collective-permute-done.6.refs_5_) | copy-start | bytes 884740
  34.6 32.6 %collective-permute-start.15 = (bf16[128,2048]{1,0:T(8,128)(2,1)S(1)}, bf16[128,2048]{1,0:T(8,128)(2,1)S(1)}, u32[]{:S(2)}, u32[]{:S(2)}) collective-permute-start(bf16[128,2048]{1,0:T(8,128)(2,1)S(1)} %pad_maximum_fusion.refs_4_), channel_id=1, source_target_pairs={{0,5},{1,4},{2,7},{3,6},{4,1},{5,0},{6,3},{7,2},{8,13},{9,12},{10,... | collective-permute-start | bytes 1572872 | tf_op jit(solution)/shard_map/ppermute | solution.py:456
  36.8 1.4 copy-start.18
  36.8 30.4 %collective-permute-start.14 = (bf16[128,2048]{1,0:T(8,128)(2,1)S(1)}, bf16[128,2048]{1,0:T(8,128)(2,1)S(1)}, u32[]{:S(2)}, u32[]{:S(2)}) collective-permute-start(bf16[128,2048]{1,0:T(8,128)(2,1)S(1)} %pad_maximum_fusion.refs_4_), channel_id=1, source_target_pairs={{0,1},{1,0},{2,3},{3,2},{4,5},{5,4},{6,7},{7,6},{8,9},{9,8},{10,11... | collective-permute-start | bytes 1572872 | tf_op jit(solution)/shard_map/ppermute | solution.py:456
  37.6 0.7 copy-start.19
  37.6 29.5 %collective-permute-start.13 = (bf16[128,2048]{1,0:T(8,128)(2,1)S(1)}, bf16[128,2048]{1,0:T(8,128)(2,1)S(1)}, u32[]{:S(2)}, u32[]{:S(2)}) collective-permute-start(bf16[128,2048]{1,0:T(8,128)(2,1)S(1)} %pad_maximum_fusion.refs_4_), channel_id=1, source_target_pairs={{0,4},{1,5},{2,6},{3,7},{4,0},{5,1},{6,2},{7,3},{8,12},{9,13},{10,... | collective-permute-start | bytes 1572872 | tf_op jit(solution)/shard_map/ppermute | solution.py:456
  38.4 121.2 %slice-start = ((s8[4718592]{0:T(1024)(128)(4,1)}), s8[524288]{0:T(1024)(128)(4,1)S(1)}, s32[]{:S(2)}) async-start(s8[4718592]{0:T(1024)(128)(4,1)} %bitcast.55), calls=%async_computation | async-start | bytes 1048576
  67.2 3.5 %copy-start.8 = (bf16[128,2048]{1,0:T(8,128)(2,1)}, bf16[128,2048]{1,0:T(8,128)(2,1)S(1)}, u32[]{:S(2)}) copy-start(bf16[128,2048]{1,0:T(8,128)(2,1)S(1)} %collective-permute-done.15.refs_7_) | copy-start | bytes 1572868
  67.2 3.5 %copy-start.9 = (bf16[128,2048]{1,0:T(8,128)(2,1)}, bf16[128,2048]{1,0:T(8,128)(2,1)S(1)}, u32[]{:S(2)}) copy-start(bf16[128,2048]{1,0:T(8,128)(2,1)S(1)} %collective-permute-done.14.refs_6_) | copy-start | bytes 1572868
  67.2 3.5 %copy-start.10 = (bf16[128,2048]{1,0:T(8,128)(2,1)}, bf16[128,2048]{1,0:T(8,128)(2,1)S(1)}, u32[]{:S(2)}) copy-start(bf16[128,2048]{1,0:T(8,128)(2,1)S(1)} %collective-permute-done.13.refs_5_) | copy-start | bytes 1572868
  67.2 2.0 collective-permute-start.17
  67.3 2.6 %collective-permute-start.18 = (bf16[128,2048]{1,0:T(8,128)(2,1)S(1)}, bf16[128,2048]{1,0:T(8,128)(2,1)S(1)}, u32[]{:S(2)}, u32[]{:S(2)}) collective-permute-start(bf16[128,2048]{1,0:T(8,128)(2,1)S(1)} %collective-permute-done.14.refs_6_), channel_id=1, source_target_pairs={{0,2},{1,3},{2,0},{3,1},{4,6},{5,7},{6,4},{7,5},{8,10},{9,11},{10,... | collective-permute-start | bytes 1572872 | tf_op jit(solution)/shard_map/ppermute | solution.py:456
  67.8 2.9 %collective-permute-start.19 = (bf16[128,2048]{1,0:T(8,128)(2,1)S(1)}, bf16[128,2048]{1,0:T(8,128)(2,1)S(1)}, u32[]{:S(2)}, u32[]{:S(2)}) collective-permute-start(bf16[128,2048]{1,0:T(8,128)(2,1)S(1)} %collective-permute-done.15.refs_7_), channel_id=1, source_target_pairs={{0,2},{1,3},{2,0},{3,1},{4,6},{5,7},{6,4},{7,5},{8,10},{9,11},{10,... | collective-permute-start | bytes 1572872 | tf_op jit(solution)/shard_map/ppermute | solution.py:456
  68.5 2.2 copy-start.7
  69.2 1.5 copy-start.11
  69.9 0.8 copy-start.12
  70.7 0.8 copy-start.13
  71.5 88.1 %slice-start.1 = ((s8[4718592]{0:T(1024)(128)(4,1)}), s8[4194304]{0:T(1024)(128)(4,1)S(1)}, s32[]{:S(2)}) async-start(s8[4718592]{0:T(1024)(128)(4,1)} %bitcast.55), calls=%async_computation.1 | async-start | bytes 8388608
  71.5 88.1 %copy-start.2 = (bf16[1024,1152]{1,0:T(8,128)(2,1)S(1)}, bf16[1024,1152]{1,0:T(8,128)(2,1)}, u32[]{:S(2)}) copy-start(bf16[1024,1152]{1,0:T(8,128)(2,1)} %get-tuple-element.53.w_ref) | copy-start | bytes 7077892
  149.2 4.8 %collective-permute-start.20 = (bf16[4,4,32,2304]{3,2,1,0:T(8,128)(2,1)}, bf16[4,4,32,2304]{3,2,1,0:T(8,128)(2,1)S(1)}, u32[]{:S(2)}, u32[]{:S(2)}) collective-permute-start(bf16[4,4,32,2304]{3,2,1,0:T(8,128)(2,1)} %get-tuple-element.50), channel_id=1, source_target_pairs={{0,2},{1,3},{2,0},{3,1},{4,6},{5,7},{6,4},{7,5},{8,10},{9,11},{10,... | collective-permute-start | bytes 7077896 | tf_op jit(solution)/shard_map/ppermute | solution.py:456
  154.0 5.6 %copy-start = (s32[6]{0:T(128)S(1)}, s32[6]{0:T(128)}, u32[]{:S(2)}) copy-start(s32[6]{0:T(128)} %stack.38.place) | copy-start | bytes 76
  154.0 5.6 %copy-start.1 = (bf16[4608,512]{1,0:T(8,128)(2,1)S(1)}, bf16[4608,512]{1,0:T(8,128)(2,1)}, u32[]{:S(2)}) copy-start(bf16[4608,512]{1,0:T(8,128)(2,1)} %get-tuple-element.51.gh_ref) | copy-start | bytes 14155780
  154.0 5.6 %copy-start.3 = (f32[8,512]{1,0:T(8,128)S(1)}, f32[8,512]{1,0:T(8,128)}, u32[]{:S(2)}) copy-start(f32[8,512]{1,0:T(8,128)} %get-tuple-element.40.refs_3_.vec_ref) | copy-start | bytes 49156
  154.0 5.6 %copy-start.4 = (f32[2,512]{1,0:T(2,128)S(1)}, f32[2,512]{1,0:T(2,128)}, u32[]{:S(2)}) copy-start(f32[2,512]{1,0:T(2,128)} %get-tuple-element.54.gvtwo_ref) | copy-start | bytes 12292
  156.0 39.7 %collective-permute-start.27 = (bf16[4,32,2304]{2,1,0:T(8,128)(2,1)S(1)}, bf16[4,32,2304]{2,1,0:T(8,128)(2,1)S(1)}, u32[]{:S(2)}, u32[]{:S(2)}) collective-permute-start(bf16[4,32,2304]{2,1,0:T(8,128)(2,1)S(1)} %get-tuple-element.64), channel_id=1, source_target_pairs={{0,5},{1,4},{2,7},{3,6},{4,1},{5,0},{6,3},{7,2},{8,13},{9,12},{10,... | collective-permute-start | bytes 1769480 | tf_op jit(solution)/shard_map/ppermute | solution.py:456
  158.4 37.4 %collective-permute-start.26 = (bf16[4,32,2304]{2,1,0:T(8,128)(2,1)S(1)}, bf16[4,32,2304]{2,1,0:T(8,128)(2,1)S(1)}, u32[]{:S(2)}, u32[]{:S(2)}) collective-permute-start(bf16[4,32,2304]{2,1,0:T(8,128)(2,1)S(1)} %get-tuple-element.65), channel_id=1, source_target_pairs={{0,1},{1,0},{2,3},{3,2},{4,5},{5,4},{6,7},{7,6},{8,9},{9,8},{10,11... | collective-permute-start | bytes 1769480 | tf_op jit(solution)/shard_map/ppermute | solution.py:456
  159.0 36.8 %collective-permute-start.25 = (bf16[4,32,2304]{2,1,0:T(8,128)(2,1)S(1)}, bf16[4,32,2304]{2,1,0:T(8,128)(2,1)S(1)}, u32[]{:S(2)}, u32[]{:S(2)}) collective-permute-start(bf16[4,32,2304]{2,1,0:T(8,128)(2,1)S(1)} %get-tuple-element.66), channel_id=1, source_target_pairs={{0,4},{1,5},{2,6},{3,7},{4,0},{5,1},{6,2},{7,3},{8,12},{9,13},{10,... | collective-permute-start | bytes 1769480 | tf_op jit(solution)/shard_map/ppermute | solution.py:456
  195.8 2.5 %collective-permute-start.21 = (bf16[4,4,32,896]{3,2,1,0:T(8,128)(2,1)S(1)}, bf16[4,4,32,896]{3,2,1,0:T(8,128)(2,1)S(1)}, u32[]{:S(2)}, u32[]{:S(2)}) collective-permute-start(bf16[4,4,32,896]{3,2,1,0:T(8,128)(2,1)S(1)} %get-tuple-element.57), channel_id=1, source_target_pairs={{0,2},{1,3},{2,0},{3,1},{4,6},{5,7},{6,4},{7,5},{8,10},{9,11},{10,... | collective-permute-start | bytes 2752520 | tf_op jit(solution)/shard_map/ppermute | solution.py:456
  198.4 6.3 %collective-permute-start.30 = (bf16[32,2304]{1,0:T(8,128)(2,1)S(1)}, bf16[32,2304]{1,0:T(8,128)(2,1)S(1)}, u32[]{:S(2)}, u32[]{:S(2)}) collective-permute-start(bf16[32,2304]{1,0:T(8,128)(2,1)S(1)} %get-tuple-element.70), channel_id=1, source_target_pairs={{0,24},{1,25},{2,26},{3,27},{4,28},{5,29},{6,30},{7,31},{8,0},{9,1... | collective-permute-start | bytes 442376 | tf_op jit(solution)/shard_map/ppermute | solution.py:456
  199.9 14.5 %collective-permute-start.29 = (bf16[32,2304]{1,0:T(8,128)(2,1)S(1)}, bf16[32,2304]{1,0:T(8,128)(2,1)S(1)}, u32[]{:S(2)}, u32[]{:S(2)}) collective-permute-start(bf16[32,2304]{1,0:T(8,128)(2,1)S(1)} %get-tuple-element.71), channel_id=1, source_target_pairs={{0,16},{1,17},{2,18},{3,19},{4,20},{5,21},{6,22},{7,23},{8,24},{9,... | collective-permute-start | bytes 442376 | tf_op jit(solution)/shard_map/ppermute | solution.py:456
  201.1 13.3 %collective-permute-start.28 = (bf16[32,2304]{1,0:T(8,128)(2,1)S(1)}, bf16[32,2304]{1,0:T(8,128)(2,1)S(1)}, u32[]{:S(2)}, u32[]{:S(2)}) collective-permute-start(bf16[32,2304]{1,0:T(8,128)(2,1)S(1)} %get-tuple-element.72), channel_id=1, source_target_pairs={{0,8},{1,9},{2,10},{3,11},{4,12},{5,13},{6,14},{7,15},{8,16},{9,17... | collective-permute-start | bytes 442376 | tf_op jit(solution)/shard_map/ppermute | solution.py:456
  201.9 13.4 %collective-permute-start.22 = (bf16[4,32,896]{2,1,0:T(8,128)(2,1)S(1)}, bf16[4,32,896]{2,1,0:T(8,128)(2,1)S(1)}, u32[]{:S(2)}, u32[]{:S(2)}) collective-permute-start(bf16[4,32,896]{2,1,0:T(8,128)(2,1)S(1)} %get-tuple-element.67), channel_id=1, source_target_pairs={{0,4},{1,5},{2,6},{3,7},{4,0},{5,1},{6,2},{7,3},{8,12},{9,13},{10,... | collective-permute-start | bytes 688136 | tf_op jit(solution)/shard_map/ppermute | solution.py:456
  203.3 12.0 %collective-permute-start.24 = (bf16[4,32,896]{2,1,0:T(8,128)(2,1)S(1)}, bf16[4,32,896]{2,1,0:T(8,128)(2,1)S(1)}, u32[]{:S(2)}, u32[]{:S(2)}) collective-permute-start(bf16[4,32,896]{2,1,0:T(8,128)(2,1)S(1)} %get-tuple-element.68), channel_id=1, source_target_pairs={{0,5},{1,4},{2,7},{3,6},{4,1},{5,0},{6,3},{7,2},{8,13},{9,12},{10,... | collective-permute-start | bytes 688136 | tf_op jit(solution)/shard_map/ppermute | solution.py:456
  204.7 11.4 %collective-permute-start.23 = (bf16[4,32,896]{2,1,0:T(8,128)(2,1)S(1)}, bf16[4,32,896]{2,1,0:T(8,128)(2,1)S(1)}, u32[]{:S(2)}, u32[]{:S(2)}) collective-permute-start(bf16[4,32,896]{2,1,0:T(8,128)(2,1)S(1)} %get-tuple-element.69), channel_id=1, source_target_pairs={{0,1},{1,0},{2,3},{3,2},{4,5},{5,4},{6,7},{7,6},{8,9},{9,8},{10,11... | collective-permute-start | bytes 688136 | tf_op jit(solution)/shard_map/ppermute | solution.py:456
  216.3 6.1 %collective-permute-start.31 = (bf16[32,896]{1,0:T(8,128)(2,1)S(1)}, bf16[32,896]{1,0:T(8,128)(2,1)S(1)}, u32[]{:S(2)}, u32[]{:S(2)}) collective-permute-start(bf16[32,896]{1,0:T(8,128)(2,1)S(1)} %get-tuple-element.75), channel_id=1, source_target_pairs={{0,8},{1,9},{2,10},{3,11},{4,12},{5,13},{6,14},{7,15},{8,16},{9,17... | collective-permute-start | bytes 172040 | tf_op jit(solution)/shard_map/ppermute | solution.py:456
  218.9 4.5 %collective-permute-start.33 = (bf16[32,896]{1,0:T(8,128)(2,1)S(1)}, bf16[32,896]{1,0:T(8,128)(2,1)S(1)}, u32[]{:S(2)}, u32[]{:S(2)}) collective-permute-start(bf16[32,896]{1,0:T(8,128)(2,1)S(1)} %get-tuple-element.76), channel_id=1, source_target_pairs={{0,24},{1,25},{2,26},{3,27},{4,28},{5,29},{6,30},{7,31},{8,0},{9,1... | collective-permute-start | bytes 172040 | tf_op jit(solution)/shard_map/ppermute | solution.py:456
  220.2 5.7 %collective-permute-start.32 = (bf16[32,896]{1,0:T(8,128)(2,1)S(1)}, bf16[32,896]{1,0:T(8,128)(2,1)S(1)}, u32[]{:S(2)}, u32[]{:S(2)}) collective-permute-start(bf16[32,896]{1,0:T(8,128)(2,1)S(1)} %get-tuple-element.77), channel_id=1, source_target_pairs={{0,16},{1,17},{2,18},{3,19},{4,20},{5,21},{6,22},{7,23},{8,24},{9,... | collective-permute-start | bytes 172040 | tf_op jit(solution)/shard_map/ppermute | solution.py:456
